TPU v7x, 32 devices: a whole 2x2x4 slice. The times are simulated.
32 devices in a mesh: view: 8 (over z, x), slab: 4 (over y, core).
Axes of the slice: x: 2, y: 2, z: 4, core: 2. Of those that a mesh axis runs over, the one named last changes fastest.
Arguments:
- leaf_coeffs: float32 [16, 64, 768], P('view', 'slab'), may hold values from -6 to 6
- measured: float32 [16, 64, 768], P('view', 'slab'), may hold values from -6 to 6
- ray_weight: float32 [16, 64, 768], P('view', 'slab'), may hold values from 0.25 to 1
- cone_weight: float32 [16, 9], P('view'), may hold values from 0.1 to 0.5
- interp_weight: float32 [3, 2, 16, 4], replicated, may hold values from -2 to 2
- shift_offset: int32 [3, 2, 16], replicated, may hold values from -24 to 24
- source_view: int32 [3, 2, 16], replicated, may hold values from 0 to 1
Outputs:
- residual: float32 [16, 64, 768], P('view', 'slab')
- updated: float32 [16, 64, 768], P('view', 'slab')
Inputs may be any that keep to these rules, and one draw needn't show every extreme that they name: source_view[l, c, v] is a view row within the supplying block.
All inputs are finite; a program needn't handle non-finite values.
Results may differ from a plain program's by a relative error of at most 0.00012.
Values sent between devices are 32-bit elements; how exact they have to be, the bound alone decides.
No kernel may reach another device: no remote copies, remote signals or barrier semaphores. Data moves between devices by JAX's collectives and lax.ppermute only.
A program may use at most 64 MiB of HBM per device.

v0:
```python
import jax
import jax.numpy as jnp
from jax import lax
from jax.sharding import PartitionSpec as P

TAPS = 4
SHIFT = 24


def from_partner(x, axis, apart):
    return lax.ppermute(x, axis, [(i, i ^ 1 << apart) for i in range(lax.axis_size(axis))])


def extended(block, sides, width):
    for axis, dim in sides:
        count = lax.axis_size(axis)
        forward = [(i, i + 1) for i in range(count - 1)]
        backward = [(target, source) for source, target in forward]
        low = lax.ppermute(
            lax.slice_in_dim(block, block.shape[dim] - width, None, axis=dim), axis, forward
        )
        high = lax.ppermute(lax.slice_in_dim(block, 0, width, axis=dim), axis, backward)
        block = jnp.concatenate([low, block, high], axis=dim)
    return block


def level_params(
    interp_weight, shift_offset, source_view, level_index, channel, device, view_count
):
    first_row = device * view_count
    tap_weights = lax.dynamic_slice_in_dim(
        interp_weight[level_index, channel], first_row, view_count, 0
    )
    tap_offsets = lax.dynamic_slice_in_dim(
        shift_offset[level_index, channel], first_row, view_count, 0
    )
    chosen_rows = lax.dynamic_slice_in_dim(
        source_view[level_index, channel], first_row, view_count, 0
    )
    return (tap_weights, tap_offsets, chosen_rows)


def row_selector(chosen_rows, view_count):
    return (chosen_rows[:, None] == lax.iota(jnp.int32, view_count)[None, :]).astype(jnp.float32)


def shift_taps(padded, tap_weights, begins, columns, forward):
    tap_count = tap_weights.shape[1]
    outputs = []
    for row_index in range(padded.shape[0]):
        window = lax.dynamic_slice_in_dim(
            padded[row_index], begins[row_index], columns + tap_count - 1, 1
        )
        summed = jnp.zeros((padded.shape[1], columns), jnp.float32)
        for tap_index in range(tap_count):
            offset_in = tap_index if forward else tap_count - 1 - tap_index
            summed = (
                summed
                + tap_weights[row_index, tap_index] * window[:, offset_in : offset_in + columns]
            )
        outputs.append(summed)
    return jnp.stack(outputs)


def resample(source_block, level_terms):
    tap_weights, tap_offsets, chosen_rows = level_terms
    view_count = source_block.shape[0]
    columns = source_block.shape[2]
    margin = SHIFT + TAPS
    selector = row_selector(chosen_rows, view_count)
    picked = jnp.einsum("vm,mzw->vzw", selector, source_block, precision=lax.Precision.HIGHEST)
    padded = jnp.pad(picked, ((0, 0), (0, 0), (margin, margin)))
    begins = tap_offsets + margin
    return shift_taps(padded, tap_weights, begins, columns, True)


def spread_back(cotangent, level_terms):
    tap_weights, tap_offsets, chosen_rows = level_terms
    view_count = cotangent.shape[0]
    columns = cotangent.shape[2]
    margin = SHIFT + TAPS
    padded = jnp.pad(cotangent, ((0, 0), (0, 0), (margin, margin)))
    begins = margin - tap_offsets - (tap_weights.shape[1] - 1)
    accumulated = shift_taps(padded, tap_weights, begins, columns, False)
    selector = row_selector(chosen_rows, view_count)
    return jnp.einsum("vm,vzw->mzw", selector, accumulated, precision=lax.Precision.HIGHEST)


def tilt_forward(padded, cone_weight, output_planes):
    accumulated = jnp.zeros((padded.shape[0], output_planes, padded.shape[2]), jnp.float32)
    for cone_index in range(cone_weight.shape[1]):
        accumulated = (
            accumulated
            + cone_weight[:, cone_index][:, None, None]
            * padded[:, cone_index : cone_index + output_planes]
        )
    return accumulated


def tilt_adjoint(padded, cone_weight, output_planes):
    widest = cone_weight.shape[1] - 1
    accumulated = jnp.zeros((padded.shape[0], output_planes, padded.shape[2]), jnp.float32)
    for cone_index in range(cone_weight.shape[1]):
        begin_at = widest - cone_index
        accumulated = (
            accumulated
            + cone_weight[:, cone_index][:, None, None]
            * padded[:, begin_at : begin_at + output_planes]
        )
    return accumulated


def body(leaf_coeffs, measured, ray_weight, cone_weight, interp_weight, shift_offset, source_view):
    view_count = leaf_coeffs.shape[0]
    planes = leaf_coeffs.shape[1]
    reach_planes = (cone_weight.shape[1] - 1) // 2
    level_count = lax.axis_size("view").bit_length() - 1
    device = lax.axis_index("view")
    current = leaf_coeffs
    for level_index in range(level_count):
        stride = 2**level_index
        partner = device + stride - 2 * stride * (device // stride % 2)
        own_terms = level_params(
            interp_weight, shift_offset, source_view, level_index, 0, device, view_count
        )
        received = from_partner(current, "view", level_index)
        far_terms = level_params(
            interp_weight, shift_offset, source_view, level_index, 1, device, view_count
        )
        current = resample(current, own_terms) + resample(received, far_terms)
    padded = extended(current, (("slab", 1),), reach_planes)
    projection = tilt_forward(padded, cone_weight, planes)
    residual = measured - projection
    weighted = ray_weight * residual
    padded_back = extended(weighted, (("slab", 1),), reach_planes)
    cotangent = tilt_adjoint(padded_back, cone_weight, planes)
    for level_index in reversed(range(level_count)):
        stride = 2**level_index
        partner = device + stride - 2 * stride * (device // stride % 2)
        own_terms = level_params(
            interp_weight, shift_offset, source_view, level_index, 0, device, view_count
        )
        received = from_partner(cotangent, "view", level_index)
        far_terms = level_params(
            interp_weight, shift_offset, source_view, level_index, 1, partner, view_count
        )
        cotangent = spread_back(cotangent, own_terms) + spread_back(received, far_terms)
    updated = leaf_coeffs + cotangent
    return (residual, updated)


def solution(mesh):
    in_specs = (
        P("view", "slab", None),
        P("view", "slab", None),
        P("view", "slab", None),
        P("view", None),
        P(),
        P(),
        P(),
    )
    out_specs = (P("view", "slab", None), P("view", "slab", None))
    return jax.shard_map(body, mesh=mesh, in_specs=in_specs, out_specs=out_specs, check_vma=False)
```

profile of v0, /device:TPU:0, one launch (start us, length us, event | category | flops | bytes accessed | tf_op | source)
XLA Modules:
  0.0 160.0 jit_solution(7893298777017997480)
XLA Ops:
  1.6 3.0 %collective-permute-start = (f32[2,16,768]{2,0,1:T(2,128)S(1)}, f32[2,16,768]{2,0,1:T(2,128)S(1)}, u32[]{:S(2)}, u32[]{:S(2)}) collective-permute-start(f32[2,16,768]{2,0,1:T(2,128)S(1)} %copy.13), channel_id=1, source_target_pairs={{0,4},{4,0},{8,12},{12,8},{16,20},{20,16},{24,28},{28,24},{1,5},{5... | collective-permute-start | bytes 294920 | tf_op jit(solution)/shard_map/ppermute | solution.py:11
  27.6 2.6 %fusion.130 = f32[16,768]{1,0:T(8,128)S(1)} fusion(f32[16,771]{1,0:T(8,128)S(1)} %bitcast.255, f32[]{:T(128)} %bitcast.21, f32[]{:T(128)} %bitcast.20, f32[]{:T(128)} %bitcast.19, f32[]{:T(128)} %bitcast.17), kind=kLoop, calls=%fused_computation.307 | loop fusion | flops 86016 | bytes 245776 | tf_op jit(solution)/shard_map/add | solution.py:58
  31.1 2.6 %fusion.134 = f32[1,16,768]{2,1,0:T(8,128)S(1)} fusion(f32[16,771]{1,0:T(8,128)S(1)} %bitcast.274, f32[]{:T(128)} %bitcast.15, f32[]{:T(128)} %bitcast.14, f32[]{:T(128)} %bitcast.13, f32[]{:T(128)} %bitcast.9), kind=kLoop, calls=%fused_computation.315 | loop fusion | flops 86016 | bytes 245776 | tf_op jit(solution)/shard_map/stack | solution.py:62
  50.2 2.6 %fusion.124 = f32[16,768]{1,0:T(8,128)S(1)} fusion(f32[16,771]{1,0:T(8,128)S(1)} %bitcast.264, f32[]{:T(128)} %bitcast.34, f32[]{:T(128)} %bitcast.33, f32[]{:T(128)} %bitcast.32, f32[]{:T(128)} %bitcast.30), kind=kLoop, calls=%fused_computation.293 | loop fusion | flops 86016 | bytes 245776 | tf_op jit(solution)/shard_map/add | solution.py:58
  53.0 2.7 %fusion.127 = f32[16,768]{1,0:T(8,128)S(1)} fusion(f32[16,771]{1,0:T(8,128)S(1)} %bitcast.260, f32[]{:T(128)} %bitcast.29, f32[]{:T(128)} %bitcast.28, f32[]{:T(128)} %bitcast.27, f32[]{:T(128)} %bitcast.23), kind=kLoop, calls=%fused_computation.300 | loop fusion | flops 86016 | bytes 245776 | tf_op jit(solution)/shard_map/add | solution.py:58
  58.7 2.5 %fusion.117 = f32[16,768]{1,0:T(8,128)S(1)} fusion(f32[16,771]{1,0:T(8,128)S(1)} %bitcast.258, f32[]{:T(128)} %bitcast.44, f32[]{:T(128)} %bitcast.43, f32[]{:T(128)} %bitcast.42, f32[]{:T(128)} %bitcast.40), kind=kLoop, calls=%fused_computation.278 | loop fusion | flops 86016 | bytes 245776 | tf_op jit(solution)/shard_map/add | solution.py:58
  61.2 2.6 %fusion.121 = f32[1,16,768]{2,1,0:T(8,128)S(1)} fusion(f32[16,771]{1,0:T(8,128)S(1)} %bitcast.272, f32[]{:T(128)} %bitcast.38, f32[]{:T(128)} %bitcast.37, f32[]{:T(128)} %bitcast.36, f32[]{:T(128)} %bitcast.5), kind=kLoop, calls=%fused_computation.286 | loop fusion | flops 86016 | bytes 245776 | tf_op jit(solution)/shard_map/stack | solution.py:62
  64.8 2.6 %fusion.111 = f32[16,768]{1,0:T(8,128)S(1)} fusion(f32[16,771]{1,0:T(8,128)S(1)} %bitcast.265, f32[]{:T(128)} %bitcast.57, f32[]{:T(128)} %bitcast.56, f32[]{:T(128)} %bitcast.55, f32[]{:T(128)} %bitcast.53), kind=kLoop, calls=%fused_computation.264 | loop fusion | flops 86016 | bytes 245776 | tf_op jit(solution)/shard_map/add | solution.py:58
  67.7 2.6 %fusion.114 = f32[16,768]{1,0:T(8,128)S(1)} fusion(f32[16,771]{1,0:T(8,128)S(1)} %bitcast.261, f32[]{:T(128)} %bitcast.52, f32[]{:T(128)} %bitcast.51, f32[]{:T(128)} %bitcast.50, f32[]{:T(128)} %bitcast.46), kind=kLoop, calls=%fused_computation.271 | loop fusion | flops 86016 | bytes 245776 | tf_op jit(solution)/shard_map/add | solution.py:58
  70.5 2.7 %collective-permute-start.2 = (f32[2,16,768]{2,0,1:T(2,128)S(1)}, f32[2,16,768]{2,0,1:T(2,128)S(1)}, u32[]{:S(2)}, u32[]{:S(2)}) collective-permute-start(f32[2,16,768]{2,0,1:T(2,128)S(1)} %maximum_add_fusion.1), channel_id=1, source_target_pairs={{0,16},{4,20},{8,24},{12,28},{16,0},{20,4},{24,8},{28,12},{1,17},{... | collective-permute-start | bytes 294920 | tf_op jit(solution)/shard_map/ppermute | solution.py:11
  74.3 2.7 %fusion.104 = f32[1,16,768]{2,1,0:T(8,128)S(1)} fusion(f32[16,771]{1,0:T(8,128)S(1)} %bitcast.259, f32[]{:T(128)} %bitcast.67, f32[]{:T(128)} %bitcast.66, f32[]{:T(128)} %bitcast.65, f32[]{:T(128)} %bitcast.63), kind=kLoop, calls=%fused_computation.249 | loop fusion | flops 86016 | bytes 245776 | tf_op jit(solution)/shard_map/stack | solution.py:62
  80.6 2.5 %fusion.96 = f32[1,16,768]{2,1,0:T(8,128)S(1)} fusion(f32[16,771]{1,0:T(8,128)S(1)} %bitcast.257, f32[]{:T(128)} %bitcast.82, f32[]{:T(128)} %bitcast.81, f32[]{:T(128)} %bitcast.80, f32[]{:T(128)} %bitcast.78), kind=kLoop, calls=%fused_computation.233 | loop fusion | flops 86016 | bytes 245776 | tf_op jit(solution)/shard_map/stack | solution.py:62
  83.1 2.6 %fusion.100 = f32[1,16,768]{2,1,0:T(8,128)S(1)} fusion(f32[16,771]{1,0:T(8,128)S(1)} %bitcast.256, f32[]{:T(128)} %bitcast.76, f32[]{:T(128)} %bitcast.75, f32[]{:T(128)} %bitcast.74, f32[]{:T(128)} %bitcast.70), kind=kLoop, calls=%fused_computation.241 | loop fusion | flops 86016 | bytes 245776 | tf_op jit(solution)/shard_map/stack | solution.py:62
  87.3 3.0 %collective-permute-start.3 = (f32[2,4,768]{2,1,0:T(4,128)S(1)}, f32[2,4,768]{2,1,0:T(4,128)S(1)}, u32[]{:S(2)}, u32[]{:S(2)}) collective-permute-start(f32[2,4,768]{2,1,0:T(4,128)S(1)} %get-tuple-element.29), channel_id=1, source_target_pairs={{0,1},{1,2},{2,3},{4,5},{5,6},{6,7},{8,9},{9,10},{10,11},{12,13},{... | collective-permute-start | bytes 73736 | tf_op jit(solution)/shard_map/ppermute | solution.py:19
  92.0 3.1 %collective-permute-start.6 = (f32[2,4,768]{2,1,0:T(4,128)S(1)}, f32[2,4,768]{2,1,0:T(4,128)S(1)}, u32[]{:S(2)}, u32[]{:S(2)}) collective-permute-start(f32[2,4,768]{2,1,0:T(4,128)S(1)} %get-tuple-element.28), channel_id=1, source_target_pairs={{0,1},{1,2},{2,3},{4,5},{5,6},{6,7},{8,9},{9,10},{10,11},{12,13},{... | collective-permute-start | bytes 73736 | tf_op jit(solution)/shard_map/ppermute | solution.py:19
  120.5 2.7 %fusion.88 = f32[16,768]{1,0:T(8,128)S(1)} fusion(f32[16,771]{1,0:T(8,128)S(1)} %dynamic-slice_bitcast_fusion.2, f32[]{:T(128)} %bitcast.67, f32[]{:T(128)} %bitcast.66, f32[]{:T(128)} %bitcast.65, f32[]{:T(128)} %bitcast.63), kind=kLoop, calls=%fused_computation.217 | loop fusion | flops 86016 | bytes 245776 | tf_op jit(solution)/shard_map/add | solution.py:58
  127.8 2.5 %fusion.82 = f32[16,768]{1,0:T(8,128)S(1)} fusion(f32[16,771]{1,0:T(8,128)S(1)} %dynamic-slice_bitcast_fusion, f32[]{:T(128)} %bitcast.106, f32[]{:T(128)} %bitcast.105, f32[]{:T(128)} %bitcast.104, f32[]{:T(128)} %bitcast.101), kind=kLoop, calls=%fused_computation.203 | loop fusion | flops 86016 | bytes 245776 | tf_op jit(solution)/shard_map/add | solution.py:58
  130.5 2.5 %fusion.85 = f32[16,768]{1,0:T(8,128)S(1)} fusion(f32[16,771]{1,0:T(8,128)S(1)} %dynamic-slice_bitcast_fusion.1, f32[]{:T(128)} %bitcast.100, f32[]{:T(128)} %bitcast.99, f32[]{:T(128)} %bitcast.98, f32[]{:T(128)} %bitcast.95), kind=kLoop, calls=%fused_computation.210 | loop fusion | flops 86016 | bytes 245776 | tf_op jit(solution)/shard_map/add | solution.py:58
  134.0 2.5 %fusion.75 = f32[1,16,768]{2,1,0:T(8,128)S(1)} fusion(f32[16,771]{1,0:T(8,128)S(1)} %bitcast.266, f32[]{:T(128)} %bitcast.44, f32[]{:T(128)} %bitcast.43, f32[]{:T(128)} %bitcast.42, f32[]{:T(128)} %bitcast.40), kind=kLoop, calls=%fused_computation.188 | loop fusion | flops 86016 | bytes 245776 | tf_op jit(solution)/shard_map/stack | solution.py:62
  136.8 2.6 %fusion.79 = f32[1,16,768]{2,1,0:T(8,128)S(1)} fusion(f32[16,771]{1,0:T(8,128)S(1)} %bitcast.267, f32[]{:T(128)} %bitcast.38, f32[]{:T(128)} %bitcast.37, f32[]{:T(128)} %bitcast.36, f32[]{:T(128)} %bitcast.5), kind=kLoop, calls=%fused_computation.196 | loop fusion | flops 86016 | bytes 245776 | tf_op jit(solution)/shard_map/stack | solution.py:62
  143.0 2.7 %fusion.71 = f32[16,768]{1,0:T(8,128)S(1)} fusion(f32[16,771]{1,0:T(8,128)S(1)} %bitcast.262, f32[]{:T(128)} %bitcast.118, f32[]{:T(128)} %bitcast.117, f32[]{:T(128)} %bitcast.116, f32[]{:T(128)} %bitcast.114), kind=kLoop, calls=%fused_computation.180 | loop fusion | flops 86016 | bytes 245776 | tf_op jit(solution)/shard_map/add | solution.py:58
  147.2 2.6 %fusion.61 = f32[1,16,768]{2,1,0:T(8,128)S(1)} fusion(f32[16,771]{1,0:T(8,128)S(1)} %bitcast.269, f32[]{:T(128)} %bitcast.21, f32[]{:T(128)} %bitcast.20, f32[]{:T(128)} %bitcast.19, f32[]{:T(128)} %bitcast.17), kind=kLoop, calls=%fused_computation.158 | loop fusion | flops 86016 | bytes 245776 | tf_op jit(solution)/shard_map/stack | solution.py:62
  150.0 2.6 %fusion.65 = f32[1,16,768]{2,1,0:T(8,128)S(1)} fusion(f32[16,771]{1,0:T(8,128)S(1)} %bitcast.270, f32[]{:T(128)} %bitcast.15, f32[]{:T(128)} %bitcast.14, f32[]{:T(128)} %bitcast.13, f32[]{:T(128)} %bitcast.9), kind=kLoop, calls=%fused_computation.166 | loop fusion | flops 86016 | bytes 245776 | tf_op jit(solution)/shard_map/stack | solution.py:62
  156.2 2.7 %fusion.57 = f32[16,768]{1,0:T(8,128)S(1)} fusion(f32[16,771]{1,0:T(8,128)S(1)} %bitcast.263, f32[]{:T(128)} %bitcast.135, f32[]{:T(128)} %bitcast.134, f32[]{:T(128)} %bitcast.133, f32[]{:T(128)} %bitcast.131), kind=kLoop, calls=%fused_computation.150 | loop fusion | flops 86016 | bytes 245776 | tf_op jit(solution)/shard_map/add | solution.py:58
  (172 shorter events, 49.4 us)
Async XLA Ops:
  1.6 47.7 %collective-permute-start = (f32[2,16,768]{2,0,1:T(2,128)S(1)}, f32[2,16,768]{2,0,1:T(2,128)S(1)}, u32[]{:S(2)}, u32[]{:S(2)}) collective-permute-start(f32[2,16,768]{2,0,1:T(2,128)S(1)} %copy.13), channel_id=1, source_target_pairs={{0,4},{4,0},{8,12},{12,8},{16,20},{20,16},{24,28},{28,24},{1,5},{5... | collective-permute-start | bytes 294920 | tf_op jit(solution)/shard_map/ppermute | solution.py:11
  4.6 0.7 copy-start.4
  23.1 1.3 copy-start.5
  26.1 0.7 copy-start.3
  36.4 1.5 copy-start.2
  55.9 8.0 %collective-permute-start.1 = (f32[2,16,768]{2,0,1:T(2,128)S(1)}, f32[2,16,768]{2,0,1:T(2,128)S(1)}, u32[]{:S(2)}, u32[]{:S(2)}) collective-permute-start(f32[2,16,768]{2,0,1:T(2,128)S(1)} %maximum_add_fusion), channel_id=1, source_target_pairs={{0,8},{4,12},{8,0},{12,4},{16,24},{20,28},{24,16},{28,20},{1,9},{5... | collective-permute-start | bytes 294920 | tf_op jit(solution)/shard_map/ppermute | solution.py:11
  70.5 9.0 %collective-permute-start.2 = (f32[2,16,768]{2,0,1:T(2,128)S(1)}, f32[2,16,768]{2,0,1:T(2,128)S(1)}, u32[]{:S(2)}, u32[]{:S(2)}) collective-permute-start(f32[2,16,768]{2,0,1:T(2,128)S(1)} %maximum_add_fusion.1), channel_id=1, source_target_pairs={{0,16},{4,20},{8,24},{12,28},{16,0},{20,4},{24,8},{28,12},{1,17},{... | collective-permute-start | bytes 294920 | tf_op jit(solution)/shard_map/ppermute | solution.py:11
  85.8 5.4 %copy-start.1 = (f32[2,16,768]{2,1,0:T(8,128)S(1)}, f32[2,16,768]{2,1,0:T(8,128)}, u32[]{:S(2)}) copy-start(f32[2,16,768]{2,1,0:T(8,128)} %param.8) | copy-start | bytes 294916
  85.8 5.3 %copy-start = (f32[2,16,768]{2,1,0:T(8,128)S(1)}, f32[2,16,768]{2,1,0:T(8,128)}, u32[]{:S(2)}) copy-start(f32[2,16,768]{2,1,0:T(8,128)} %param.9) | copy-start | bytes 294916
  85.8 5.1 %collective-permute-start.4 = (f32[2,4,768]{2,1,0:T(4,128)S(1)}, f32[2,4,768]{2,1,0:T(4,128)S(1)}, u32[]{:S(2)}, u32[]{:S(2)}) collective-permute-start(f32[2,4,768]{2,1,0:T(4,128)S(1)} %get-tuple-element.30), channel_id=1, source_target_pairs={{1,0},{2,1},{3,2},{5,4},{6,5},{7,6},{9,8},{10,9},{11,10},{13,12},{... | collective-permute-start | bytes 73736 | tf_op jit(solution)/shard_map/ppermute | solution.py:22
  87.3 3.9 %collective-permute-start.3 = (f32[2,4,768]{2,1,0:T(4,128)S(1)}, f32[2,4,768]{2,1,0:T(4,128)S(1)}, u32[]{:S(2)}, u32[]{:S(2)}) collective-permute-start(f32[2,4,768]{2,1,0:T(4,128)S(1)} %get-tuple-element.29), channel_id=1, source_target_pairs={{0,1},{1,2},{2,3},{4,5},{5,6},{6,7},{8,9},{9,10},{10,11},{12,13},{... | collective-permute-start | bytes 73736 | tf_op jit(solution)/shard_map/ppermute | solution.py:19
  92.0 27.8 %collective-permute-start.6 = (f32[2,4,768]{2,1,0:T(4,128)S(1)}, f32[2,4,768]{2,1,0:T(4,128)S(1)}, u32[]{:S(2)}, u32[]{:S(2)}) collective-permute-start(f32[2,4,768]{2,1,0:T(4,128)S(1)} %get-tuple-element.28), channel_id=1, source_target_pairs={{0,1},{1,2},{2,3},{4,5},{5,6},{6,7},{8,9},{9,10},{10,11},{12,13},{... | collective-permute-start | bytes 73736 | tf_op jit(solution)/shard_map/ppermute | solution.py:19
  95.1 24.6 %collective-permute-start.5 = (f32[2,4,768]{2,1,0:T(4,128)S(1)}, f32[2,4,768]{2,1,0:T(4,128)S(1)}, u32[]{:S(2)}, u32[]{:S(2)}) collective-permute-start(f32[2,4,768]{2,1,0:T(4,128)S(1)} %get-tuple-element.27), channel_id=1, source_target_pairs={{1,0},{2,1},{3,2},{5,4},{6,5},{7,6},{9,8},{10,9},{11,10},{13,12},{... | collective-permute-start | bytes 73736 | tf_op jit(solution)/shard_map/ppermute | solution.py:22
  120.0 7.6 %collective-permute-start.7 = (f32[2,16,768]{2,1,0:T(8,128)S(1)}, f32[2,16,768]{2,1,0:T(8,128)S(1)}, u32[]{:S(2)}, u32[]{:S(2)}) collective-permute-start(f32[2,16,768]{2,1,0:T(8,128)S(1)} %fusion.4), channel_id=1, source_target_pairs={{0,16},{4,20},{8,24},{12,28},{16,0},{20,4},{24,8},{28,12},{1,17},{... | collective-permute-start | bytes 294920 | tf_op jit(solution)/shard_map/ppermute | solution.py:11
  133.7 6.0 %collective-permute-start.8 = (f32[2,16,768]{2,0,1:T(2,128)S(1)}, f32[2,16,768]{2,0,1:T(2,128)S(1)}, u32[]{:S(2)}, u32[]{:S(2)}) collective-permute-start(f32[2,16,768]{2,0,1:T(2,128)S(1)} %convolution_add_fusion.2), channel_id=1, source_target_pairs={{0,8},{4,12},{8,0},{12,4},{16,24},{20,28},{24,16},{28,20},{1,9},{5... | collective-permute-start | bytes 294920 | tf_op jit(solution)/shard_map/ppermute | solution.py:11
  146.4 6.5 %collective-permute-start.9 = (f32[2,16,768]{2,0,1:T(2,128)S(1)}, f32[2,16,768]{2,0,1:T(2,128)S(1)}, u32[]{:S(2)}, u32[]{:S(2)}) collective-permute-start(f32[2,16,768]{2,0,1:T(2,128)S(1)} %convolution_add_fusion.1), channel_id=1, source_target_pairs={{0,4},{4,0},{8,12},{12,8},{16,20},{20,16},{24,28},{28,24},{1,5},{5... | collective-permute-start | bytes 294920 | tf_op jit(solution)/shard_map/ppermute | solution.py:11
where the time goes:
time: 163 us; the launch traced here: 160 us
  other arithmetic  63.6 us (39%)
  between operations  46.8 us (29%)
  local copies, waits for them, and re-layouts  26.3 us (16%)
  starting transfers between devices  17.4 us (11%)
  matrix products  4.39 us (3%)
    add x13, other arithmetic, shift_taps(): summed + tap_weights[row_index, tap_index] * window[:, offset_in:offset_i...  33.8 us
    another operation x13, other arithmetic, shift_taps(): return jnp.stack(outputs)  28.3 us
    ppermute x6, starting transfers between devices, from_partner(): lax.ppermute(x, axis, [(i, i ^ 1 << apart) for i in range(lax.axis_size(a...  8.36 us
    slice x12, local copies, waits for them, and re-layouts, shift_taps(): begins[row_index]  7.41 us
    ppermute x2, starting transfers between devices, extended(): lax.ppermute(lax.slice_in_dim(block, block.shape[dim] - width, None, axis...  6.18 us
    slice x9, local copies, waits for them, and re-layouts, shift_taps(): tap_weights[row_index, tap_index] * window[:, offset_in:offset_in + columns]  6.09 us
    dynamic_slice x24, local copies, waits for them, and re-layouts, shift_taps(): lax.dynamic_slice_in_dim(padded[row_index], begins[row_index], columns +...  4.1 us
  transfers between devices with their start and end apart: 10, of which 2 were waited for; matrix products, arithmetic and copies ran while one was open for 32% of the time, Pallas kernels for 0%

commit v1 on v0

v1 whole, which is shorter than its diff:
```python
import functools

import jax
import jax.numpy as jnp
from jax import lax
from jax.experimental import pallas as pl
from jax.experimental.pallas import tpu as pltpu
from jax.sharding import PartitionSpec as P

LANES = 128
SHIFT = 24


def shifted_sum(rows, moves, weights, total):
    planes, columns = rows.shape
    count = columns // LANES
    tiles = [rows[:, LANES * j : LANES * (j + 1)] for j in range(count)]
    lane = lax.broadcasted_iota(jnp.int32, (planes, LANES), 1)
    nothing = jnp.zeros((planes, LANES), jnp.float32)
    for move, weight in zip(moves, weights):
        turned = [pltpu.roll(tile, (LANES - move) & (LANES - 1), 1) for tile in tiles]
        below = lane + move < 0
        above = lane + move >= LANES
        for j in range(count):
            left = turned[j - 1] if j > 0 else nothing
            right = turned[j + 1] if j + 1 < count else nothing
            term = weight * jnp.where(below, left, jnp.where(above, right, turned[j]))
            total[j] = term if total[j] is None else total[j] + term
    return total


def join(tiles):
    return jnp.concatenate(tiles, axis=1)


def level_forward(level, block, own, partner, out, params):
    weight, offset, source = params
    views, _, columns = own.shape
    taps = weight.shape[3]
    for v in range(views):
        row = block * views + v
        total = [None] * (columns // LANES)
        for channel, held in enumerate((own, partner)):
            begin = offset[level, channel, row]
            total = shifted_sum(
                held[source[level, channel, row]],
                [begin + k for k in range(taps)],
                [weight[level, channel, row, k] for k in range(taps)],
                total,
            )
        out[v] = join(total)


def level_back(level, block, own, partner, out, params):
    weight, offset, source = params
    views, _, columns = own.shape
    taps = weight.shape[3]
    out[...] = jnp.zeros(out.shape, jnp.float32)
    for channel, held in enumerate((own, partner)):
        owner = block ^ (channel << level)
        for v in range(views):
            row = owner * views + v
            begin = offset[level, channel, row]
            total = shifted_sum(
                held[v],
                [-begin - k for k in range(taps)],
                [weight[level, channel, row, k] for k in range(taps)],
                [None] * (columns // LANES),
            )
            target = source[level, channel, row]
            out[target] = out[target] + join(total)


def forward_kernel(levels, count, last, weight, offset, source, *refs):
    params = (weight, offset, source)
    states, refs = refs[:count], refs[count:]
    out = refs[0]
    me = lax.axis_index("view")
    if len(levels) == 2:
        near, far = refs[-2:]
        low, high = levels
        level_forward(low, me, states[0], states[1], near, params)
        level_forward(low, me ^ (1 << high), states[2], states[3], far, params)
        level_forward(high, me, near, far, out, params)
    else:
        level_forward(levels[0], me, states[0], states[1], out, params)
    if last:
        pair, across = refs[1:3]
        width = pair.shape[1]
        planes = out.shape[1]
        odd = lax.axis_index("slab") % 2
        top = pl.multiple_of((1 - odd) * (planes - width), 8)
        bottom = pl.multiple_of(odd * (planes - width), 8)
        pair[...] = out[:, pl.ds(top, width), :]
        across[...] = out[:, pl.ds(bottom, width), :]


def back_kernel(levels, count, last, weight, offset, source, *refs):
    params = (weight, offset, source)
    states, refs = refs[:count], refs[count:]
    me = lax.axis_index("view")
    if last:
        leaf, refs = refs[0], refs[1:]
    out = refs[0]
    if len(levels) == 2:
        near, far = refs[-2:]
        low, high = levels
        level_back(high, me, states[0], states[2], near, params)
        level_back(high, me ^ (1 << low), states[1], states[3], far, params)
        level_back(low, me, near, far, out, params)
    else:
        level_back(levels[0], me, states[0], states[1], out, params)
    if last:
        out[...] = leaf[...] + out[...]


def tilt_kernel(cone, split, pair, across, measured, ray, residual, cotangent, wide, weighted):
    views, planes, columns = split.shape
    width = pair.shape[1]
    crossed = cone.shape[1]
    reach = crossed // 2
    odd = lax.axis_index("slab") % 2
    far = planes + width
    wide[:, pl.ds(width, planes), :] = split[...]
    wide[:, pl.ds(pl.multiple_of((1 - odd) * far, 8), width), :] = pair[...]
    wide[:, pl.ds(pl.multiple_of(odd * far, 8), width), :] = across[...]
    extended = planes + 2 * reach
    for v in range(views):
        for j in range(columns // LANES):
            at = pl.ds(LANES * j, LANES)
            total = cone[v, 0] * wide[v, pl.ds(width - 2 * reach, extended), at]
            for e in range(1, crossed):
                total = total + cone[v, e] * wide[v, pl.ds(width - 2 * reach + e, extended), at]
            left = measured[v, :, at] - total
            residual[v, :, at] = left[reach : reach + planes]
            weighted[v, :, at] = ray[v, :, at] * left
            total = cone[v, 0] * weighted[v, pl.ds(2 * reach, planes), at]
            for e in range(1, crossed):
                total = total + cone[v, e] * weighted[v, pl.ds(2 * reach - e, planes), at]
            cotangent[v, :, at] = total


SCALARS = pl.BlockSpec(memory_space=pltpu.SMEM)
BLOCK = pl.BlockSpec(memory_space=pltpu.VMEM)


def shaped(*shape):
    return jax.ShapeDtypeStruct(shape, jnp.float32)


def across_view(x, apart):
    return lax.ppermute(x, "view", [(i, i ^ apart) for i in range(lax.axis_size("view"))])


def with_pair(x):
    return lax.ppermute(x, "slab", [(i, i ^ 1) for i in range(lax.axis_size("slab"))])


def across_pairs(x):
    lower = range(1, lax.axis_size("slab") - 1, 2)
    return lax.ppermute(x, "slab", [(i, i + 1) for i in lower] + [(i + 1, i) for i in lower])


def gathered(x, levels):
    steps = [1 << level for level in levels]
    if len(steps) == 2:
        steps.append(steps[0] + steps[1])
    return [x] + [across_view(x, step) for step in steps]


def body(leaf_coeffs, measured, ray_weight, cone_weight, interp_weight, shift_offset, source_view):
    views, planes, columns = leaf_coeffs.shape
    reach = cone_weight.shape[1] // 2
    level_count = lax.axis_size("view").bit_length() - 1
    groups = [tuple(range(i, min(i + 2, level_count))) for i in range(0, level_count, 2)]
    params = (interp_weight, shift_offset, source_view)
    whole = shaped(views, planes, columns)
    part = shaped(views, 2 * reach, columns)
    scratch = [pltpu.VMEM((views, planes, columns), jnp.float32)] * 2

    odd = lax.axis_index("slab") % 2 == 1
    both = jnp.stack([measured, ray_weight])
    low, high = both[:, :, :reach], both[:, :, planes - reach :]
    paired = with_pair(jnp.where(odd, low, high))
    crossing = across_pairs(jnp.where(odd, high, low))
    both = jnp.concatenate(
        [jnp.where(odd, paired, crossing), both, jnp.where(odd, crossing, paired)], axis=2
    )

    state = leaf_coeffs
    for levels in groups:
        states = gathered(state, levels)
        last = levels == groups[-1]
        state = pl.pallas_call(
            functools.partial(forward_kernel, levels, len(states), last),
            out_shape=[whole] + [part] * 2 * last,
            in_specs=[SCALARS] * 3 + [BLOCK] * len(states),
            out_specs=[BLOCK] * (1 + 2 * last),
            scratch_shapes=scratch if len(levels) == 2 else [],
            name="split",
        )(*params, *states)
        if last:
            split, to_pair, to_across = state
        else:
            state = state[0]

    residual, cotangent = pl.pallas_call(
        tilt_kernel,
        out_shape=[whole, whole],
        in_specs=[SCALARS] + [BLOCK] * 5,
        out_specs=[BLOCK] * 2,
        scratch_shapes=[
            pltpu.VMEM((views, planes + 4 * reach, columns), jnp.float32),
            pltpu.VMEM((views, planes + 2 * reach, columns), jnp.float32),
        ],
        name="tilt",
    )(cone_weight, split, with_pair(to_pair), across_pairs(to_across), both[0], both[1])

    state = cotangent
    for levels in reversed(groups):
        states = gathered(state, levels)
        last = levels == groups[0]
        state = pl.pallas_call(
            functools.partial(back_kernel, levels, len(states), last),
            out_shape=whole,
            in_specs=[SCALARS] * 3 + [BLOCK] * (len(states) + last),
            out_specs=BLOCK,
            scratch_shapes=scratch if len(levels) == 2 else [],
            name="back",
        )(*params, *states, *([leaf_coeffs] if last else []))
    return (residual, state)


def solution(mesh):
    in_specs = (
        P("view", "slab", None),
        P("view", "slab", None),
        P("view", "slab", None),
        P("view", None),
        P(),
        P(),
        P(),
    )
    out_specs = (P("view", "slab", None), P("view", "slab", None))
    return jax.shard_map(body, mesh=mesh, in_specs=in_specs, out_specs=out_specs, check_vma=False)
```

time: 163 us -> 57 us (0.35)
  the two profiles are of different devices: /device:TPU:0 before, /device:TPU:1 now
where the time goes in v1:
time: 57 us; the launch traced here: 56.5 us
  starting transfers between devices  19 us (33%)
  waiting for transfers between devices  17.9 us (31%)
  Pallas kernels  13.3 us (23%)
  local copies, waits for them, and re-layouts  4.65 us (8%)
  other arithmetic  0.96 us (2%)
  between operations  0.75 us (1%)
    ppermute x8, waiting for transfers between devices, across_view(): lax.ppermute(x, 'view', [(i, i ^ apart) for i in range(lax.axis_size('vie...  15 us
    ppermute x8, starting transfers between devices, across_view(): lax.ppermute(x, 'view', [(i, i ^ apart) for i in range(lax.axis_size('vie...  9.03 us
    ppermute x2, starting transfers between devices, across_pairs(): lax.ppermute(x, 'slab', [(i, i + 1) for i in lower] + [(i + 1, i) for i i...  6.58 us
    pallas_call x2, Pallas kernels, body(): pl.pallas_call(functools.partial(forward_kernel, levels, len(states), las...  5.6 us
    pallas_call x2, Pallas kernels, body(): pl.pallas_call(functools.partial(back_kernel, levels, len(states), last),...  5.56 us
    unnamed x29, local copies, waits for them, and re-layouts  3.92 us
    ppermute x2, starting transfers between devices, with_pair(): lax.ppermute(x, 'slab', [(i, i ^ 1) for i in range(lax.axis_size('slab'))])  3.35 us
    ppermute x2, waiting for transfers between devices, across_pairs(): lax.ppermute(x, 'slab', [(i, i + 1) for i in lower] + [(i + 1, i) for i i...  2.96 us
  transfers between devices with their start and end apart: 12, of which 9 were waited for; matrix products, arithmetic and copies ran while one was open for 3% of the time, Pallas kernels for 0%

profile of v1, /device:TPU:1, one launch (start us, length us, event | category | flops | bytes accessed | tf_op | source)
XLA Modules:
  0.0 56.5 jit_solution(16528651605431159708)
XLA Ops:
  0.6 0.9 %broadcast_select_fusion.3 = (f32[2,2,4,768]{3,2,1,0:T(4,128)S(1)}, f32[2,2,4,768]{3,2,1,0:T(4,128)S(1)}, f32[2,2,4,768]{3,2,1,0:T(4,128)S(1)}) fusion(pred[]{:T(512)S(6)} %eq.5, f32[1,2,16,768]{3,2,1,0:T(8,128)} %bitcast.13, f32[1,2,16,768]{3,2,1,0:T(8,128)} %bitcast.15), kind=kLoop, calls=%fused_computation.8 | loop fusion | flops 36864 | bytes 344065 | tf_op jit(solution)/shard_map/jit(_where)/select_n | solution.py:184
  1.6 4.7 %collective-permute-start.7 = (f32[2,2,4,768]{3,2,1,0:T(4,128)S(1)}, f32[2,2,4,768]{3,2,1,0:T(4,128)S(1)}, u32[]{:S(2)}, u32[]{:S(2)}) collective-permute-start(f32[2,2,4,768]{3,2,1,0:T(4,128)S(1)} %bitcast.23), channel_id=1, source_target_pairs={{1,2},{2,1},{5,6},{6,5},{9,10},{10,9},{13,14},{14,13},{17,18},{18,... | collective-permute-start | bytes 147464 | tf_op jit(solution)/shard_map/ppermute | solution.py:161
  6.3 1.3 %collective-permute-start = (f32[2,16,768]{2,1,0:T(8,128)S(1)}, f32[2,16,768]{2,1,0:T(8,128)S(1)}, u32[]{:S(2)}, u32[]{:S(2)}) collective-permute-start(f32[2,16,768]{2,1,0:T(8,128)S(1)} %copy-done.2), channel_id=1, source_target_pairs={{0,4},{4,0},{8,12},{12,8},{16,20},{20,16},{24,28},{28,24},{1,5},{5... | collective-permute-start | bytes 294920 | tf_op jit(solution)/shard_map/ppermute | solution.py:152
  7.6 1.3 %collective-permute-start.1 = (f32[2,16,768]{2,1,0:T(8,128)S(1)}, f32[2,16,768]{2,1,0:T(8,128)S(1)}, u32[]{:S(2)}, u32[]{:S(2)}) collective-permute-start(f32[2,16,768]{2,1,0:T(8,128)S(1)} %copy-done.2), channel_id=1, source_target_pairs={{0,8},{4,12},{8,0},{12,4},{16,24},{20,28},{24,16},{28,20},{1,9},{5... | collective-permute-start | bytes 294920 | tf_op jit(solution)/shard_map/ppermute | solution.py:152
  9.1 0.7 %copy.10.weight = f32[3,2,16,4]{3,2,1,0:T(8,128)} copy(f32[3,2,16,4]{2,3,1,0:T(4,128)S(1)} %copy-done.13) | data formatting | bytes 3072 | tf_op args[4]
  10.4 0.9 %collective-permute-done.1.refs_2_ = f32[2,16,768]{2,1,0:T(8,128)S(1)} collective-permute-done((f32[2,16,768]{2,1,0:T(8,128)S(1)}, f32[2,16,768]{2,1,0:T(8,128)S(1)}, u32[]{:S(2)}, u32[]{:S(2)}) %collective-permute-start.1) | collective-permute-done | bytes 98336 | tf_op jit(solution)/shard_map/ppermute | solution.py:152
  11.2 2.1 %collective-permute-done.2.refs_3_ = f32[2,16,768]{2,1,0:T(8,128)S(1)} collective-permute-done((f32[2,16,768]{2,1,0:T(8,128)S(1)}, f32[2,16,768]{2,1,0:T(8,128)S(1)}, u32[]{:S(2)}, u32[]{:S(2)}) %collective-permute-start.2) | collective-permute-done | bytes 98336 | tf_op jit(solution)/shard_map/ppermute | solution.py:152
  13.9 3.1 %split.2.refs_0_ = f32[2,16,768]{2,1,0:T(8,128)} custom-call(f32[3,2,16,4]{3,2,1,0:T(8,128)} %copy.10.weight, s32[3,2,16]{2,1,0:T(2,128)} %offset.7, s32[3,2,16]{2,1,0:T(2,128)} %source.7, f32[2,16,768]{2,1,0:T(8,128)} %refs_4_.1, f32[2,16,768]{2,1,0:T(8,128)} %copy-done.8, f32[2,16,768]{2,1,0:T(8,128)} %copy-done.9, f32[2,16,768]{2,1,0:T(8,128)} %copy-done.10), custom_call_target="tpu_custom_call" | custom-call | tf_op jit(solution)/shard_map/split/pallas_call | solution.py:194
  17.0 2.3 %collective-permute-start.3 = (f32[2,16,768]{2,1,0:T(8,128)}, f32[2,16,768]{2,1,0:T(8,128)S(1)}, u32[]{:S(2)}, u32[]{:S(2)}) collective-permute-start(f32[2,16,768]{2,1,0:T(8,128)} %split.2.refs_0_), channel_id=1, source_target_pairs={{0,16},{4,20},{8,24},{12,28},{16,0},{20,4},{24,8},{28,12},{1,17},{... | collective-permute-start | bytes 294920 | tf_op jit(solution)/shard_map/ppermute | solution.py:152
  19.4 3.3 %collective-permute-done.3.refs_1_ = f32[2,16,768]{2,1,0:T(8,128)S(1)} collective-permute-done((f32[2,16,768]{2,1,0:T(8,128)}, f32[2,16,768]{2,1,0:T(8,128)S(1)}, u32[]{:S(2)}, u32[]{:S(2)}) %collective-permute-start.3) | collective-permute-done | bytes 98336 | tf_op jit(solution)/shard_map/ppermute | solution.py:152
  23.3 2.5 %split.3 = (f32[2,16,768]{2,1,0:T(8,128)}, f32[2,8,768]{2,1,0:T(8,128)}, f32[2,8,768]{2,1,0:T(8,128)}) custom-call(f32[3,2,16,4]{3,2,1,0:T(8,128)} %copy.10.weight, s32[3,2,16]{2,1,0:T(2,128)} %offset.7, s32[3,2,16]{2,1,0:T(2,128)} %source.7, f32[2,16,768]{2,1,0:T(8,128)} %split.2.refs_0_, f32[2,16,768]{2,1,0:T(8,128)} %copy-done.6), custom_call_target="tpu_custom_call" | custom-call | tf_op jit(solution)/shard_map/split/pallas_call | solution.py:194
  25.8 3.3 %collective-permute-start.4 = (f32[2,8,768]{2,1,0:T(8,128)}, f32[2,8,768]{2,1,0:T(8,128)S(1)}, u32[]{:S(2)}, u32[]{:S(2)}) collective-permute-start(f32[2,8,768]{2,1,0:T(8,128)} %get-tuple-element.8), channel_id=1, source_target_pairs={{0,1},{1,0},{2,3},{3,2},{4,5},{5,4},{6,7},{7,6},{8,9},{9,8},{10,11... | collective-permute-start | bytes 147464 | tf_op jit(solution)/shard_map/ppermute | solution.py:156
  29.1 1.9 %collective-permute-start.5 = (f32[2,8,768]{2,1,0:T(8,128)}, f32[2,8,768]{2,1,0:T(8,128)S(1)}, u32[]{:S(2)}, u32[]{:S(2)}) collective-permute-start(f32[2,8,768]{2,1,0:T(8,128)} %get-tuple-element.9), channel_id=1, source_target_pairs={{1,2},{2,1},{5,6},{6,5},{9,10},{10,9},{13,14},{14,13},{17,18},{18,... | collective-permute-start | bytes 147464 | tf_op jit(solution)/shard_map/ppermute | solution.py:161
  31.0 0.7 %slice_bitcast_fusion = (f32[2,24,768]{2,1,0:T(8,128)}, f32[2,24,768]{2,1,0:T(8,128)}) fusion(f32[2,2,24,768]{3,2,1,0:T(8,128)S(1)} %pad_maximum_fusion), kind=kLoop, calls=%fused_computation.1 | loop fusion | bytes 589824 | tf_op jit(solution)/shard_map/squeeze | solution.py:217
  31.7 3.0 %collective-permute-done.5.across = f32[2,8,768]{2,1,0:T(8,128)S(1)} collective-permute-done((f32[2,8,768]{2,1,0:T(8,128)}, f32[2,8,768]{2,1,0:T(8,128)S(1)}, u32[]{:S(2)}, u32[]{:S(2)}) %collective-permute-start.5) | collective-permute-done | bytes 49184 | tf_op jit(solution)/shard_map/ppermute | solution.py:161
  35.3 2.1 %tilt.1 = (f32[2,16,768]{2,1,0:T(8,128)}, f32[2,16,768]{2,1,0:T(8,128)}) custom-call(f32[2,9]{1,0:T(2,128)} %cone.1, f32[2,16,768]{2,1,0:T(8,128)} %get-tuple-element.7.split, f32[2,8,768]{2,1,0:T(8,128)} %copy-done.11, f32[2,8,768]{2,1,0:T(8,128)} %copy-done.12, f32[2,24,768]{2,1,0:T(8,128)} %get-tuple-element.16.measured, f32[2,24,768]{2,1,0:T(8,128)} %get-tuple-element.15.ray), custom_call_target="tpu_custom_call" | custom-call | tf_op jit(solution)/shard_map/tilt/pallas_call | solution.py:207
  37.4 1.4 %collective-permute-start.8 = (f32[2,16,768]{2,1,0:T(8,128)}, f32[2,16,768]{2,1,0:T(8,128)S(1)}, u32[]{:S(2)}, u32[]{:S(2)}) collective-permute-start(f32[2,16,768]{2,1,0:T(8,128)} %get-tuple-element.11.refs_0_), channel_id=1, source_target_pairs={{0,16},{4,20},{8,24},{12,28},{16,0},{20,4},{24,8},{28,12},{1,17},{... | collective-permute-start | bytes 294920 | tf_op jit(solution)/shard_map/ppermute | solution.py:152
  38.8 4.3 %collective-permute-done.8.refs_1_ = f32[2,16,768]{2,1,0:T(8,128)S(1)} collective-permute-done((f32[2,16,768]{2,1,0:T(8,128)}, f32[2,16,768]{2,1,0:T(8,128)S(1)}, u32[]{:S(2)}, u32[]{:S(2)}) %collective-permute-start.8) | collective-permute-done | bytes 98336 | tf_op jit(solution)/shard_map/ppermute | solution.py:152
  43.7 2.5 %back.2.refs_0_ = f32[2,16,768]{2,1,0:T(8,128)} custom-call(f32[3,2,16,4]{3,2,1,0:T(8,128)} %copy.10.weight, s32[3,2,16]{2,1,0:T(2,128)} %offset.7, s32[3,2,16]{2,1,0:T(2,128)} %source.7, f32[2,16,768]{2,1,0:T(8,128)} %get-tuple-element.11.refs_0_, f32[2,16,768]{2,1,0:T(8,128)} %copy-done.7), custom_call_target="tpu_custom_call" | custom-call | tf_op jit(solution)/shard_map/back/pallas_call | solution.py:223
  46.2 2.3 %collective-permute-start.11 = (f32[2,16,768]{2,1,0:T(8,128)}, f32[2,16,768]{2,1,0:T(8,128)S(1)}, u32[]{:S(2)}, u32[]{:S(2)}) collective-permute-start(f32[2,16,768]{2,1,0:T(8,128)} %back.2.refs_0_), channel_id=1, source_target_pairs={{0,12},{4,8},{8,4},{12,0},{16,28},{20,24},{24,20},{28,16},{1,13},{... | collective-permute-start | bytes 294920 | tf_op jit(solution)/shard_map/ppermute | solution.py:152
  48.8 1.3 %collective-permute-done.10.refs_2_ = f32[2,16,768]{2,1,0:T(8,128)S(1)} collective-permute-done((f32[2,16,768]{2,1,0:T(8,128)}, f32[2,16,768]{2,1,0:T(8,128)S(1)}, u32[]{:S(2)}, u32[]{:S(2)}) %collective-permute-start.10) | collective-permute-done | bytes 98336 | tf_op jit(solution)/shard_map/ppermute | solution.py:152
  50.2 1.6 %collective-permute-done.11.refs_3_ = f32[2,16,768]{2,1,0:T(8,128)S(1)} collective-permute-done((f32[2,16,768]{2,1,0:T(8,128)}, f32[2,16,768]{2,1,0:T(8,128)S(1)}, u32[]{:S(2)}, u32[]{:S(2)}) %collective-permute-start.11) | collective-permute-done | bytes 98336 | tf_op jit(solution)/shard_map/ppermute | solution.py:152
  51.8 1.0 %collective-permute-done.9.refs_1_ = f32[2,16,768]{2,1,0:T(8,128)S(1)} collective-permute-done((f32[2,16,768]{2,1,0:T(8,128)}, f32[2,16,768]{2,1,0:T(8,128)S(1)}, u32[]{:S(2)}, u32[]{:S(2)}) %collective-permute-start.9) | collective-permute-done | bytes 98336 | tf_op jit(solution)/shard_map/ppermute | solution.py:152
  53.5 3.1 %back.3 = f32[2,16,768]{2,1,0:T(8,128)} custom-call(f32[3,2,16,4]{3,2,1,0:T(8,128)} %copy.10.weight, s32[3,2,16]{2,1,0:T(2,128)} %offset.7, s32[3,2,16]{2,1,0:T(2,128)} %source.7, f32[2,16,768]{2,1,0:T(8,128)} %back.2.refs_0_, f32[2,16,768]{2,1,0:T(8,128)} %copy-done.5, f32[2,16,768]{2,1,0:T(8,128)} %copy-done.3, f32[2,16,768]{2,1,0:T(8,128)} %copy-done.4, ...), custom_call_target="tpu_custom_call" | custom-call | tf_op jit(solution)/shard_map/back/pallas_call | solution.py:223
  (39 shorter events, 4.4 us)
Async XLA Ops:
  1.5 4.8 %copy-start.2 = (f32[2,16,768]{2,1,0:T(8,128)S(1)}, f32[2,16,768]{2,1,0:T(8,128)}, u32[]{:S(2)}) copy-start(f32[2,16,768]{2,1,0:T(8,128)} %refs_4_.1) | copy-start | bytes 294916
  1.6 7.5 %copy-start.13 = (f32[3,2,16,4]{2,3,1,0:T(4,128)S(1)}, f32[3,2,16,4]{2,3,1,0:T(4,128)}, u32[]{:S(2)}) copy-start(f32[3,2,16,4]{2,3,1,0:T(4,128)} %param.11) | copy-start | bytes 4612
  1.6 8.2 %collective-permute-start.7 = (f32[2,2,4,768]{3,2,1,0:T(4,128)S(1)}, f32[2,2,4,768]{3,2,1,0:T(4,128)S(1)}, u32[]{:S(2)}, u32[]{:S(2)}) collective-permute-start(f32[2,2,4,768]{3,2,1,0:T(4,128)S(1)} %bitcast.23), channel_id=1, source_target_pairs={{1,2},{2,1},{5,6},{6,5},{9,10},{10,9},{13,14},{14,13},{17,18},{18,... | collective-permute-start | bytes 147464 | tf_op jit(solution)/shard_map/ppermute | solution.py:161
  6.3 3.5 %collective-permute-start.6 = (f32[2,2,4,768]{3,2,1,0:T(4,128)S(1)}, f32[2,2,4,768]{3,2,1,0:T(4,128)S(1)}, u32[]{:S(2)}, u32[]{:S(2)}) collective-permute-start(f32[2,2,4,768]{3,2,1,0:T(4,128)S(1)} %get-tuple-element.12), channel_id=1, source_target_pairs={{0,1},{1,0},{2,3},{3,2},{4,5},{5,4},{6,7},{7,6},{8,9},{9,8},{10,11... | collective-permute-start | bytes 147464 | tf_op jit(solution)/shard_map/ppermute | solution.py:156
  6.3 4.0 %collective-permute-start = (f32[2,16,768]{2,1,0:T(8,128)S(1)}, f32[2,16,768]{2,1,0:T(8,128)S(1)}, u32[]{:S(2)}, u32[]{:S(2)}) collective-permute-start(f32[2,16,768]{2,1,0:T(8,128)S(1)} %copy-done.2), channel_id=1, source_target_pairs={{0,4},{4,0},{8,12},{12,8},{16,20},{20,16},{24,28},{28,24},{1,5},{5... | collective-permute-start | bytes 294920 | tf_op jit(solution)/shard_map/ppermute | solution.py:152
  7.6 3.6 %collective-permute-start.1 = (f32[2,16,768]{2,1,0:T(8,128)S(1)}, f32[2,16,768]{2,1,0:T(8,128)S(1)}, u32[]{:S(2)}, u32[]{:S(2)}) collective-permute-start(f32[2,16,768]{2,1,0:T(8,128)S(1)} %copy-done.2), channel_id=1, source_target_pairs={{0,8},{4,12},{8,0},{12,4},{16,24},{20,28},{24,16},{28,20},{1,9},{5... | collective-permute-start | bytes 294920 | tf_op jit(solution)/shard_map/ppermute | solution.py:152
  8.9 4.4 %collective-permute-start.2 = (f32[2,16,768]{2,1,0:T(8,128)S(1)}, f32[2,16,768]{2,1,0:T(8,128)S(1)}, u32[]{:S(2)}, u32[]{:S(2)}) collective-permute-start(f32[2,16,768]{2,1,0:T(8,128)S(1)} %copy-done.2), channel_id=1, source_target_pairs={{0,12},{4,8},{8,4},{12,0},{16,28},{20,24},{24,20},{28,16},{1,13},{... | collective-permute-start | bytes 294920 | tf_op jit(solution)/shard_map/ppermute | solution.py:152
  9.8 9.5 %copy-start = (f32[2,16,768]{2,1,0:T(8,128)S(1)}, f32[2,16,768]{2,1,0:T(8,128)}, u32[]{:S(2)}) copy-start(f32[2,16,768]{2,1,0:T(8,128)} %param.9) | copy-start | bytes 294916
  9.8 9.5 %copy-start.1 = (f32[2,16,768]{2,1,0:T(8,128)S(1)}, f32[2,16,768]{2,1,0:T(8,128)}, u32[]{:S(2)}) copy-start(f32[2,16,768]{2,1,0:T(8,128)} %param.8) | copy-start | bytes 294916
  10.4 2.9 %copy-start.8 = (f32[2,16,768]{2,1,0:T(8,128)}, f32[2,16,768]{2,1,0:T(8,128)S(1)}, u32[]{:S(2)}) copy-start(f32[2,16,768]{2,1,0:T(8,128)S(1)} %collective-permute-done.refs_1_) | copy-start | bytes 294916
  11.2 2.1 %copy-start.9 = (f32[2,16,768]{2,1,0:T(8,128)}, f32[2,16,768]{2,1,0:T(8,128)S(1)}, u32[]{:S(2)}) copy-start(f32[2,16,768]{2,1,0:T(8,128)S(1)} %collective-permute-done.1.refs_2_) | copy-start | bytes 294916
  13.3 0.6 %copy-start.10 = (f32[2,16,768]{2,1,0:T(8,128)}, f32[2,16,768]{2,1,0:T(8,128)S(1)}, u32[]{:S(2)}) copy-start(f32[2,16,768]{2,1,0:T(8,128)S(1)} %collective-permute-done.2.refs_3_) | copy-start | bytes 294916
  17.0 5.6 %collective-permute-start.3 = (f32[2,16,768]{2,1,0:T(8,128)}, f32[2,16,768]{2,1,0:T(8,128)S(1)}, u32[]{:S(2)}, u32[]{:S(2)}) collective-permute-start(f32[2,16,768]{2,1,0:T(8,128)} %split.2.refs_0_), channel_id=1, source_target_pairs={{0,16},{4,20},{8,24},{12,28},{16,0},{20,4},{24,8},{28,12},{1,17},{... | collective-permute-start | bytes 294920 | tf_op jit(solution)/shard_map/ppermute | solution.py:152
  22.6 0.6 %copy-start.6 = (f32[2,16,768]{2,1,0:T(8,128)}, f32[2,16,768]{2,1,0:T(8,128)S(1)}, u32[]{:S(2)}) copy-start(f32[2,16,768]{2,1,0:T(8,128)S(1)} %collective-permute-done.3.refs_1_) | copy-start | bytes 294916
  25.8 5.9 %collective-permute-start.4 = (f32[2,8,768]{2,1,0:T(8,128)}, f32[2,8,768]{2,1,0:T(8,128)S(1)}, u32[]{:S(2)}, u32[]{:S(2)}) collective-permute-start(f32[2,8,768]{2,1,0:T(8,128)} %get-tuple-element.8), channel_id=1, source_target_pairs={{0,1},{1,0},{2,3},{3,2},{4,5},{5,4},{6,7},{7,6},{8,9},{9,8},{10,11... | collective-permute-start | bytes 147464 | tf_op jit(solution)/shard_map/ppermute | solution.py:156
  29.1 5.6 %collective-permute-start.5 = (f32[2,8,768]{2,1,0:T(8,128)}, f32[2,8,768]{2,1,0:T(8,128)S(1)}, u32[]{:S(2)}, u32[]{:S(2)}) collective-permute-start(f32[2,8,768]{2,1,0:T(8,128)} %get-tuple-element.9), channel_id=1, source_target_pairs={{1,2},{2,1},{5,6},{6,5},{9,10},{10,9},{13,14},{14,13},{17,18},{18,... | collective-permute-start | bytes 147464 | tf_op jit(solution)/shard_map/ppermute | solution.py:161
  31.7 3.0 %copy-start.11 = (f32[2,8,768]{2,1,0:T(8,128)}, f32[2,8,768]{2,1,0:T(8,128)S(1)}, u32[]{:S(2)}) copy-start(f32[2,8,768]{2,1,0:T(8,128)S(1)} %collective-permute-done.4.pair) | copy-start | bytes 147460
  37.4 5.6 %collective-permute-start.8 = (f32[2,16,768]{2,1,0:T(8,128)}, f32[2,16,768]{2,1,0:T(8,128)S(1)}, u32[]{:S(2)}, u32[]{:S(2)}) collective-permute-start(f32[2,16,768]{2,1,0:T(8,128)} %get-tuple-element.11.refs_0_), channel_id=1, source_target_pairs={{0,16},{4,20},{8,24},{12,28},{16,0},{20,4},{24,8},{28,12},{1,17},{... | collective-permute-start | bytes 294920 | tf_op jit(solution)/shard_map/ppermute | solution.py:152
  46.2 4.0 %collective-permute-start.10 = (f32[2,16,768]{2,1,0:T(8,128)}, f32[2,16,768]{2,1,0:T(8,128)S(1)}, u32[]{:S(2)}, u32[]{:S(2)}) collective-permute-start(f32[2,16,768]{2,1,0:T(8,128)} %back.2.refs_0_), channel_id=1, source_target_pairs={{0,8},{4,12},{8,0},{12,4},{16,24},{20,28},{24,16},{28,20},{1,9},{5... | collective-permute-start | bytes 294920 | tf_op jit(solution)/shard_map/ppermute | solution.py:152
  46.2 5.6 %collective-permute-start.11 = (f32[2,16,768]{2,1,0:T(8,128)}, f32[2,16,768]{2,1,0:T(8,128)S(1)}, u32[]{:S(2)}, u32[]{:S(2)}) collective-permute-start(f32[2,16,768]{2,1,0:T(8,128)} %back.2.refs_0_), channel_id=1, source_target_pairs={{0,12},{4,8},{8,4},{12,0},{16,28},{20,24},{24,20},{28,16},{1,13},{... | collective-permute-start | bytes 294920 | tf_op jit(solution)/shard_map/ppermute | solution.py:152
  48.5 4.3 %collective-permute-start.9 = (f32[2,16,768]{2,1,0:T(8,128)}, f32[2,16,768]{2,1,0:T(8,128)S(1)}, u32[]{:S(2)}, u32[]{:S(2)}) collective-permute-start(f32[2,16,768]{2,1,0:T(8,128)} %back.2.refs_0_), channel_id=1, source_target_pairs={{0,4},{4,0},{8,12},{12,8},{16,20},{20,16},{24,28},{28,24},{1,5},{5... | collective-permute-start | bytes 294920 | tf_op jit(solution)/shard_map/ppermute | solution.py:152
  50.2 2.6 %copy-start.3 = (f32[2,16,768]{2,1,0:T(8,128)}, f32[2,16,768]{2,1,0:T(8,128)S(1)}, u32[]{:S(2)}) copy-start(f32[2,16,768]{2,1,0:T(8,128)S(1)} %collective-permute-done.10.refs_2_) | copy-start | bytes 294916
  51.8 1.0 %copy-start.4 = (f32[2,16,768]{2,1,0:T(8,128)}, f32[2,16,768]{2,1,0:T(8,128)S(1)}, u32[]{:S(2)}) copy-start(f32[2,16,768]{2,1,0:T(8,128)S(1)} %collective-permute-done.11.refs_3_) | copy-start | bytes 294916
  52.8 0.6 %copy-start.5 = (f32[2,16,768]{2,1,0:T(8,128)}, f32[2,16,768]{2,1,0:T(8,128)S(1)}, u32[]{:S(2)}) copy-start(f32[2,16,768]{2,1,0:T(8,128)S(1)} %collective-permute-done.9.refs_1_) | copy-start | bytes 294916
  (2 other events, 1.2 us)

commit v2 on v1

--- a/solution.py
+++ b/solution.py
@@ -36,7 +36,7 @@
 def level_forward(level, block, own, partner, out, params):
     weight, offset, source = params
     views, _, columns = own.shape
-    taps = weight.shape[3]
+    taps = weight.shape[2]
     for v in range(views):
         row = block * views + v
         total = [None] * (columns // LANES)
@@ -45,7 +45,7 @@
             total = shifted_sum(
                 held[source[level, channel, row]],
                 [begin + k for k in range(taps)],
-                [weight[level, channel, row, k] for k in range(taps)],
+                [weight[level, channel, k, row] for k in range(taps)],
                 total,
             )
         out[v] = join(total)
@@ -54,7 +54,7 @@
 def level_back(level, block, own, partner, out, params):
     weight, offset, source = params
     views, _, columns = own.shape
-    taps = weight.shape[3]
+    taps = weight.shape[2]
     out[...] = jnp.zeros(out.shape, jnp.float32)
     for channel, held in enumerate((own, partner)):
         owner = block ^ (channel << level)
@@ -64,7 +64,7 @@
             total = shifted_sum(
                 held[v],
                 [-begin - k for k in range(taps)],
-                [weight[level, channel, row, k] for k in range(taps)],
+                [weight[level, channel, k, row] for k in range(taps)],
                 [None] * (columns // LANES),
             )
             target = source[level, channel, row]
@@ -142,6 +142,7 @@
 
 SCALARS = pl.BlockSpec(memory_space=pltpu.SMEM)
 BLOCK = pl.BlockSpec(memory_space=pltpu.VMEM)
+SMALL = pltpu.CompilerParams(vmem_limit_bytes=8 << 20)
 
 
 def shaped(*shape):
@@ -173,7 +174,7 @@
     reach = cone_weight.shape[1] // 2
     level_count = lax.axis_size("view").bit_length() - 1
     groups = [tuple(range(i, min(i + 2, level_count))) for i in range(0, level_count, 2)]
-    params = (interp_weight, shift_offset, source_view)
+    params = (jnp.swapaxes(interp_weight, 2, 3), shift_offset, source_view)
     whole = shaped(views, planes, columns)
     part = shaped(views, 2 * reach, columns)
     scratch = [pltpu.VMEM((views, planes, columns), jnp.float32)] * 2
@@ -197,6 +198,7 @@
             in_specs=[SCALARS] * 3 + [BLOCK] * len(states),
             out_specs=[BLOCK] * (1 + 2 * last),
             scratch_shapes=scratch if len(levels) == 2 else [],
+            compiler_params=SMALL,
             name="split",
         )(*params, *states)
         if last:
@@ -213,6 +215,7 @@
             pltpu.VMEM((views, planes + 4 * reach, columns), jnp.float32),
             pltpu.VMEM((views, planes + 2 * reach, columns), jnp.float32),
         ],
+        compiler_params=SMALL,
         name="tilt",
     )(cone_weight, split, with_pair(to_pair), across_pairs(to_across), both[0], both[1])
 
@@ -226,6 +229,7 @@
             in_specs=[SCALARS] * 3 + [BLOCK] * (len(states) + last),
             out_specs=BLOCK,
             scratch_shapes=scratch if len(levels) == 2 else [],
+            compiler_params=SMALL,
             name="back",
         )(*params, *states, *([leaf_coeffs] if last else []))
     return (residual, state)

time: 57 us -> 47.9 us (0.84)
  Pallas kernels: 13.3 us -> 7.52 us
  local copies, waits for them, and re-layouts: 4.65 us -> 0.74 us
  waiting for transfers between devices: 17.9 us -> 18.5 us
    unnamed x29 -> x14, local copies, waits for them, and re-layouts: 3.92 us -> 0.71 us
    pallas_call x2, Pallas kernels: 5.6 us -> 2.68 us  [body(): pl.pallas_call(functools.partial(forward_kernel, levels, len(states), las...]
    pallas_call x2, Pallas kernels: 5.56 us -> 3.29 us  [body(): pl.pallas_call(functools.partial(back_kernel, levels, len(states), last),...]
    squeeze x1, local copies, waits for them, and re-layouts: 0.73 us -> 0.02 us  [body(): both[1]]
    pallas_call x1, Pallas kernels: 2.12 us -> 1.55 us  [body(): pl.pallas_call(tilt_kernel, out_shape=[whole, whole], in_specs=[SCALARS]...]
  transfers between devices with their start and end apart: 12 -> 12, of which waited for: 9 -> 9; matrix products, arithmetic and copies ran while one was open for 3% -> 0% of each run, Pallas kernels for 0% -> 0%
where the time goes in v2:
time: 47.9 us; the launch traced here: 47.6 us
  starting transfers between devices  19.1 us (40%)
  waiting for transfers between devices  18.5 us (39%)
  Pallas kernels  7.52 us (16%)
  other arithmetic  0.96 us (2%)
  between operations  0.8 us (2%)
  local copies, waits for them, and re-layouts  0.74 us (2%)
    ppermute x8, waiting for transfers between devices, across_view(): lax.ppermute(x, 'view', [(i, i ^ apart) for i in range(lax.axis_size('vie...  15 us
    ppermute x8, starting transfers between devices, across_view(): lax.ppermute(x, 'view', [(i, i ^ apart) for i in range(lax.axis_size('vie...  9.15 us
    ppermute x2, starting transfers between devices, across_pairs(): lax.ppermute(x, 'slab', [(i, i + 1) for i in lower] + [(i + 1, i) for i i...  6.58 us
    ppermute x2, waiting for transfers between devices, across_pairs(): lax.ppermute(x, 'slab', [(i, i + 1) for i in lower] + [(i + 1, i) for i i...  3.44 us
    ppermute x2, starting transfers between devices, with_pair(): lax.ppermute(x, 'slab', [(i, i ^ 1) for i in range(lax.axis_size('slab'))])  3.42 us
    pallas_call x2, Pallas kernels, body(): pl.pallas_call(functools.partial(back_kernel, levels, len(states), last),...  3.29 us
    pallas_call x2, Pallas kernels, body(): pl.pallas_call(functools.partial(forward_kernel, levels, len(states), las...  2.68 us
    pallas_call x1, Pallas kernels, body(): pl.pallas_call(tilt_kernel, out_shape=[whole, whole], in_specs=[SCALARS]...  1.55 us
  transfers between devices with their start and end apart: 12, of which 9 were waited for; matrix products, arithmetic and copies ran while one was open for 0% of the time, Pallas kernels for 0%

profile of v2, /device:TPU:1, one launch (start us, length us, event | category | flops | bytes accessed | tf_op | source)
XLA Modules:
  0.0 47.6 jit_solution(12130666182425829246)
XLA Ops:
  0.6 0.9 %broadcast_select_fusion.3 = (f32[2,2,4,768]{3,2,1,0:T(4,128)S(1)}, f32[2,2,4,768]{3,2,1,0:T(4,128)S(1)}, f32[2,2,4,768]{3,2,1,0:T(4,128)S(1)}) fusion(pred[]{:T(512)S(6)} %eq.5, f32[1,2,16,768]{3,2,1,0:T(8,128)} %bitcast.18, f32[1,2,16,768]{3,2,1,0:T(8,128)} %bitcast.20), kind=kLoop, calls=%fused_computation.8 | loop fusion | flops 36864 | bytes 344065 | tf_op jit(solution)/shard_map/jit(_where)/select_n | solution.py:185
  1.6 4.7 %collective-permute-start.7 = (f32[2,2,4,768]{3,2,1,0:T(4,128)S(1)}, f32[2,2,4,768]{3,2,1,0:T(4,128)S(1)}, u32[]{:S(2)}, u32[]{:S(2)}) collective-permute-start(f32[2,2,4,768]{3,2,1,0:T(4,128)S(1)} %bitcast.28), channel_id=1, source_target_pairs={{1,2},{2,1},{5,6},{6,5},{9,10},{10,9},{13,14},{14,13},{17,18},{18,... | collective-permute-start | bytes 147464 | tf_op jit(solution)/shard_map/ppermute | solution.py:162
  6.3 1.3 %collective-permute-start = (f32[2,16,768]{2,1,0:T(8,128)S(1)}, f32[2,16,768]{2,1,0:T(8,128)S(1)}, u32[]{:S(2)}, u32[]{:S(2)}) collective-permute-start(f32[2,16,768]{2,1,0:T(8,128)S(1)} %copy-done), channel_id=1, source_target_pairs={{0,4},{4,0},{8,12},{12,8},{16,20},{20,16},{24,28},{28,24},{1,5},{5... | collective-permute-start | bytes 294920 | tf_op jit(solution)/shard_map/ppermute | solution.py:153
  7.6 1.3 %collective-permute-start.1 = (f32[2,16,768]{2,1,0:T(8,128)S(1)}, f32[2,16,768]{2,1,0:T(8,128)S(1)}, u32[]{:S(2)}, u32[]{:S(2)}) collective-permute-start(f32[2,16,768]{2,1,0:T(8,128)S(1)} %copy-done), channel_id=1, source_target_pairs={{0,8},{4,12},{8,0},{12,4},{16,24},{20,28},{24,16},{28,20},{1,9},{5... | collective-permute-start | bytes 294920 | tf_op jit(solution)/shard_map/ppermute | solution.py:153
  9.1 1.2 %collective-permute-done.refs_1_ = f32[2,16,768]{2,1,0:T(8,128)S(1)} collective-permute-done((f32[2,16,768]{2,1,0:T(8,128)S(1)}, f32[2,16,768]{2,1,0:T(8,128)S(1)}, u32[]{:S(2)}, u32[]{:S(2)}) %collective-permute-start) | collective-permute-done | bytes 98336 | tf_op jit(solution)/shard_map/ppermute | solution.py:153
  10.3 0.9 %collective-permute-done.1.refs_2_ = f32[2,16,768]{2,1,0:T(8,128)S(1)} collective-permute-done((f32[2,16,768]{2,1,0:T(8,128)S(1)}, f32[2,16,768]{2,1,0:T(8,128)S(1)}, u32[]{:S(2)}, u32[]{:S(2)}) %collective-permute-start.1) | collective-permute-done | bytes 98336 | tf_op jit(solution)/shard_map/ppermute | solution.py:153
  11.2 2.1 %collective-permute-done.2.refs_3_ = f32[2,16,768]{2,1,0:T(8,128)S(1)} collective-permute-done((f32[2,16,768]{2,1,0:T(8,128)S(1)}, f32[2,16,768]{2,1,0:T(8,128)S(1)}, u32[]{:S(2)}, u32[]{:S(2)}) %collective-permute-start.2) | collective-permute-done | bytes 98336 | tf_op jit(solution)/shard_map/ppermute | solution.py:153
  13.3 1.5 %split.2.refs_0_ = f32[2,16,768]{2,1,0:T(8,128)S(1)} custom-call(f32[3,2,4,16]{3,2,1,0:T(4,128)S(1)} %bitcast.14, s32[3,2,16]{2,1,0:T(2,128)S(1)} %copy-done.2, s32[3,2,16]{2,1,0:T(2,128)S(1)} %copy-done.3, f32[2,16,768]{2,1,0:T(8,128)S(1)} %copy-done, f32[2,16,768]{2,1,0:T(8,128)S(1)} %collective-permute-done.refs_1_, ...), custom_call_target="tpu_custom_call" | custom-call | tf_op jit(solution)/shard_map/split/pallas_call | solution.py:195
  14.9 2.4 %collective-permute-start.3 = (f32[2,16,768]{2,1,0:T(8,128)S(1)}, f32[2,16,768]{2,1,0:T(8,128)S(1)}, u32[]{:S(2)}, u32[]{:S(2)}) collective-permute-start(f32[2,16,768]{2,1,0:T(8,128)S(1)} %split.2.refs_0_), channel_id=1, source_target_pairs={{0,16},{4,20},{8,24},{12,28},{16,0},{20,4},{24,8},{28,12},{1,17},{... | collective-permute-start | bytes 294920 | tf_op jit(solution)/shard_map/ppermute | solution.py:153
  17.3 3.1 %collective-permute-done.3.refs_1_ = f32[2,16,768]{2,1,0:T(8,128)S(1)} collective-permute-done((f32[2,16,768]{2,1,0:T(8,128)S(1)}, f32[2,16,768]{2,1,0:T(8,128)S(1)}, u32[]{:S(2)}, u32[]{:S(2)}) %collective-permute-start.3) | collective-permute-done | bytes 98336 | tf_op jit(solution)/shard_map/ppermute | solution.py:153
  20.4 1.1 %split.3 = (f32[2,16,768]{2,1,0:T(8,128)S(1)}, f32[2,8,768]{2,1,0:T(8,128)S(1)}, f32[2,8,768]{2,1,0:T(8,128)S(1)}) custom-call(f32[3,2,4,16]{3,2,1,0:T(4,128)S(1)} %bitcast.15, s32[3,2,16]{2,1,0:T(2,128)S(1)} %copy-done.2, s32[3,2,16]{2,1,0:T(2,128)S(1)} %copy-done.3, f32[2,16,768]{2,1,0:T(8,128)S(1)} %split.2.refs_0_, ...), custom_call_target="tpu_custom_call" | custom-call | tf_op jit(solution)/shard_map/split/pallas_call | solution.py:195
  21.5 3.3 %collective-permute-start.4 = (f32[2,8,768]{2,1,0:T(8,128)S(1)}, f32[2,8,768]{2,1,0:T(8,128)S(1)}, u32[]{:S(2)}, u32[]{:S(2)}) collective-permute-start(f32[2,8,768]{2,1,0:T(8,128)S(1)} %get-tuple-element.8), channel_id=1, source_target_pairs={{0,1},{1,0},{2,3},{3,2},{4,5},{5,4},{6,7},{7,6},{8,9},{9,8},{10,11... | collective-permute-start | bytes 147464 | tf_op jit(solution)/shard_map/ppermute | solution.py:157
  24.8 1.9 %collective-permute-start.5 = (f32[2,8,768]{2,1,0:T(8,128)S(1)}, f32[2,8,768]{2,1,0:T(8,128)S(1)}, u32[]{:S(2)}, u32[]{:S(2)}) collective-permute-start(f32[2,8,768]{2,1,0:T(8,128)S(1)} %get-tuple-element.9), channel_id=1, source_target_pairs={{1,2},{2,1},{5,6},{6,5},{9,10},{10,9},{13,14},{14,13},{17,18},{18,... | collective-permute-start | bytes 147464 | tf_op jit(solution)/shard_map/ppermute | solution.py:162
  26.8 3.4 %collective-permute-done.5.across = f32[2,8,768]{2,1,0:T(8,128)S(1)} collective-permute-done((f32[2,8,768]{2,1,0:T(8,128)S(1)}, f32[2,8,768]{2,1,0:T(8,128)S(1)}, u32[]{:S(2)}, u32[]{:S(2)}) %collective-permute-start.5) | collective-permute-done | bytes 49184 | tf_op jit(solution)/shard_map/ppermute | solution.py:162
  30.2 0.7 %copy-done.4 = f32[2,9]{1,0:T(2,128)S(1)} copy-done((f32[2,9]{1,0:T(2,128)S(1)}, f32[2,9]{1,0:T(2,128)}, u32[]{:S(2)}) %copy-start.4) | copy-done | bytes 96
  30.9 1.5 %tilt.1 = (f32[2,16,768]{2,1,0:T(8,128)}, f32[2,16,768]{2,1,0:T(8,128)S(1)}) custom-call(f32[2,9]{1,0:T(2,128)S(1)} %copy-done.4, f32[2,16,768]{2,1,0:T(8,128)S(1)} %get-tuple-element.7.split, f32[2,8,768]{2,1,0:T(8,128)S(1)} %collective-permute-done.4.pair, f32[2,8,768]{2,1,0:T(8,128)S(1)} %collective-permute-done.5.across, ...), custom_call_target="tpu_custom_call" | custom-call | tf_op jit(solution)/shard_map/tilt/pallas_call | solution.py:209
  32.5 1.4 %collective-permute-start.8 = (f32[2,16,768]{2,1,0:T(8,128)S(1)}, f32[2,16,768]{2,1,0:T(8,128)S(1)}, u32[]{:S(2)}, u32[]{:S(2)}) collective-permute-start(f32[2,16,768]{2,1,0:T(8,128)S(1)} %get-tuple-element.11.refs_0_), channel_id=1, source_target_pairs={{0,16},{4,20},{8,24},{12,28},{16,0},{20,4},{24,8},{28,12},{1,17},{... | collective-permute-start | bytes 294920 | tf_op jit(solution)/shard_map/ppermute | solution.py:153
  33.8 4.1 %collective-permute-done.8.refs_1_ = f32[2,16,768]{2,1,0:T(8,128)S(1)} collective-permute-done((f32[2,16,768]{2,1,0:T(8,128)S(1)}, f32[2,16,768]{2,1,0:T(8,128)S(1)}, u32[]{:S(2)}, u32[]{:S(2)}) %collective-permute-start.8) | collective-permute-done | bytes 98336 | tf_op jit(solution)/shard_map/ppermute | solution.py:153
  37.9 1.1 %back.2.refs_0_ = f32[2,16,768]{2,1,0:T(8,128)S(1)} custom-call(f32[3,2,4,16]{3,2,1,0:T(4,128)S(1)} %bitcast.16, s32[3,2,16]{2,1,0:T(2,128)S(1)} %copy-done.2, s32[3,2,16]{2,1,0:T(2,128)S(1)} %copy-done.3, f32[2,16,768]{2,1,0:T(8,128)S(1)} %get-tuple-element.11.refs_0_, f32[2,16,768]{2,1,0:T(8,128)S(1)} %collective-permute-done.8.refs_1_), custom_call_target="tpu_custom_call" | custom-call | tf_op jit(solution)/shard_map/back/pallas_call | solution.py:226
  39.1 2.3 %collective-permute-start.11 = (f32[2,16,768]{2,1,0:T(8,128)S(1)}, f32[2,16,768]{2,1,0:T(8,128)S(1)}, u32[]{:S(2)}, u32[]{:S(2)}) collective-permute-start(f32[2,16,768]{2,1,0:T(8,128)S(1)} %back.2.refs_0_), channel_id=1, source_target_pairs={{0,12},{4,8},{8,4},{12,0},{16,28},{20,24},{24,20},{28,16},{1,13},{... | collective-permute-start | bytes 294920 | tf_op jit(solution)/shard_map/ppermute | solution.py:153
  41.7 1.1 %collective-permute-done.10.refs_2_ = f32[2,16,768]{2,1,0:T(8,128)S(1)} collective-permute-done((f32[2,16,768]{2,1,0:T(8,128)S(1)}, f32[2,16,768]{2,1,0:T(8,128)S(1)}, u32[]{:S(2)}, u32[]{:S(2)}) %collective-permute-start.10) | collective-permute-done | bytes 98336 | tf_op jit(solution)/shard_map/ppermute | solution.py:153
  42.8 1.7 %collective-permute-done.11.refs_3_ = f32[2,16,768]{2,1,0:T(8,128)S(1)} collective-permute-done((f32[2,16,768]{2,1,0:T(8,128)S(1)}, f32[2,16,768]{2,1,0:T(8,128)S(1)}, u32[]{:S(2)}, u32[]{:S(2)}) %collective-permute-start.11) | collective-permute-done | bytes 98336 | tf_op jit(solution)/shard_map/ppermute | solution.py:153
  44.5 1.0 %collective-permute-done.9.refs_1_ = f32[2,16,768]{2,1,0:T(8,128)S(1)} collective-permute-done((f32[2,16,768]{2,1,0:T(8,128)S(1)}, f32[2,16,768]{2,1,0:T(8,128)S(1)}, u32[]{:S(2)}, u32[]{:S(2)}) %collective-permute-start.9) | collective-permute-done | bytes 98336 | tf_op jit(solution)/shard_map/ppermute | solution.py:153
  45.5 2.2 %back.3 = f32[2,16,768]{2,1,0:T(8,128)} custom-call(f32[3,2,4,16]{3,2,1,0:T(4,128)S(1)} %bitcast.17, s32[3,2,16]{2,1,0:T(2,128)S(1)} %copy-done.2, s32[3,2,16]{2,1,0:T(2,128)S(1)} %copy-done.3, f32[2,16,768]{2,1,0:T(8,128)S(1)} %back.2.refs_0_, f32[2,16,768]{2,1,0:T(8,128)S(1)} %collective-permute-done.9.refs_1_, ...), custom_call_target="tpu_custom_call" | custom-call | tf_op jit(solution)/shard_map/back/pallas_call | solution.py:226
  (24 shorter events, 0.8 us)
Async XLA Ops:
  1.5 4.8 %copy-start = (f32[2,16,768]{2,1,0:T(8,128)S(1)}, f32[2,16,768]{2,1,0:T(8,128)}, u32[]{:S(2)}) copy-start(f32[2,16,768]{2,1,0:T(8,128)} %refs_4_.1) | copy-start | bytes 294916
  1.6 7.5 %collective-permute-start.7 = (f32[2,2,4,768]{3,2,1,0:T(4,128)S(1)}, f32[2,2,4,768]{3,2,1,0:T(4,128)S(1)}, u32[]{:S(2)}, u32[]{:S(2)}) collective-permute-start(f32[2,2,4,768]{3,2,1,0:T(4,128)S(1)} %bitcast.28), channel_id=1, source_target_pairs={{1,2},{2,1},{5,6},{6,5},{9,10},{10,9},{13,14},{14,13},{17,18},{18,... | collective-permute-start | bytes 147464 | tf_op jit(solution)/shard_map/ppermute | solution.py:162
  6.2 2.8 %collective-permute-start.6 = (f32[2,2,4,768]{3,2,1,0:T(4,128)S(1)}, f32[2,2,4,768]{3,2,1,0:T(4,128)S(1)}, u32[]{:S(2)}, u32[]{:S(2)}) collective-permute-start(f32[2,2,4,768]{3,2,1,0:T(4,128)S(1)} %get-tuple-element.12), channel_id=1, source_target_pairs={{0,1},{1,0},{2,3},{3,2},{4,5},{5,4},{6,7},{7,6},{8,9},{9,8},{10,11... | collective-permute-start | bytes 147464 | tf_op jit(solution)/shard_map/ppermute | solution.py:157
  6.3 4.0 %collective-permute-start = (f32[2,16,768]{2,1,0:T(8,128)S(1)}, f32[2,16,768]{2,1,0:T(8,128)S(1)}, u32[]{:S(2)}, u32[]{:S(2)}) collective-permute-start(f32[2,16,768]{2,1,0:T(8,128)S(1)} %copy-done), channel_id=1, source_target_pairs={{0,4},{4,0},{8,12},{12,8},{16,20},{20,16},{24,28},{28,24},{1,5},{5... | collective-permute-start | bytes 294920 | tf_op jit(solution)/shard_map/ppermute | solution.py:153
  7.6 3.6 %collective-permute-start.1 = (f32[2,16,768]{2,1,0:T(8,128)S(1)}, f32[2,16,768]{2,1,0:T(8,128)S(1)}, u32[]{:S(2)}, u32[]{:S(2)}) collective-permute-start(f32[2,16,768]{2,1,0:T(8,128)S(1)} %copy-done), channel_id=1, source_target_pairs={{0,8},{4,12},{8,0},{12,4},{16,24},{20,28},{24,16},{28,20},{1,9},{5... | collective-permute-start | bytes 294920 | tf_op jit(solution)/shard_map/ppermute | solution.py:153
  8.9 4.4 %collective-permute-start.2 = (f32[2,16,768]{2,1,0:T(8,128)S(1)}, f32[2,16,768]{2,1,0:T(8,128)S(1)}, u32[]{:S(2)}, u32[]{:S(2)}) collective-permute-start(f32[2,16,768]{2,1,0:T(8,128)S(1)} %copy-done), channel_id=1, source_target_pairs={{0,12},{4,8},{8,4},{12,0},{16,28},{20,24},{24,20},{28,16},{1,13},{... | collective-permute-start | bytes 294920 | tf_op jit(solution)/shard_map/ppermute | solution.py:153
  9.1 4.2 %copy-start.1 = (f32[3,2,16,4]{2,3,1,0:T(4,128)S(1)}, f32[3,2,16,4]{2,3,1,0:T(4,128)}, u32[]{:S(2)}) copy-start(f32[3,2,16,4]{2,3,1,0:T(4,128)} %param.11) | copy-start | bytes 4612
  9.1 4.2 %copy-start.2 = (s32[3,2,16]{2,1,0:T(2,128)S(1)}, s32[3,2,16]{2,1,0:T(2,128)}, u32[]{:S(2)}) copy-start(s32[3,2,16]{2,1,0:T(2,128)} %offset.7) | copy-start | bytes 1156
  9.1 4.2 %copy-start.3 = (s32[3,2,16]{2,1,0:T(2,128)S(1)}, s32[3,2,16]{2,1,0:T(2,128)}, u32[]{:S(2)}) copy-start(s32[3,2,16]{2,1,0:T(2,128)} %source.7) | copy-start | bytes 1156
  13.3 4.0 %copy-start.5 = (f32[2,16,768]{2,1,0:T(8,128)S(1)}, f32[2,16,768]{2,1,0:T(8,128)}, u32[]{:S(2)}) copy-start(f32[2,16,768]{2,1,0:T(8,128)} %param.9) | copy-start | bytes 294916
  13.3 3.9 %copy-start.6 = (f32[2,16,768]{2,1,0:T(8,128)S(1)}, f32[2,16,768]{2,1,0:T(8,128)}, u32[]{:S(2)}) copy-start(f32[2,16,768]{2,1,0:T(8,128)} %param.8) | copy-start | bytes 294916
  14.9 5.5 %collective-permute-start.3 = (f32[2,16,768]{2,1,0:T(8,128)S(1)}, f32[2,16,768]{2,1,0:T(8,128)S(1)}, u32[]{:S(2)}, u32[]{:S(2)}) collective-permute-start(f32[2,16,768]{2,1,0:T(8,128)S(1)} %split.2.refs_0_), channel_id=1, source_target_pairs={{0,16},{4,20},{8,24},{12,28},{16,0},{20,4},{24,8},{28,12},{1,17},{... | collective-permute-start | bytes 294920 | tf_op jit(solution)/shard_map/ppermute | solution.py:153
  21.5 5.3 %collective-permute-start.4 = (f32[2,8,768]{2,1,0:T(8,128)S(1)}, f32[2,8,768]{2,1,0:T(8,128)S(1)}, u32[]{:S(2)}, u32[]{:S(2)}) collective-permute-start(f32[2,8,768]{2,1,0:T(8,128)S(1)} %get-tuple-element.8), channel_id=1, source_target_pairs={{0,1},{1,0},{2,3},{3,2},{4,5},{5,4},{6,7},{7,6},{8,9},{9,8},{10,11... | collective-permute-start | bytes 147464 | tf_op jit(solution)/shard_map/ppermute | solution.py:157
  24.8 5.4 %collective-permute-start.5 = (f32[2,8,768]{2,1,0:T(8,128)S(1)}, f32[2,8,768]{2,1,0:T(8,128)S(1)}, u32[]{:S(2)}, u32[]{:S(2)}) collective-permute-start(f32[2,8,768]{2,1,0:T(8,128)S(1)} %get-tuple-element.9), channel_id=1, source_target_pairs={{1,2},{2,1},{5,6},{6,5},{9,10},{10,9},{13,14},{14,13},{17,18},{18,... | collective-permute-start | bytes 147464 | tf_op jit(solution)/shard_map/ppermute | solution.py:162
  30.2 0.7 %copy-start.4 = (f32[2,9]{1,0:T(2,128)S(1)}, f32[2,9]{1,0:T(2,128)}, u32[]{:S(2)}) copy-start(f32[2,9]{1,0:T(2,128)} %cone.1) | copy-start | bytes 220
  32.5 5.4 %collective-permute-start.8 = (f32[2,16,768]{2,1,0:T(8,128)S(1)}, f32[2,16,768]{2,1,0:T(8,128)S(1)}, u32[]{:S(2)}, u32[]{:S(2)}) collective-permute-start(f32[2,16,768]{2,1,0:T(8,128)S(1)} %get-tuple-element.11.refs_0_), channel_id=1, source_target_pairs={{0,16},{4,20},{8,24},{12,28},{16,0},{20,4},{24,8},{28,12},{1,17},{... | collective-permute-start | bytes 294920 | tf_op jit(solution)/shard_map/ppermute | solution.py:153
  39.0 3.8 %collective-permute-start.10 = (f32[2,16,768]{2,1,0:T(8,128)S(1)}, f32[2,16,768]{2,1,0:T(8,128)S(1)}, u32[]{:S(2)}, u32[]{:S(2)}) collective-permute-start(f32[2,16,768]{2,1,0:T(8,128)S(1)} %back.2.refs_0_), channel_id=1, source_target_pairs={{0,8},{4,12},{8,0},{12,4},{16,24},{20,28},{24,16},{28,20},{1,9},{5... | collective-permute-start | bytes 294920 | tf_op jit(solution)/shard_map/ppermute | solution.py:153
  39.1 5.4 %collective-permute-start.11 = (f32[2,16,768]{2,1,0:T(8,128)S(1)}, f32[2,16,768]{2,1,0:T(8,128)S(1)}, u32[]{:S(2)}, u32[]{:S(2)}) collective-permute-start(f32[2,16,768]{2,1,0:T(8,128)S(1)} %back.2.refs_0_), channel_id=1, source_target_pairs={{0,12},{4,8},{8,4},{12,0},{16,28},{20,24},{24,20},{28,16},{1,13},{... | collective-permute-start | bytes 294920 | tf_op jit(solution)/shard_map/ppermute | solution.py:153
  41.4 4.1 %collective-permute-start.9 = (f32[2,16,768]{2,1,0:T(8,128)S(1)}, f32[2,16,768]{2,1,0:T(8,128)S(1)}, u32[]{:S(2)}, u32[]{:S(2)}) collective-permute-start(f32[2,16,768]{2,1,0:T(8,128)S(1)} %back.2.refs_0_), channel_id=1, source_target_pairs={{0,4},{4,0},{8,12},{12,8},{16,20},{20,16},{24,28},{28,24},{1,5},{5... | collective-permute-start | bytes 294920 | tf_op jit(solution)/shard_map/ppermute | solution.py:153

commit v3 on v1

v3 whole, which is shorter than its diff:
```python
import functools

import jax
import jax.numpy as jnp
from jax import lax
from jax.experimental import pallas as pl
from jax.experimental.pallas import tpu as pltpu
from jax.sharding import PartitionSpec as P

LANES = 128
SCALARS = pl.BlockSpec(memory_space=pltpu.SMEM)
BLOCK = pl.BlockSpec(memory_space=pltpu.VMEM)
SMALL = pltpu.CompilerParams(vmem_limit_bytes=8 << 20)


def shifted_sum(rows, moves, weights, total):
    planes, columns = rows.shape
    count = columns // LANES
    tiles = [rows[:, LANES * j : LANES * (j + 1)] for j in range(count)]
    lane = lax.broadcasted_iota(jnp.int32, (planes, LANES), 1)
    nothing = jnp.zeros((planes, LANES), jnp.float32)
    for move, weight in zip(moves, weights):
        turned = [pltpu.roll(tile, (LANES - move) & (LANES - 1), 1) for tile in tiles]
        below = lane + move < 0
        above = lane + move >= LANES
        for j in range(count):
            left = turned[j - 1] if j > 0 else nothing
            right = turned[j + 1] if j + 1 < count else nothing
            term = weight * jnp.where(below, left, jnp.where(above, right, turned[j]))
            total[j] = term if total[j] is None else total[j] + term
    return total


def table_kernel(entries, views, weight, offset, source, whole_numbers, weights):
    me = lax.axis_index("view")
    taps = weight.shape[2]
    for index, (level, channel, apart, direction) in enumerate(entries):
        for v in range(views):
            row = (me ^ apart) * views + v
            at = index * views + v
            begin = offset[level, channel, row] * direction
            whole_numbers[2 * at, :] = jnp.full((LANES,), begin, jnp.int32)
            whole_numbers[2 * at + 1, :] = jnp.full((LANES,), source[level, channel, row], jnp.int32)
            for k in range(taps):
                weights[at * taps + k, :] = jnp.full((LANES,), weight[level, channel, k, row])


def level_part(index, direction, whole_numbers, weights, given, base, out):
    views, planes, columns = given.shape
    taps = weights.shape[0] // (whole_numbers.shape[0] // 2)
    count = columns // LANES
    if direction < 0:
        out[...] = jnp.zeros(out.shape, jnp.float32) if base is None else base[...]
    for v in range(views):
        at = index * views + v
        begin, source = whole_numbers[2 * at, 0], whole_numbers[2 * at + 1, 0]
        moves = [begin + direction * k for k in range(taps)]
        factors = [
            jnp.broadcast_to(weights[pl.ds(at * taps + k, 1), :], (planes, LANES))
            for k in range(taps)
        ]
        if direction > 0:
            total = [None] * count
            if base is not None:
                total = [base[v, :, LANES * j : LANES * (j + 1)] for j in range(count)]
            total = shifted_sum(given[source], moves, factors, total)
            for j in range(count):
                out[v, :, LANES * j : LANES * (j + 1)] = total[j]
        else:
            total = shifted_sum(given[v], moves, factors, [None] * count)
            out[source] = out[source] + jnp.concatenate(total, axis=1)


def part_kernel(index, direction, based, whole_numbers, weights, given, *refs):
    level_part(index, direction, whole_numbers, weights, given, refs[0] if based else None, refs[-1])


def two_kernel(first, second, direction, whole_numbers, weights, given, base, other, out, between):
    level_part(first, direction, whole_numbers, weights, given, base, between)
    level_part(second, direction, whole_numbers, weights, between, other, out)


def edges_kernel(index, whole_numbers, weights, given, base, out, pair, across):
    level_part(index, 1, whole_numbers, weights, given, base, out)
    width = pair.shape[1]
    planes = out.shape[1]
    odd = lax.axis_index("slab") % 2
    pair[...] = out[:, pl.ds(pl.multiple_of((1 - odd) * (planes - width), 8), width), :]
    across[...] = out[:, pl.ds(pl.multiple_of(odd * (planes - width), 8), width), :]


def tilt_kernel(cone, split, pair, across, measured, ray, residual, cotangent, wide, weighted):
    views, planes, columns = split.shape
    width = pair.shape[1]
    crossed = cone.shape[0] // views
    reach = crossed // 2
    odd = lax.axis_index("slab") % 2
    far = planes + width
    wide[:, pl.ds(width, planes), :] = split[...]
    wide[:, pl.ds(pl.multiple_of((1 - odd) * far, 8), width), :] = pair[...]
    wide[:, pl.ds(pl.multiple_of(odd * far, 8), width), :] = across[...]
    extended = planes + 2 * reach
    for v in range(views):
        factors = [cone[pl.ds(v * crossed + e, 1), :] for e in range(crossed)]
        for j in range(columns // LANES):
            at = pl.ds(LANES * j, LANES)
            total = factors[0] * wide[v, pl.ds(width - 2 * reach, extended), at]
            for e in range(1, crossed):
                total = total + factors[e] * wide[v, pl.ds(width - 2 * reach + e, extended), at]
            left = measured[v, :, at] - total
            residual[v, :, at] = left[reach : reach + planes]
            weighted[v, :, at] = ray[v, :, at] * left
            total = factors[0] * weighted[v, pl.ds(2 * reach, planes), at]
            for e in range(1, crossed):
                total = total + factors[e] * weighted[v, pl.ds(2 * reach - e, planes), at]
            cotangent[v, :, at] = total


def shaped(*shape, dtype=jnp.float32):
    return jax.ShapeDtypeStruct(shape, dtype)


def call(kernel, out_shape, *args, scratch=(), specs=None, name):
    return pl.pallas_call(
        kernel,
        out_shape=out_shape,
        in_specs=[BLOCK] * len(args) if specs is None else specs,
        out_specs=jax.tree.map(lambda _: BLOCK, out_shape),
        scratch_shapes=scratch,
        compiler_params=SMALL,
        name=name,
    )(*args)


def across_view(x, apart):
    return lax.ppermute(x, "view", [(i, i ^ apart) for i in range(lax.axis_size("view"))])


def with_pair(x):
    return lax.ppermute(x, "slab", [(i, i ^ 1) for i in range(lax.axis_size("slab"))])


def across_pairs(x):
    lower = range(1, lax.axis_size("slab") - 1, 2)
    return lax.ppermute(x, "slab", [(i, i + 1) for i in lower] + [(i + 1, i) for i in lower])


def after(x, *earlier):
    return lax.optimization_barrier((x, *earlier))[0]


def body(leaf_coeffs, measured, ray_weight, cone_weight, interp_weight, shift_offset, source_view):
    views, planes, columns = leaf_coeffs.shape
    crossed = cone_weight.shape[1]
    reach = crossed // 2
    taps = interp_weight.shape[3]
    level_count = lax.axis_size("view").bit_length() - 1
    groups = [tuple(range(i, min(i + 2, level_count))) for i in range(0, level_count, 2)]
    whole = shaped(views, planes, columns)
    part = shaped(views, 2 * reach, columns)
    scratch = [pltpu.VMEM((views, planes, columns), jnp.float32)]

    entries = []

    def entry(level, channel, apart, direction):
        entries.append((level, channel, apart, direction))
        return len(entries) - 1

    forward_entries, back_entries = {}, {}
    for levels in groups:
        low, high = levels[0], levels[-1]
        shapes = [(low, 0), (low, 1)]
        if len(levels) == 2:
            shapes = [(low, 0), (low, 1 << high), (high, 0)]
            backs = [(high, 0), (high, 1 << low), (low, 0)]
        else:
            shapes = backs = [(low, 0)]
        forward_entries[levels] = [
            [entry(level, channel, apart, 1) for channel in (0, 1)] for level, apart in shapes
        ]
        back_entries[levels] = [
            [entry(level, channel, apart ^ (channel << level), -1) for channel in (0, 1)]
            for level, apart in backs
        ]
    tables = call(
        functools.partial(table_kernel, entries, views),
        [
            shaped(len(entries) * views * 2, LANES, dtype=jnp.int32),
            shaped(len(entries) * views * taps, LANES),
        ],
        jnp.swapaxes(interp_weight, 2, 3),
        shift_offset,
        source_view,
        specs=[SCALARS] * 3,
        name="tables",
    )
    cone = jnp.broadcast_to(cone_weight.reshape(-1, 1), (views * crossed, LANES))

    def one(index, direction, given, base=None):
        return call(
            functools.partial(part_kernel, index, direction, base is not None),
            whole,
            *tables,
            given,
            *(() if base is None else (base,)),
            name="part",
        )

    def two(first, second, direction, given, base, other):
        return call(
            functools.partial(two_kernel, first, second, direction),
            whole,
            *tables,
            given,
            base,
            other,
            scratch=scratch,
            name="two_parts",
        )

    def pair_group(steps, direction, state, first, second, third, base=None):
        near, far, joined = steps
        near_sum = one(near[0], direction, state)
        near_sum = one(near[1], direction, first, near_sum)
        far_sum = one(far[0], direction, second)
        joined_sum = one(joined[0], direction, near_sum, base)
        return two(far[1], joined[1], direction, third, far_sum, joined_sum)

    state = leaf_coeffs
    for levels in groups:
        steps = forward_entries[levels]
        near = 1 << levels[0]
        if len(levels) == 2:
            far = 1 << levels[1]
            received = [across_view(state, apart) for apart in (near, far, near + far)]
            state = pair_group(steps, 1, state, *received)
            begun = state
        else:
            received = across_view(state, near)
            begun = one(steps[0][0], 1, state)
            if levels != groups[-1]:
                state = one(steps[0][1], 1, received, begun)
            else:
                state, to_pair, to_across = call(
                    functools.partial(edges_kernel, steps[0][1]),
                    [whole, part, part],
                    *tables,
                    received,
                    begun,
                    name="edges",
                )

    odd = lax.axis_index("slab") % 2 == 1
    both = jnp.stack([measured, ray_weight])
    both = after(both, begun)
    low, high = both[:, :, :reach], both[:, :, planes - reach :]
    paired = with_pair(jnp.where(odd, low, high))
    crossing = across_pairs(jnp.where(odd, high, low))
    both = jnp.concatenate(
        [jnp.where(odd, paired, crossing), both, jnp.where(odd, crossing, paired)], axis=2
    )

    from_across = across_pairs(to_across)
    from_pair = with_pair(to_pair)
    residual, cotangent = call(
        tilt_kernel,
        [whole, whole],
        cone,
        state,
        from_pair,
        from_across,
        both[0],
        both[1],
        scratch=[
            pltpu.VMEM((views, planes + 4 * reach, columns), jnp.float32),
            pltpu.VMEM((views, planes + 2 * reach, columns), jnp.float32),
        ],
        name="tilt",
    )

    state = cotangent
    for levels in reversed(groups):
        steps = back_entries[levels]
        near = 1 << levels[0]
        base = leaf_coeffs if levels == groups[0] else None
        if len(levels) == 2:
            far = 1 << levels[1]
            received = [across_view(state, apart) for apart in (far, near, near + far)]
            state = pair_group(steps, -1, state, *received, base)
        else:
            received = across_view(state, near)
            begun = one(steps[0][0], -1, state, base)
            state = one(steps[0][1], -1, received, begun)
    return (residual, state)


def solution(mesh):
    in_specs = (
        P("view", "slab", None),
        P("view", "slab", None),
        P("view", "slab", None),
        P("view", None),
        P(),
        P(),
        P(),
    )
    out_specs = (P("view", "slab", None), P("view", "slab", None))
    return jax.shard_map(body, mesh=mesh, in_specs=in_specs, out_specs=out_specs, check_vma=False)
```

time: 57 us -> 41.8 us (0.73)
  the two profiles are of different devices: /device:TPU:1 before, /device:TPU:20 now
where the time goes in v3:
time: 41.8 us; the launch traced here: 41.5 us
  waiting for transfers between devices  18.5 us (44%)
  starting transfers between devices  13.6 us (33%)
  Pallas kernels  5.89 us (14%)
  local copies, waits for them, and re-layouts  2.51 us (6%)
  between operations  0.87 us (2%)
    ppermute x8, waiting for transfers between devices, across_view(): lax.ppermute(x, 'view', [(i, i ^ apart) for i in range(lax.axis_size('vie...  12.6 us
    ppermute x8, starting transfers between devices, across_view(): lax.ppermute(x, 'view', [(i, i ^ apart) for i in range(lax.axis_size('vie...  9.05 us
    ppermute x2, waiting for transfers between devices, across_pairs(): lax.ppermute(x, 'slab', [(i, i + 1) for i in lower] + [(i + 1, i) for i i...  5.91 us
    pallas_call x16, Pallas kernels, call(): pl.pallas_call(kernel, out_shape=out_shape, in_specs=[BLOCK] * len(args)...  5.89 us
    ppermute x2, starting transfers between devices, across_pairs(): lax.ppermute(x, 'slab', [(i, i + 1) for i in lower] + [(i + 1, i) for i i...  4.42 us
    unnamed x16, local copies, waits for them, and re-layouts  2.34 us
  transfers between devices with their start and end apart: 12, of which 8 were waited for; matrix products, arithmetic and copies ran while one was open for 0% of the time, Pallas kernels for 7%

profile of v3, /device:TPU:20, one launch (start us, length us, event | category | flops | bytes accessed | tf_op | source)
XLA Modules:
  0.0 41.5 jit_solution(7387713693079299888)
XLA Ops:
  0.6 1.6 %collective-permute-start.2 = (f32[2,16,768]{2,1,0:T(8,128)}, f32[2,16,768]{2,1,0:T(8,128)S(1)}, u32[]{:S(2)}, u32[]{:S(2)}) collective-permute-start(f32[2,16,768]{2,1,0:T(8,128)} %refs_0_.1), channel_id=1, source_target_pairs={{0,4},{4,0},{8,12},{12,8},{16,20},{20,16},{24,28},{28,24},{1,5},{5... | collective-permute-start | bytes 294920 | tf_op jit(solution)/shard_map/ppermute | solution.py:136
  2.2 1.6 %collective-permute-start.1 = (f32[2,16,768]{2,1,0:T(8,128)}, f32[2,16,768]{2,1,0:T(8,128)S(1)}, u32[]{:S(2)}, u32[]{:S(2)}) collective-permute-start(f32[2,16,768]{2,1,0:T(8,128)} %refs_0_.1), channel_id=1, source_target_pairs={{0,8},{4,12},{8,0},{12,4},{16,24},{20,28},{24,16},{28,20},{1,9},{5... | collective-permute-start | bytes 294920 | tf_op jit(solution)/shard_map/ppermute | solution.py:136
  3.8 0.4 %collective-permute-start = (f32[2,16,768]{2,1,0:T(8,128)}, f32[2,16,768]{2,1,0:T(8,128)S(1)}, u32[]{:S(2)}, u32[]{:S(2)}) collective-permute-start(f32[2,16,768]{2,1,0:T(8,128)} %refs_0_.1), channel_id=1, source_target_pairs={{0,12},{4,8},{8,4},{12,0},{16,28},{20,24},{24,20},{28,16},{1,13},{... | collective-permute-start | bytes 294920 | tf_op jit(solution)/shard_map/ppermute | solution.py:136
  4.2 0.7 %copy-done.2 = f32[3,2,16,4]{2,3,1,0:T(4,128)S(1)} copy-done((f32[3,2,16,4]{2,3,1,0:T(4,128)S(1)}, f32[3,2,16,4]{2,3,1,0:T(4,128)}, u32[]{:S(2)}) %copy-start.2) | copy-done | bytes 1560
  4.9 1.0 %tables.1 = (s32[64,128]{1,0:T(8,128)S(1)}, f32[128,128]{1,0:T(8,128)S(1)}) custom-call(f32[3,2,4,16]{3,2,1,0:T(4,128)S(1)} %bitcast.11, s32[3,2,16]{2,1,0:T(2,128)S(1)} %copy-done.3, s32[3,2,16]{2,1,0:T(2,128)S(1)} %copy-done.4), custom_call_target="tpu_custom_call" | custom-call | tf_op jit(solution)/shard_map/tables/pallas_call | solution.py:124
  5.9 0.9 %copy-done = f32[2,16,768]{2,1,0:T(8,128)S(1)} copy-done((f32[2,16,768]{2,1,0:T(8,128)S(1)}, f32[2,16,768]{2,1,0:T(8,128)}, u32[]{:S(2)}) %copy-start) | copy-done | bytes 98328
  7.0 0.7 %copy-done.5 = f32[2,16,768]{2,1,0:T(8,128)S(1)} copy-done((f32[2,16,768]{2,1,0:T(8,128)S(1)}, f32[2,16,768]{2,1,0:T(8,128)}, u32[]{:S(2)}) %copy-start.5) | copy-done | bytes 98328
  8.4 1.0 %collective-permute-done.given = f32[2,16,768]{2,1,0:T(8,128)S(1)} collective-permute-done((f32[2,16,768]{2,1,0:T(8,128)}, f32[2,16,768]{2,1,0:T(8,128)S(1)}, u32[]{:S(2)}, u32[]{:S(2)}) %collective-permute-start) | collective-permute-done | bytes 98336 | tf_op jit(solution)/shard_map/ppermute | solution.py:136
  9.5 0.4 two_parts.2.given
  10.2 2.5 %collective-permute-start.7 = (f32[2,2,4,768]{3,2,1,0:T(4,128)S(1)}, f32[2,2,4,768]{3,2,1,0:T(4,128)S(1)}, u32[]{:S(2)}, u32[]{:S(2)}) collective-permute-start(f32[2,2,4,768]{3,2,1,0:T(4,128)S(1)} %get-tuple-element.21), channel_id=1, source_target_pairs={{1,2},{2,1},{5,6},{6,5},{9,10},{10,9},{13,14},{14,13},{17,18},{18,... | collective-permute-start | bytes 147464 | tf_op jit(solution)/shard_map/ppermute | solution.py:145
  13.2 2.5 %collective-permute-done.7 = f32[2,2,4,768]{3,2,1,0:T(4,128)S(1)} collective-permute-done((f32[2,2,4,768]{3,2,1,0:T(4,128)S(1)}, f32[2,2,4,768]{3,2,1,0:T(4,128)S(1)}, u32[]{:S(2)}, u32[]{:S(2)}) %collective-permute-start.7) | collective-permute-done | bytes 49184 | tf_op jit(solution)/shard_map/ppermute | solution.py:145
  15.7 2.7 %collective-permute-done.3.given = f32[2,16,768]{2,1,0:T(8,128)S(1)} collective-permute-done((f32[2,16,768]{2,1,0:T(8,128)S(1)}, f32[2,16,768]{2,1,0:T(8,128)S(1)}, u32[]{:S(2)}, u32[]{:S(2)}) %collective-permute-start.3) | collective-permute-done | bytes 98336 | tf_op jit(solution)/shard_map/ppermute | solution.py:136
  18.7 1.9 %collective-permute-start.5 = (f32[2,8,768]{2,1,0:T(8,128)S(1)}, f32[2,8,768]{2,1,0:T(8,128)S(1)}, u32[]{:S(2)}, u32[]{:S(2)}) collective-permute-start(f32[2,8,768]{2,1,0:T(8,128)S(1)} %get-tuple-element.14), channel_id=1, source_target_pairs={{1,2},{2,1},{5,6},{6,5},{9,10},{10,9},{13,14},{14,13},{17,18},{18,... | collective-permute-start | bytes 147464 | tf_op jit(solution)/shard_map/ppermute | solution.py:145
  20.7 3.4 %collective-permute-done.5.across = f32[2,8,768]{2,1,0:T(8,128)S(1)} collective-permute-done((f32[2,8,768]{2,1,0:T(8,128)S(1)}, f32[2,8,768]{2,1,0:T(8,128)S(1)}, u32[]{:S(2)}, u32[]{:S(2)}) %collective-permute-start.5) | collective-permute-done | bytes 49184 | tf_op jit(solution)/shard_map/ppermute | solution.py:145
  24.2 1.0 %tilt.1 = (f32[2,16,768]{2,1,0:T(8,128)}, f32[2,16,768]{2,1,0:T(8,128)S(1)}) custom-call(f32[18,128]{1,0:T(8,128)S(1)} %broadcast_in_dim.8.cone, f32[2,16,768]{2,1,0:T(8,128)S(1)} %get-tuple-element.12.split, f32[2,8,768]{2,1,0:T(8,128)S(1)} %collective-permute-done.4.pair, f32[2,8,768]{2,1,0:T(8,128)S(1)} %collective-permute-done.5.across, ...), custom_call_target="tpu_custom_call" | custom-call | tf_op jit(solution)/shard_map/tilt/pallas_call | solution.py:124
  25.2 1.3 %collective-permute-start.8 = (f32[2,16,768]{2,1,0:T(8,128)S(1)}, f32[2,16,768]{2,1,0:T(8,128)S(1)}, u32[]{:S(2)}, u32[]{:S(2)}) collective-permute-start(f32[2,16,768]{2,1,0:T(8,128)S(1)} %get-tuple-element.17.given), channel_id=1, source_target_pairs={{0,16},{4,20},{8,24},{12,28},{16,0},{20,4},{24,8},{28,12},{1,17},{... | collective-permute-start | bytes 294920 | tf_op jit(solution)/shard_map/ppermute | solution.py:136
  26.7 4.5 %collective-permute-done.8.given = f32[2,16,768]{2,1,0:T(8,128)S(1)} collective-permute-done((f32[2,16,768]{2,1,0:T(8,128)S(1)}, f32[2,16,768]{2,1,0:T(8,128)S(1)}, u32[]{:S(2)}, u32[]{:S(2)}) %collective-permute-start.8) | collective-permute-done | bytes 98336 | tf_op jit(solution)/shard_map/ppermute | solution.py:136
  31.4 2.3 %collective-permute-start.11 = (f32[2,16,768]{2,1,0:T(8,128)S(1)}, f32[2,16,768]{2,1,0:T(8,128)S(1)}, u32[]{:S(2)}, u32[]{:S(2)}) collective-permute-start(f32[2,16,768]{2,1,0:T(8,128)S(1)} %part.17.given), channel_id=1, source_target_pairs={{0,8},{4,12},{8,0},{12,4},{16,24},{20,28},{24,16},{28,20},{1,9},{5... | collective-permute-start | bytes 294920 | tf_op jit(solution)/shard_map/ppermute | solution.py:136
  33.8 1.2 %collective-permute-start.10 = (f32[2,16,768]{2,1,0:T(8,128)S(1)}, f32[2,16,768]{2,1,0:T(8,128)S(1)}, u32[]{:S(2)}, u32[]{:S(2)}) collective-permute-start(f32[2,16,768]{2,1,0:T(8,128)S(1)} %part.17.given), channel_id=1, source_target_pairs={{0,4},{4,0},{8,12},{12,8},{16,20},{20,16},{24,28},{28,24},{1,5},{5... | collective-permute-start | bytes 294920 | tf_op jit(solution)/shard_map/ppermute | solution.py:136
  35.0 0.4 collective-permute-start.9
  35.5 0.8 %collective-permute-done.11.given = f32[2,16,768]{2,1,0:T(8,128)S(1)} collective-permute-done((f32[2,16,768]{2,1,0:T(8,128)S(1)}, f32[2,16,768]{2,1,0:T(8,128)S(1)}, u32[]{:S(2)}, u32[]{:S(2)}) %collective-permute-start.11) | collective-permute-done | bytes 98336 | tf_op jit(solution)/shard_map/ppermute | solution.py:136
  36.8 1.6 %collective-permute-done.10.given = f32[2,16,768]{2,1,0:T(8,128)S(1)} collective-permute-done((f32[2,16,768]{2,1,0:T(8,128)S(1)}, f32[2,16,768]{2,1,0:T(8,128)S(1)}, u32[]{:S(2)}, u32[]{:S(2)}) %collective-permute-start.10) | collective-permute-done | bytes 98336 | tf_op jit(solution)/shard_map/ppermute | solution.py:136
  38.6 1.9 %collective-permute-done.9.given = f32[2,16,768]{2,1,0:T(8,128)S(1)} collective-permute-done((f32[2,16,768]{2,1,0:T(8,128)S(1)}, f32[2,16,768]{2,1,0:T(8,128)S(1)}, u32[]{:S(2)}, u32[]{:S(2)}) %collective-permute-start.9) | collective-permute-done | bytes 98336 | tf_op jit(solution)/shard_map/ppermute | solution.py:136
  40.5 1.0 %two_parts.3 = f32[2,16,768]{2,1,0:T(8,128)} custom-call(s32[64,128]{1,0:T(8,128)S(1)} %get-tuple-element.10.whole_numbers, f32[128,128]{1,0:T(8,128)S(1)} %get-tuple-element.11.weights, f32[2,16,768]{2,1,0:T(8,128)S(1)} %collective-permute-done.9.given, f32[2,16,768]{2,1,0:T(8,128)S(1)} %part.18.base, f32[2,16,768]{2,1,0:T(8,128)S(1)} %part.21.other), custom_call_target="tpu_custom_call" | custom-call | tf_op jit(solution)/shard_map/two_parts/pallas_call | solution.py:124
  (39 shorter events, 3.3 us)
Async XLA Ops:
  0.6 7.2 %collective-permute-start.2 = (f32[2,16,768]{2,1,0:T(8,128)}, f32[2,16,768]{2,1,0:T(8,128)S(1)}, u32[]{:S(2)}, u32[]{:S(2)}) collective-permute-start(f32[2,16,768]{2,1,0:T(8,128)} %refs_0_.1), channel_id=1, source_target_pairs={{0,4},{4,0},{8,12},{12,8},{16,20},{20,16},{24,28},{28,24},{1,5},{5... | collective-permute-start | bytes 294920 | tf_op jit(solution)/shard_map/ppermute | solution.py:136
  2.2 6.0 %collective-permute-start.1 = (f32[2,16,768]{2,1,0:T(8,128)}, f32[2,16,768]{2,1,0:T(8,128)S(1)}, u32[]{:S(2)}, u32[]{:S(2)}) collective-permute-start(f32[2,16,768]{2,1,0:T(8,128)} %refs_0_.1), channel_id=1, source_target_pairs={{0,8},{4,12},{8,0},{12,4},{16,24},{20,28},{24,16},{28,20},{1,9},{5... | collective-permute-start | bytes 294920 | tf_op jit(solution)/shard_map/ppermute | solution.py:136
  3.8 5.7 %collective-permute-start = (f32[2,16,768]{2,1,0:T(8,128)}, f32[2,16,768]{2,1,0:T(8,128)S(1)}, u32[]{:S(2)}, u32[]{:S(2)}) collective-permute-start(f32[2,16,768]{2,1,0:T(8,128)} %refs_0_.1), channel_id=1, source_target_pairs={{0,12},{4,8},{8,4},{12,0},{16,28},{20,24},{24,20},{28,16},{1,13},{... | collective-permute-start | bytes 294920 | tf_op jit(solution)/shard_map/ppermute | solution.py:136
  4.2 0.7 %copy-start.2 = (f32[3,2,16,4]{2,3,1,0:T(4,128)S(1)}, f32[3,2,16,4]{2,3,1,0:T(4,128)}, u32[]{:S(2)}) copy-start(f32[3,2,16,4]{2,3,1,0:T(4,128)} %param.11) | copy-start | bytes 4612
  4.2 0.7 %copy-start.4 = (s32[3,2,16]{2,1,0:T(2,128)S(1)}, s32[3,2,16]{2,1,0:T(2,128)}, u32[]{:S(2)}) copy-start(s32[3,2,16]{2,1,0:T(2,128)} %source.1) | copy-start | bytes 1156
  4.2 0.7 %copy-start.3 = (s32[3,2,16]{2,1,0:T(2,128)S(1)}, s32[3,2,16]{2,1,0:T(2,128)}, u32[]{:S(2)}) copy-start(s32[3,2,16]{2,1,0:T(2,128)} %offset.1) | copy-start | bytes 1156
  5.9 0.9 %copy-start = (f32[2,16,768]{2,1,0:T(8,128)S(1)}, f32[2,16,768]{2,1,0:T(8,128)}, u32[]{:S(2)}) copy-start(f32[2,16,768]{2,1,0:T(8,128)} %refs_0_.1) | copy-start | bytes 294916
  6.8 0.9 %copy-start.5 = (f32[2,16,768]{2,1,0:T(8,128)S(1)}, f32[2,16,768]{2,1,0:T(8,128)}, u32[]{:S(2)}) copy-start(f32[2,16,768]{2,1,0:T(8,128)} %param.9) | copy-start | bytes 294916
  6.8 0.9 %copy-start.6 = (f32[2,16,768]{2,1,0:T(8,128)S(1)}, f32[2,16,768]{2,1,0:T(8,128)}, u32[]{:S(2)}) copy-start(f32[2,16,768]{2,1,0:T(8,128)} %param.8) | copy-start | bytes 294916
  10.1 2.6 %copy-start.7 = (f32[2,9]{1,0:T(2,128)S(1)}, f32[2,9]{1,0:T(2,128)}, u32[]{:S(2)}) copy-start(f32[2,9]{1,0:T(2,128)} %param.10) | copy-start | bytes 220
  10.1 3.0 %collective-permute-start.6 = (f32[2,2,4,768]{3,2,1,0:T(4,128)S(1)}, f32[2,2,4,768]{3,2,1,0:T(4,128)S(1)}, u32[]{:S(2)}, u32[]{:S(2)}) collective-permute-start(f32[2,2,4,768]{3,2,1,0:T(4,128)S(1)} %get-tuple-element.20), channel_id=1, source_target_pairs={{0,1},{1,0},{2,3},{3,2},{4,5},{5,4},{6,7},{7,6},{8,9},{9,8},{10,11... | collective-permute-start | bytes 147464 | tf_op jit(solution)/shard_map/ppermute | solution.py:140
  10.2 5.4 %collective-permute-start.7 = (f32[2,2,4,768]{3,2,1,0:T(4,128)S(1)}, f32[2,2,4,768]{3,2,1,0:T(4,128)S(1)}, u32[]{:S(2)}, u32[]{:S(2)}) collective-permute-start(f32[2,2,4,768]{3,2,1,0:T(4,128)S(1)} %get-tuple-element.21), channel_id=1, source_target_pairs={{1,2},{2,1},{5,6},{6,5},{9,10},{10,9},{13,14},{14,13},{17,18},{18,... | collective-permute-start | bytes 147464 | tf_op jit(solution)/shard_map/ppermute | solution.py:145
  12.8 5.6 %collective-permute-start.3 = (f32[2,16,768]{2,1,0:T(8,128)S(1)}, f32[2,16,768]{2,1,0:T(8,128)S(1)}, u32[]{:S(2)}, u32[]{:S(2)}) collective-permute-start(f32[2,16,768]{2,1,0:T(8,128)S(1)} %two_parts.2.given), channel_id=1, source_target_pairs={{0,16},{4,20},{8,24},{12,28},{16,0},{20,4},{24,8},{28,12},{1,17},{... | collective-permute-start | bytes 294920 | tf_op jit(solution)/shard_map/ppermute | solution.py:136
  18.7 2.0 %collective-permute-start.4 = (f32[2,8,768]{2,1,0:T(8,128)S(1)}, f32[2,8,768]{2,1,0:T(8,128)S(1)}, u32[]{:S(2)}, u32[]{:S(2)}) collective-permute-start(f32[2,8,768]{2,1,0:T(8,128)S(1)} %get-tuple-element.13), channel_id=1, source_target_pairs={{0,1},{1,0},{2,3},{3,2},{4,5},{5,4},{6,7},{7,6},{8,9},{9,8},{10,11... | collective-permute-start | bytes 147464 | tf_op jit(solution)/shard_map/ppermute | solution.py:140
  18.7 5.4 %collective-permute-start.5 = (f32[2,8,768]{2,1,0:T(8,128)S(1)}, f32[2,8,768]{2,1,0:T(8,128)S(1)}, u32[]{:S(2)}, u32[]{:S(2)}) collective-permute-start(f32[2,8,768]{2,1,0:T(8,128)S(1)} %get-tuple-element.14), channel_id=1, source_target_pairs={{1,2},{2,1},{5,6},{6,5},{9,10},{10,9},{13,14},{14,13},{17,18},{18,... | collective-permute-start | bytes 147464 | tf_op jit(solution)/shard_map/ppermute | solution.py:145
  25.2 6.0 %collective-permute-start.8 = (f32[2,16,768]{2,1,0:T(8,128)S(1)}, f32[2,16,768]{2,1,0:T(8,128)S(1)}, u32[]{:S(2)}, u32[]{:S(2)}) collective-permute-start(f32[2,16,768]{2,1,0:T(8,128)S(1)} %get-tuple-element.17.given), channel_id=1, source_target_pairs={{0,16},{4,20},{8,24},{12,28},{16,0},{20,4},{24,8},{28,12},{1,17},{... | collective-permute-start | bytes 294920 | tf_op jit(solution)/shard_map/ppermute | solution.py:136
  31.4 4.9 %collective-permute-start.11 = (f32[2,16,768]{2,1,0:T(8,128)S(1)}, f32[2,16,768]{2,1,0:T(8,128)S(1)}, u32[]{:S(2)}, u32[]{:S(2)}) collective-permute-start(f32[2,16,768]{2,1,0:T(8,128)S(1)} %part.17.given), channel_id=1, source_target_pairs={{0,8},{4,12},{8,0},{12,4},{16,24},{20,28},{24,16},{28,20},{1,9},{5... | collective-permute-start | bytes 294920 | tf_op jit(solution)/shard_map/ppermute | solution.py:136
  33.8 4.6 %collective-permute-start.10 = (f32[2,16,768]{2,1,0:T(8,128)S(1)}, f32[2,16,768]{2,1,0:T(8,128)S(1)}, u32[]{:S(2)}, u32[]{:S(2)}) collective-permute-start(f32[2,16,768]{2,1,0:T(8,128)S(1)} %part.17.given), channel_id=1, source_target_pairs={{0,4},{4,0},{8,12},{12,8},{16,20},{20,16},{24,28},{28,24},{1,5},{5... | collective-permute-start | bytes 294920 | tf_op jit(solution)/shard_map/ppermute | solution.py:136
  35.0 5.5 %collective-permute-start.9 = (f32[2,16,768]{2,1,0:T(8,128)S(1)}, f32[2,16,768]{2,1,0:T(8,128)S(1)}, u32[]{:S(2)}, u32[]{:S(2)}) collective-permute-start(f32[2,16,768]{2,1,0:T(8,128)S(1)} %part.17.given), channel_id=1, source_target_pairs={{0,12},{4,8},{8,4},{12,0},{16,28},{20,24},{24,20},{28,16},{1,13},{... | collective-permute-start | bytes 294920 | tf_op jit(solution)/shard_map/ppermute | solution.py:136
  35.5 1.1 %copy-start.1 = (f32[2,16,768]{2,1,0:T(8,128)S(1)}, f32[2,16,768]{2,1,0:T(8,128)}, u32[]{:S(2)}) copy-start(f32[2,16,768]{2,1,0:T(8,128)} %refs_0_.1) | copy-start | bytes 294916

commit v4 on v3

--- a/solution.py
+++ b/solution.py
@@ -31,7 +31,7 @@
     return total
 
 
-def table_kernel(entries, views, weight, offset, source, whole_numbers, weights):
+def table_kernel(entries, views, weight, offset, source, cone, whole_numbers, weights, crossing):
     me = lax.axis_index("view")
     taps = weight.shape[2]
     for index, (level, channel, apart, direction) in enumerate(entries):
@@ -43,6 +43,10 @@
             whole_numbers[2 * at + 1, :] = jnp.full((LANES,), source[level, channel, row], jnp.int32)
             for k in range(taps):
                 weights[at * taps + k, :] = jnp.full((LANES,), weight[level, channel, k, row])
+    crossed = cone.shape[1]
+    for v in range(views):
+        for e in range(crossed):
+            crossing[v * crossed + e, :] = jnp.full((LANES,), cone[v, e])
 
 
 def level_part(index, direction, whole_numbers, weights, given, base, out):
@@ -80,40 +84,59 @@
     level_part(second, direction, whole_numbers, weights, between, other, out)
 
 
-def edges_kernel(index, whole_numbers, weights, given, base, out, pair, across):
+def edges_kernel(
+    reach, index, whole_numbers, weights, given, base, measured, ray, out, pair, across
+):
     level_part(index, 1, whole_numbers, weights, given, base, out)
-    width = pair.shape[1]
-    planes = out.shape[1]
+    views, planes, columns = out.shape
+    width = 2 * reach
     odd = lax.axis_index("slab") % 2
-    pair[...] = out[:, pl.ds(pl.multiple_of((1 - odd) * (planes - width), 8), width), :]
-    across[...] = out[:, pl.ds(pl.multiple_of(odd * (planes - width), 8), width), :]
-
-
-def tilt_kernel(cone, split, pair, across, measured, ray, residual, cotangent, wide, weighted):
+    row = lax.broadcasted_iota(jnp.int32, (views, width, columns), 1)
+    for message, top in ((pair, 1 - odd), (across, odd)):
+        edge = pl.ds(pl.multiple_of(top * (planes - width), width), width)
+        message[:, :width] = out[:, edge, :]
+        own = (row >= reach) == (top == 1)
+        message[:, width:] = jnp.where(own, measured[:, edge], pltpu.roll(ray[:, edge], reach, 1))
+
+
+def tilt_kernel(
+    cone, split, pair, across, measured, ray, residual, cotangent, wide, seen, lengths, weighted
+):
     views, planes, columns = split.shape
-    width = pair.shape[1]
+    width = pair.shape[1] // 2
+    reach = width // 2
     crossed = cone.shape[0] // views
-    reach = crossed // 2
     odd = lax.axis_index("slab") % 2
     far = planes + width
-    wide[:, pl.ds(width, planes), :] = split[...]
-    wide[:, pl.ds(pl.multiple_of((1 - odd) * far, 8), width), :] = pair[...]
-    wide[:, pl.ds(pl.multiple_of(odd * far, 8), width), :] = across[...]
     extended = planes + 2 * reach
+    own = pl.ds(width, planes)
     for v in range(views):
         factors = [cone[pl.ds(v * crossed + e, 1), :] for e in range(crossed)]
         for j in range(columns // LANES):
             at = pl.ds(LANES * j, LANES)
-            total = factors[0] * wide[v, pl.ds(width - 2 * reach, extended), at]
+            wide[v, j, own] = split[v, :, at]
+            seen[v, j, own] = measured[v, :, at]
+            lengths[v, j, own] = ray[v, :, at]
+            for message, side in ((pair, 1 - odd), (across, odd)):
+                edge = pl.ds(pl.multiple_of(side * far, width), width)
+                mixed = message[v, width:, at]
+                wide[v, j, edge] = message[v, :width, at]
+                seen[v, j, edge] = mixed
+                lengths[v, j, edge] = pltpu.roll(mixed, reach, 0)
+            total = factors[0] * wide[v, j, pl.ds(0, extended)]
             for e in range(1, crossed):
-                total = total + factors[e] * wide[v, pl.ds(width - 2 * reach + e, extended), at]
-            left = measured[v, :, at] - total
+                total = total + factors[e] * wide[v, j, pl.ds(e, extended)]
+            left = seen[v, j, pl.ds(reach, extended)] - total
+            weighted[v, j] = lengths[v, j, pl.ds(reach, extended)] * left
             residual[v, :, at] = left[reach : reach + planes]
-            weighted[v, :, at] = ray[v, :, at] * left
-            total = factors[0] * weighted[v, pl.ds(2 * reach, planes), at]
+            total = factors[0] * weighted[v, j, pl.ds(2 * reach, planes)]
             for e in range(1, crossed):
-                total = total + factors[e] * weighted[v, pl.ds(2 * reach - e, planes), at]
+                total = total + factors[e] * weighted[v, j, pl.ds(2 * reach - e, planes)]
             cotangent[v, :, at] = total
+
+
+def copy_kernel(given, out):
+    out[...] = given[...]
 
 
 def shaped(*shape, dtype=jnp.float32):
@@ -145,10 +168,6 @@
     return lax.ppermute(x, "slab", [(i, i + 1) for i in lower] + [(i + 1, i) for i in lower])
 
 
-def after(x, *earlier):
-    return lax.optimization_barrier((x, *earlier))[0]
-
-
 def body(leaf_coeffs, measured, ray_weight, cone_weight, interp_weight, shift_offset, source_view):
     views, planes, columns = leaf_coeffs.shape
     crossed = cone_weight.shape[1]
@@ -157,7 +176,8 @@
     level_count = lax.axis_size("view").bit_length() - 1
     groups = [tuple(range(i, min(i + 2, level_count))) for i in range(0, level_count, 2)]
     whole = shaped(views, planes, columns)
-    part = shaped(views, 2 * reach, columns)
+    message = shaped(views, 4 * reach, columns)
+    assert 2 * reach == 8 and planes % 8 == 0 and columns % LANES == 0
     scratch = [pltpu.VMEM((views, planes, columns), jnp.float32)]
 
     entries = []
@@ -187,14 +207,16 @@
         [
             shaped(len(entries) * views * 2, LANES, dtype=jnp.int32),
             shaped(len(entries) * views * taps, LANES),
+            shaped(views * crossed, LANES),
         ],
         jnp.swapaxes(interp_weight, 2, 3),
         shift_offset,
         source_view,
-        specs=[SCALARS] * 3,
+        cone_weight,
+        specs=[SCALARS] * 4,
         name="tables",
     )
-    cone = jnp.broadcast_to(cone_weight.reshape(-1, 1), (views * crossed, LANES))
+    *tables, cone = tables
 
     def one(index, direction, given, base=None):
         return call(
@@ -234,7 +256,6 @@
             far = 1 << levels[1]
             received = [across_view(state, apart) for apart in (near, far, near + far)]
             state = pair_group(steps, 1, state, *received)
-            begun = state
         else:
             received = across_view(state, near)
             begun = one(steps[0][0], 1, state)
@@ -242,23 +263,15 @@
                 state = one(steps[0][1], 1, received, begun)
             else:
                 state, to_pair, to_across = call(
-                    functools.partial(edges_kernel, steps[0][1]),
-                    [whole, part, part],
+                    functools.partial(edges_kernel, reach, steps[0][1]),
+                    [whole, message, message],
                     *tables,
                     received,
                     begun,
+                    measured,
+                    ray_weight,
                     name="edges",
                 )
-
-    odd = lax.axis_index("slab") % 2 == 1
-    both = jnp.stack([measured, ray_weight])
-    both = after(both, begun)
-    low, high = both[:, :, :reach], both[:, :, planes - reach :]
-    paired = with_pair(jnp.where(odd, low, high))
-    crossing = across_pairs(jnp.where(odd, high, low))
-    both = jnp.concatenate(
-        [jnp.where(odd, paired, crossing), both, jnp.where(odd, crossing, paired)], axis=2
-    )
 
     from_across = across_pairs(to_across)
     from_pair = with_pair(to_pair)
@@ -269,14 +282,16 @@
         state,
         from_pair,
         from_across,
-        both[0],
-        both[1],
+        measured,
+        ray_weight,
         scratch=[
-            pltpu.VMEM((views, planes + 4 * reach, columns), jnp.float32),
-            pltpu.VMEM((views, planes + 2 * reach, columns), jnp.float32),
+            pltpu.VMEM((views, columns // LANES, planes + beyond * reach, LANES), jnp.float32)
+            for beyond in (4, 4, 4, 2)
         ],
         name="tilt",
     )
+
+    residual = call(copy_kernel, whole, residual, name="residual")
 
     state = cotangent
     for levels in reversed(groups):

time: 41.8 us -> 38.8 us (0.928)
  waiting for transfers between devices: 18.5 us -> 16.3 us
  starting transfers between devices: 13.6 us -> 12.1 us
  local copies, waits for them, and re-layouts: 2.51 us -> 3.47 us
    ppermute x2 -> x1, waiting for transfers between devices: 5.91 us -> 3.41 us  [across_pairs(): lax.ppermute(x, 'slab', [(i, i + 1) for i in lower] + [(i + 1, i) for i i...]
    ppermute x2 -> x1, starting transfers between devices: 4.42 us -> 2.5 us  [across_pairs(): lax.ppermute(x, 'slab', [(i, i + 1) for i in lower] + [(i + 1, i) for i i...]
    unnamed x16, local copies, waits for them, and re-layouts: 2.34 us -> 3.47 us
    ppermute x8, starting transfers between devices: 9.05 us -> 9.49 us  [across_view(): lax.ppermute(x, 'view', [(i, i ^ apart) for i in range(lax.axis_size('vie...]
    pallas_call x16 -> x17, Pallas kernels: 5.89 us -> 5.83 us  [call(): pl.pallas_call(kernel, out_shape=out_shape, in_specs=[BLOCK] * len(args)...]
  transfers between devices with their start and end apart: 12 -> 10, of which waited for: 8 -> 7; matrix products, arithmetic and copies ran while one was open for 0% -> 0% of each run, Pallas kernels for 7% -> 10%
where the time goes in v4:
time: 38.8 us; the launch traced here: 38.5 us
  waiting for transfers between devices  16.3 us (42%)
  starting transfers between devices  12.1 us (31%)
  Pallas kernels  5.83 us (15%)
  local copies, waits for them, and re-layouts  3.47 us (9%)
  between operations  0.83 us (2%)
    ppermute x8, waiting for transfers between devices, across_view(): lax.ppermute(x, 'view', [(i, i ^ apart) for i in range(lax.axis_size('vie...  12.9 us
    ppermute x8, starting transfers between devices, across_view(): lax.ppermute(x, 'view', [(i, i ^ apart) for i in range(lax.axis_size('vie...  9.49 us
    pallas_call x17, Pallas kernels, call(): pl.pallas_call(kernel, out_shape=out_shape, in_specs=[BLOCK] * len(args)...  5.83 us
    unnamed x16, local copies, waits for them, and re-layouts  3.47 us
    ppermute x1, waiting for transfers between devices, across_pairs(): lax.ppermute(x, 'slab', [(i, i + 1) for i in lower] + [(i + 1, i) for i i...  3.41 us
    ppermute x1, starting transfers between devices, across_pairs(): lax.ppermute(x, 'slab', [(i, i + 1) for i in lower] + [(i + 1, i) for i i...  2.5 us
  transfers between devices with their start and end apart: 10, of which 7 were waited for; matrix products, arithmetic and copies ran while one was open for 0% of the time, Pallas kernels for 10%

profile of v4, /device:TPU:20, one launch (start us, length us, event | category | flops | bytes accessed | tf_op | source)
XLA Modules:
  0.0 38.5 jit_solution(4548143831747691097)
XLA Ops:
  0.6 1.6 %collective-permute-start.2 = (f32[2,16,768]{2,1,0:T(8,128)}, f32[2,16,768]{2,1,0:T(8,128)S(1)}, u32[]{:S(2)}, u32[]{:S(2)}) collective-permute-start(f32[2,16,768]{2,1,0:T(8,128)} %refs_0_.1), channel_id=1, source_target_pairs={{0,4},{4,0},{8,12},{12,8},{16,20},{20,16},{24,28},{28,24},{1,5},{5... | collective-permute-start | bytes 294920 | tf_op jit(solution)/shard_map/ppermute | solution.py:159
  2.2 1.6 %collective-permute-start.1 = (f32[2,16,768]{2,1,0:T(8,128)}, f32[2,16,768]{2,1,0:T(8,128)S(1)}, u32[]{:S(2)}, u32[]{:S(2)}) collective-permute-start(f32[2,16,768]{2,1,0:T(8,128)} %refs_0_.1), channel_id=1, source_target_pairs={{0,8},{4,12},{8,0},{12,4},{16,24},{20,28},{24,16},{28,20},{1,9},{5... | collective-permute-start | bytes 294920 | tf_op jit(solution)/shard_map/ppermute | solution.py:159
  3.8 0.4 %collective-permute-start = (f32[2,16,768]{2,1,0:T(8,128)}, f32[2,16,768]{2,1,0:T(8,128)S(1)}, u32[]{:S(2)}, u32[]{:S(2)}) collective-permute-start(f32[2,16,768]{2,1,0:T(8,128)} %refs_0_.1), channel_id=1, source_target_pairs={{0,12},{4,8},{8,4},{12,0},{16,28},{20,24},{24,20},{28,16},{1,13},{... | collective-permute-start | bytes 294920 | tf_op jit(solution)/shard_map/ppermute | solution.py:159
  4.2 0.7 %copy-done.4 = f32[3,2,16,4]{2,3,1,0:T(4,128)S(1)} copy-done((f32[3,2,16,4]{2,3,1,0:T(4,128)S(1)}, f32[3,2,16,4]{2,3,1,0:T(4,128)}, u32[]{:S(2)}) %copy-start.4) | copy-done | bytes 1560
  4.9 0.7 %copy-done.5 = s32[3,2,16]{2,1,0:T(2,128)S(1)} copy-done((s32[3,2,16]{2,1,0:T(2,128)S(1)}, s32[3,2,16]{2,1,0:T(2,128)}, u32[]{:S(2)}) %copy-start.5) | copy-done | bytes 408
  5.6 0.7 %copy-done.6 = s32[3,2,16]{2,1,0:T(2,128)S(1)} copy-done((s32[3,2,16]{2,1,0:T(2,128)S(1)}, s32[3,2,16]{2,1,0:T(2,128)}, u32[]{:S(2)}) %copy-start.6) | copy-done | bytes 408
  6.3 1.0 %tables.1 = (s32[64,128]{1,0:T(8,128)S(1)}, f32[128,128]{1,0:T(8,128)S(1)}, f32[18,128]{1,0:T(8,128)S(1)}) custom-call(f32[3,2,4,16]{3,2,1,0:T(4,128)S(1)} %bitcast.1, s32[3,2,16]{2,1,0:T(2,128)S(1)} %copy-done.5, s32[3,2,16]{2,1,0:T(2,128)S(1)} %copy-done.6, f32[2,9]{1,0:T(2,128)S(1)} %copy-done.7), custom_call_target="tpu_custom_call" | custom-call | tf_op jit(solution)/shard_map/tables/pallas_call | solution.py:147
  7.3 0.9 %copy-done = f32[2,16,768]{2,1,0:T(8,128)S(1)} copy-done((f32[2,16,768]{2,1,0:T(8,128)S(1)}, f32[2,16,768]{2,1,0:T(8,128)}, u32[]{:S(2)}) %copy-start) | copy-done | bytes 98328
  9.1 0.4 %collective-permute-done.given = f32[2,16,768]{2,1,0:T(8,128)S(1)} collective-permute-done((f32[2,16,768]{2,1,0:T(8,128)}, f32[2,16,768]{2,1,0:T(8,128)S(1)}, u32[]{:S(2)}, u32[]{:S(2)}) %collective-permute-start) | collective-permute-done | bytes 98336 | tf_op jit(solution)/shard_map/ppermute | solution.py:159
  9.5 0.4 two_parts.2.given
  9.9 0.4 %collective-permute-start.3 = (f32[2,16,768]{2,1,0:T(8,128)S(1)}, f32[2,16,768]{2,1,0:T(8,128)S(1)}, u32[]{:S(2)}, u32[]{:S(2)}) collective-permute-start(f32[2,16,768]{2,1,0:T(8,128)S(1)} %two_parts.2.given), channel_id=1, source_target_pairs={{0,16},{4,20},{8,24},{12,28},{16,0},{20,4},{24,8},{28,12},{1,17},{... | collective-permute-start | bytes 294920 | tf_op jit(solution)/shard_map/ppermute | solution.py:159
  10.5 5.1 %collective-permute-done.3.given = f32[2,16,768]{2,1,0:T(8,128)S(1)} collective-permute-done((f32[2,16,768]{2,1,0:T(8,128)S(1)}, f32[2,16,768]{2,1,0:T(8,128)S(1)}, u32[]{:S(2)}, u32[]{:S(2)}) %collective-permute-start.3) | collective-permute-done | bytes 98336 | tf_op jit(solution)/shard_map/ppermute | solution.py:159
  15.9 2.5 %collective-permute-start.5 = (f32[2,16,768]{2,1,0:T(8,128)S(1)}, f32[2,16,768]{2,1,0:T(8,128)S(1)}, u32[]{:S(2)}, u32[]{:S(2)}) collective-permute-start(f32[2,16,768]{2,1,0:T(8,128)S(1)} %get-tuple-element.15), channel_id=1, source_target_pairs={{1,2},{2,1},{5,6},{6,5},{9,10},{10,9},{13,14},{14,13},{17,18},{18,... | collective-permute-start | bytes 294920 | tf_op jit(solution)/shard_map/ppermute | solution.py:168
  18.4 3.4 %collective-permute-done.5.across = f32[2,16,768]{2,1,0:T(8,128)S(1)} collective-permute-done((f32[2,16,768]{2,1,0:T(8,128)S(1)}, f32[2,16,768]{2,1,0:T(8,128)S(1)}, u32[]{:S(2)}, u32[]{:S(2)}) %collective-permute-start.5) | collective-permute-done | bytes 98336 | tf_op jit(solution)/shard_map/ppermute | solution.py:168
  21.8 0.3 tilt.1
  22.1 1.4 %collective-permute-start.6 = (f32[2,16,768]{2,1,0:T(8,128)S(1)}, f32[2,16,768]{2,1,0:T(8,128)S(1)}, u32[]{:S(2)}, u32[]{:S(2)}) collective-permute-start(f32[2,16,768]{2,1,0:T(8,128)S(1)} %get-tuple-element.17.given), channel_id=1, source_target_pairs={{0,16},{4,20},{8,24},{12,28},{16,0},{20,4},{24,8},{28,12},{1,17},{... | collective-permute-start | bytes 294920 | tf_op jit(solution)/shard_map/ppermute | solution.py:159
  23.7 4.1 %collective-permute-done.6.given = f32[2,16,768]{2,1,0:T(8,128)S(1)} collective-permute-done((f32[2,16,768]{2,1,0:T(8,128)S(1)}, f32[2,16,768]{2,1,0:T(8,128)S(1)}, u32[]{:S(2)}, u32[]{:S(2)}) %collective-permute-start.6) | collective-permute-done | bytes 98336 | tf_op jit(solution)/shard_map/ppermute | solution.py:159
  27.9 2.6 %collective-permute-start.9 = (f32[2,16,768]{2,1,0:T(8,128)S(1)}, f32[2,16,768]{2,1,0:T(8,128)S(1)}, u32[]{:S(2)}, u32[]{:S(2)}) collective-permute-start(f32[2,16,768]{2,1,0:T(8,128)S(1)} %part.17.given), channel_id=1, source_target_pairs={{0,8},{4,12},{8,0},{12,4},{16,24},{20,28},{24,16},{28,20},{1,9},{5... | collective-permute-start | bytes 294920 | tf_op jit(solution)/shard_map/ppermute | solution.py:159
  30.6 1.3 %collective-permute-start.8 = (f32[2,16,768]{2,1,0:T(8,128)S(1)}, f32[2,16,768]{2,1,0:T(8,128)S(1)}, u32[]{:S(2)}, u32[]{:S(2)}) collective-permute-start(f32[2,16,768]{2,1,0:T(8,128)S(1)} %part.17.given), channel_id=1, source_target_pairs={{0,4},{4,0},{8,12},{12,8},{16,20},{20,16},{24,28},{28,24},{1,5},{5... | collective-permute-start | bytes 294920 | tf_op jit(solution)/shard_map/ppermute | solution.py:159
  32.1 0.6 %residual.1 = f32[2,16,768]{2,1,0:T(8,128)} custom-call(f32[2,16,768]{2,1,0:T(8,128)S(1)} %get-tuple-element.16.given), custom_call_target="tpu_custom_call" | custom-call | tf_op jit(solution)/shard_map/residual/pallas_call | solution.py:147
  33.4 0.5 %copy-done.1 = f32[2,16,768]{2,1,0:T(8,128)S(1)} copy-done((f32[2,16,768]{2,1,0:T(8,128)S(1)}, f32[2,16,768]{2,1,0:T(8,128)}, u32[]{:S(2)}) %copy-start.1) | copy-done | bytes 98328
  34.1 1.1 %collective-permute-done.8.given = f32[2,16,768]{2,1,0:T(8,128)S(1)} collective-permute-done((f32[2,16,768]{2,1,0:T(8,128)S(1)}, f32[2,16,768]{2,1,0:T(8,128)S(1)}, u32[]{:S(2)}, u32[]{:S(2)}) %collective-permute-start.8) | collective-permute-done | bytes 98336 | tf_op jit(solution)/shard_map/ppermute | solution.py:159
  35.4 2.0 %collective-permute-done.7.given = f32[2,16,768]{2,1,0:T(8,128)S(1)} collective-permute-done((f32[2,16,768]{2,1,0:T(8,128)S(1)}, f32[2,16,768]{2,1,0:T(8,128)S(1)}, u32[]{:S(2)}, u32[]{:S(2)}) %collective-permute-start.7) | collective-permute-done | bytes 98336 | tf_op jit(solution)/shard_map/ppermute | solution.py:159
  37.4 1.0 %two_parts.3 = f32[2,16,768]{2,1,0:T(8,128)} custom-call(s32[64,128]{1,0:T(8,128)S(1)} %get-tuple-element.11.whole_numbers, f32[128,128]{1,0:T(8,128)S(1)} %get-tuple-element.12.weights, f32[2,16,768]{2,1,0:T(8,128)S(1)} %collective-permute-done.7.given, f32[2,16,768]{2,1,0:T(8,128)S(1)} %part.18.base, f32[2,16,768]{2,1,0:T(8,128)S(1)} %part.21.other), custom_call_target="tpu_custom_call" | custom-call | tf_op jit(solution)/shard_map/two_parts/pallas_call | solution.py:147
  (29 shorter events, 3.0 us)
Async XLA Ops:
  0.6 3.6 %copy-start.7 = (f32[2,9]{1,0:T(2,128)S(1)}, f32[2,9]{1,0:T(2,128)}, u32[]{:S(2)}) copy-start(f32[2,9]{1,0:T(2,128)} %cone.1) | copy-start | bytes 220
  0.6 7.8 %collective-permute-start.2 = (f32[2,16,768]{2,1,0:T(8,128)}, f32[2,16,768]{2,1,0:T(8,128)S(1)}, u32[]{:S(2)}, u32[]{:S(2)}) collective-permute-start(f32[2,16,768]{2,1,0:T(8,128)} %refs_0_.1), channel_id=1, source_target_pairs={{0,4},{4,0},{8,12},{12,8},{16,20},{20,16},{24,28},{28,24},{1,5},{5... | collective-permute-start | bytes 294920 | tf_op jit(solution)/shard_map/ppermute | solution.py:159
  2.2 6.7 %collective-permute-start.1 = (f32[2,16,768]{2,1,0:T(8,128)}, f32[2,16,768]{2,1,0:T(8,128)S(1)}, u32[]{:S(2)}, u32[]{:S(2)}) collective-permute-start(f32[2,16,768]{2,1,0:T(8,128)} %refs_0_.1), channel_id=1, source_target_pairs={{0,8},{4,12},{8,0},{12,4},{16,24},{20,28},{24,16},{28,20},{1,9},{5... | collective-permute-start | bytes 294920 | tf_op jit(solution)/shard_map/ppermute | solution.py:159
  3.8 5.7 %collective-permute-start = (f32[2,16,768]{2,1,0:T(8,128)}, f32[2,16,768]{2,1,0:T(8,128)S(1)}, u32[]{:S(2)}, u32[]{:S(2)}) collective-permute-start(f32[2,16,768]{2,1,0:T(8,128)} %refs_0_.1), channel_id=1, source_target_pairs={{0,12},{4,8},{8,4},{12,0},{16,28},{20,24},{24,20},{28,16},{1,13},{... | collective-permute-start | bytes 294920 | tf_op jit(solution)/shard_map/ppermute | solution.py:159
  4.2 0.7 %copy-start.4 = (f32[3,2,16,4]{2,3,1,0:T(4,128)S(1)}, f32[3,2,16,4]{2,3,1,0:T(4,128)}, u32[]{:S(2)}) copy-start(f32[3,2,16,4]{2,3,1,0:T(4,128)} %param.11) | copy-start | bytes 4612
  4.9 0.7 %copy-start.5 = (s32[3,2,16]{2,1,0:T(2,128)S(1)}, s32[3,2,16]{2,1,0:T(2,128)}, u32[]{:S(2)}) copy-start(s32[3,2,16]{2,1,0:T(2,128)} %offset.1) | copy-start | bytes 1156
  5.6 0.7 %copy-start.6 = (s32[3,2,16]{2,1,0:T(2,128)S(1)}, s32[3,2,16]{2,1,0:T(2,128)}, u32[]{:S(2)}) copy-start(s32[3,2,16]{2,1,0:T(2,128)} %source.1) | copy-start | bytes 1156
  7.3 0.9 %copy-start = (f32[2,16,768]{2,1,0:T(8,128)S(1)}, f32[2,16,768]{2,1,0:T(8,128)}, u32[]{:S(2)}) copy-start(f32[2,16,768]{2,1,0:T(8,128)} %refs_0_.1) | copy-start | bytes 294916
  9.9 5.7 %copy-start.2 = (f32[2,16,768]{2,1,0:T(8,128)S(1)}, f32[2,16,768]{2,1,0:T(8,128)}, u32[]{:S(2)}) copy-start(f32[2,16,768]{2,1,0:T(8,128)} %measured.3) | copy-start | bytes 294916
  9.9 5.7 %copy-start.3 = (f32[2,16,768]{2,1,0:T(8,128)S(1)}, f32[2,16,768]{2,1,0:T(8,128)}, u32[]{:S(2)}) copy-start(f32[2,16,768]{2,1,0:T(8,128)} %ray.3) | copy-start | bytes 294916
  9.9 5.7 %collective-permute-start.3 = (f32[2,16,768]{2,1,0:T(8,128)S(1)}, f32[2,16,768]{2,1,0:T(8,128)S(1)}, u32[]{:S(2)}, u32[]{:S(2)}) collective-permute-start(f32[2,16,768]{2,1,0:T(8,128)S(1)} %two_parts.2.given), channel_id=1, source_target_pairs={{0,16},{4,20},{8,24},{12,28},{16,0},{20,4},{24,8},{28,12},{1,17},{... | collective-permute-start | bytes 294920 | tf_op jit(solution)/shard_map/ppermute | solution.py:159
  15.8 2.6 %collective-permute-start.4 = (f32[2,16,768]{2,1,0:T(8,128)S(1)}, f32[2,16,768]{2,1,0:T(8,128)S(1)}, u32[]{:S(2)}, u32[]{:S(2)}) collective-permute-start(f32[2,16,768]{2,1,0:T(8,128)S(1)} %get-tuple-element.14), channel_id=1, source_target_pairs={{0,1},{1,0},{2,3},{3,2},{4,5},{5,4},{6,7},{7,6},{8,9},{9,8},{10,11... | collective-permute-start | bytes 294920 | tf_op jit(solution)/shard_map/ppermute | solution.py:163
  15.9 5.9 %collective-permute-start.5 = (f32[2,16,768]{2,1,0:T(8,128)S(1)}, f32[2,16,768]{2,1,0:T(8,128)S(1)}, u32[]{:S(2)}, u32[]{:S(2)}) collective-permute-start(f32[2,16,768]{2,1,0:T(8,128)S(1)} %get-tuple-element.15), channel_id=1, source_target_pairs={{1,2},{2,1},{5,6},{6,5},{9,10},{10,9},{13,14},{14,13},{17,18},{18,... | collective-permute-start | bytes 294920 | tf_op jit(solution)/shard_map/ppermute | solution.py:168
  22.1 5.6 %collective-permute-start.6 = (f32[2,16,768]{2,1,0:T(8,128)S(1)}, f32[2,16,768]{2,1,0:T(8,128)S(1)}, u32[]{:S(2)}, u32[]{:S(2)}) collective-permute-start(f32[2,16,768]{2,1,0:T(8,128)S(1)} %get-tuple-element.17.given), channel_id=1, source_target_pairs={{0,16},{4,20},{8,24},{12,28},{16,0},{20,4},{24,8},{28,12},{1,17},{... | collective-permute-start | bytes 294920 | tf_op jit(solution)/shard_map/ppermute | solution.py:159
  27.9 5.2 %collective-permute-start.9 = (f32[2,16,768]{2,1,0:T(8,128)S(1)}, f32[2,16,768]{2,1,0:T(8,128)S(1)}, u32[]{:S(2)}, u32[]{:S(2)}) collective-permute-start(f32[2,16,768]{2,1,0:T(8,128)S(1)} %part.17.given), channel_id=1, source_target_pairs={{0,8},{4,12},{8,0},{12,4},{16,24},{20,28},{24,16},{28,20},{1,9},{5... | collective-permute-start | bytes 294920 | tf_op jit(solution)/shard_map/ppermute | solution.py:159
  30.6 4.6 %collective-permute-start.8 = (f32[2,16,768]{2,1,0:T(8,128)S(1)}, f32[2,16,768]{2,1,0:T(8,128)S(1)}, u32[]{:S(2)}, u32[]{:S(2)}) collective-permute-start(f32[2,16,768]{2,1,0:T(8,128)S(1)} %part.17.given), channel_id=1, source_target_pairs={{0,4},{4,0},{8,12},{12,8},{16,20},{20,16},{24,28},{28,24},{1,5},{5... | collective-permute-start | bytes 294920 | tf_op jit(solution)/shard_map/ppermute | solution.py:159
  31.9 5.5 %collective-permute-start.7 = (f32[2,16,768]{2,1,0:T(8,128)S(1)}, f32[2,16,768]{2,1,0:T(8,128)S(1)}, u32[]{:S(2)}, u32[]{:S(2)}) collective-permute-start(f32[2,16,768]{2,1,0:T(8,128)S(1)} %part.17.given), channel_id=1, source_target_pairs={{0,12},{4,8},{8,4},{12,0},{16,28},{20,24},{24,20},{28,16},{1,13},{... | collective-permute-start | bytes 294920 | tf_op jit(solution)/shard_map/ppermute | solution.py:159
  33.0 0.9 %copy-start.1 = (f32[2,16,768]{2,1,0:T(8,128)S(1)}, f32[2,16,768]{2,1,0:T(8,128)}, u32[]{:S(2)}) copy-start(f32[2,16,768]{2,1,0:T(8,128)} %refs_0_.1) | copy-start | bytes 294916

commit v5 on v4

v5 whole, which is shorter than its diff:
```python
import functools

import jax
import jax.numpy as jnp
from jax import lax
from jax.experimental import pallas as pl
from jax.experimental.pallas import tpu as pltpu
from jax.sharding import PartitionSpec as P

LANES = 128
BLOCK = pl.BlockSpec(memory_space=pltpu.VMEM)
SMALL = pltpu.CompilerParams(vmem_limit_bytes=8 << 20)


def shifted_sum(rows, moves, weights, total):
    planes, columns = rows.shape
    count = columns // LANES
    tiles = [rows[:, LANES * j : LANES * (j + 1)] for j in range(count)]
    lane = lax.broadcasted_iota(jnp.int32, (planes, LANES), 1)
    nothing = jnp.zeros((planes, LANES), jnp.float32)
    for move, weight in zip(moves, weights):
        turned = [pltpu.roll(tile, (LANES - move) & (LANES - 1), 1) for tile in tiles]
        below = lane + move < 0
        above = lane + move >= LANES
        for j in range(count):
            left = turned[j - 1] if j > 0 else nothing
            right = turned[j + 1] if j + 1 < count else nothing
            term = weight * jnp.where(below, left, jnp.where(above, right, turned[j]))
            total[j] = term if total[j] is None else total[j] + term
    return total


def table_kernel(entries, views, packed, whole_numbers, weights):
    me = lax.axis_index("view")
    kinds, rows = packed.shape[2:]
    taps = kinds - 2
    lane = lax.broadcasted_iota(jnp.int32, (kinds, rows), 1)
    for index, (level, channel, apart, direction) in enumerate(entries):
        block = packed[level, channel]
        for v in range(views):
            at = index * views + v
            chosen = jnp.sum(
                jnp.where(lane == (me ^ apart) * views + v, block, 0.0), axis=1, keepdims=True
            )
            numbers = chosen[taps:].astype(jnp.int32)
            whole_numbers[2 * at, :] = jnp.broadcast_to(numbers[0] * direction, (LANES,))
            whole_numbers[2 * at + 1, :] = jnp.broadcast_to(numbers[1], (LANES,))
            weights[pl.ds(at * taps, taps), :] = jnp.broadcast_to(chosen[:taps], (taps, LANES))


def level_part(index, direction, whole_numbers, weights, given, base, out):
    views, planes, columns = given.shape
    taps = weights.shape[0] // (whole_numbers.shape[0] // 2)
    count = columns // LANES
    if direction < 0:
        out[...] = jnp.zeros(out.shape, jnp.float32) if base is None else base[...]
    for v in range(views):
        at = index * views + v
        begin, source = whole_numbers[2 * at, 0], whole_numbers[2 * at + 1, 0]
        moves = [begin + direction * k for k in range(taps)]
        factors = [
            jnp.broadcast_to(weights[pl.ds(at * taps + k, 1), :], (planes, LANES))
            for k in range(taps)
        ]
        if direction > 0:
            total = [None] * count
            if base is not None:
                total = [base[v, :, LANES * j : LANES * (j + 1)] for j in range(count)]
            total = shifted_sum(given[source], moves, factors, total)
            for j in range(count):
                out[v, :, LANES * j : LANES * (j + 1)] = total[j]
        else:
            total = shifted_sum(given[v], moves, factors, [None] * count)
            out[source] = out[source] + jnp.concatenate(total, axis=1)


def part_kernel(index, direction, first, whole_numbers, weights, given, *refs):
    out = refs[-1]
    base = refs[0].at[:, pl.ds(first, out.shape[1])] if len(refs) == 2 else None
    level_part(index, direction, whole_numbers, weights, given, base, out)


def own_kernel(index, whole_numbers, weights, given, out, kept):
    level_part(index, 1, whole_numbers, weights, given, None, out)
    kept[...] = given[...]


def two_kernel(first, second, direction, whole_numbers, weights, given, base, other, out, between):
    level_part(first, direction, whole_numbers, weights, given, base, between)
    level_part(second, direction, whole_numbers, weights, between, other, out)


def halves_kernel(state, facing, rest):
    planes, width = state.shape[1], facing.shape[1]
    odd = lax.axis_index("slab") % 2
    facing[...] = state[:, pl.ds(pl.multiple_of(odd * (planes - width), width), width), :]
    rest[...] = state[:, pl.ds(pl.multiple_of((1 - odd) * width, width), planes - width), :]


def edge_kernel(
    reach, beyond, index, whole_numbers, weights, given, base, measured, ray, out, message
):
    level_part(index, 1, whole_numbers, weights, given, base, out)
    width = 2 * reach
    odd = lax.axis_index("slab") % 2
    top = odd if beyond else 1 - odd
    last = pl.multiple_of(top * (out.shape[1] - width), width)
    message[:, :width] = out[:, pl.ds(last, width), :]
    edge = pl.ds(pl.multiple_of(top * (measured.shape[1] - width), width), width)
    row = lax.broadcasted_iota(jnp.int32, (out.shape[0], width, out.shape[2]), 1)
    own = (row >= reach) == (top == 1)
    message[:, width:] = jnp.where(own, measured[:, edge], pltpu.roll(ray[:, edge], reach, 1))


def tilt_kernel(
    cone, rest, facing, pair, across, measured, ray, residual, cotangent, wide, seen, lengths, weighted
):
    views, planes, columns = measured.shape
    width = facing.shape[1]
    reach = width // 2
    crossed = cone.shape[0] // views
    slab = lax.axis_index("slab")
    odd = slab % 2
    at_end = (slab == 0) | (slab == lax.axis_size("slab") - 1)
    far = planes + width
    extended = planes + 2 * reach
    own = pl.ds(width, planes)
    at_facing = pl.ds(pl.multiple_of(width + odd * (planes - width), width), width)
    at_rest = pl.ds(pl.multiple_of(width + (1 - odd) * width, width), planes - width)
    for v in range(views):
        factors = [cone[pl.ds(v * crossed + e, 1), :] for e in range(crossed)]
        for j in range(columns // LANES):
            at = pl.ds(LANES * j, LANES)
            wide[v, j, at_facing] = facing[v, :, at]
            wide[v, j, at_rest] = rest[v, :, at]
            seen[v, j, own] = measured[v, :, at]
            lengths[v, j, own] = ray[v, :, at]
            for message, side, outside in ((pair, 1 - odd, False), (across, odd, at_end)):
                edge = pl.ds(pl.multiple_of(side * far, width), width)
                mixed = jnp.where(outside, 0.0, message[v, width:, at])
                wide[v, j, edge] = jnp.where(outside, 0.0, message[v, :width, at])
                seen[v, j, edge] = mixed
                lengths[v, j, edge] = pltpu.roll(mixed, reach, 0)
            total = factors[0] * wide[v, j, pl.ds(0, extended)]
            for e in range(1, crossed):
                total = total + factors[e] * wide[v, j, pl.ds(e, extended)]
            left = seen[v, j, pl.ds(reach, extended)] - total
            weighted[v, j] = lengths[v, j, pl.ds(reach, extended)] * left
            residual[v, :, at] = left[reach : reach + planes]
            total = factors[0] * weighted[v, j, pl.ds(2 * reach, planes)]
            for e in range(1, crossed):
                total = total + factors[e] * weighted[v, j, pl.ds(2 * reach - e, planes)]
            cotangent[v, :, at] = total


def copy_kernel(given, out):
    out[...] = given[...]


def shaped(*shape, dtype=jnp.float32):
    return jax.ShapeDtypeStruct(shape, dtype)


def call(kernel, out_shape, *args, scratch=(), name):
    return pl.pallas_call(
        kernel,
        out_shape=out_shape,
        in_specs=[BLOCK] * len(args),
        out_specs=jax.tree.map(lambda _: BLOCK, out_shape),
        scratch_shapes=scratch,
        compiler_params=SMALL,
        name=name,
    )(*args)


def across_view(x, apart):
    return lax.ppermute(x, "view", [(i, i ^ apart) for i in range(lax.axis_size("view"))])


def with_pair(x):
    return lax.ppermute(x, "slab", [(i, i ^ 1) for i in range(lax.axis_size("slab"))])


def across_pairs(x):
    views, count = lax.axis_size("view"), lax.axis_size("slab")
    moves = []
    for v in range(views):
        for i in range(count):
            beyond = i + 1 if i % 2 else i - 1
            to = (v, beyond) if 0 <= beyond < count else (v ^ 1, i)
            moves.append((v * count + i, to[0] * count + to[1]))
    return lax.ppermute(x, ("view", "slab"), moves)


def body(leaf_coeffs, measured, ray_weight, cone_weight, interp_weight, shift_offset, source_view):
    views, planes, columns = leaf_coeffs.shape
    crossed = cone_weight.shape[1]
    reach = crossed // 2
    taps = interp_weight.shape[3]
    level_count = lax.axis_size("view").bit_length() - 1
    groups = [(i, i + 1) for i in range(0, level_count - 2, 2)]
    groups += [(i,) for i in range(2 * len(groups), level_count)]
    whole = shaped(views, planes, columns)
    message = shaped(views, 4 * reach, columns)
    assert 2 * reach == 8 and planes % 16 == 0 and columns % LANES == 0

    entries = []

    def entry(level, channel, apart, direction):
        entries.append((level, channel, apart, direction))
        return len(entries) - 1

    forward_entries, back_entries = {}, {}
    for levels in groups:
        low, high = levels[0], levels[-1]
        shapes = [(low, 0), (low, 1)]
        if len(levels) == 2:
            shapes = [(low, 0), (low, 1 << high), (high, 0)]
            backs = [(high, 0), (high, 1 << low), (low, 0)]
        else:
            shapes = backs = [(low, 0)]
        forward_entries[levels] = [
            [entry(level, channel, apart, 1) for channel in (0, 1)] for level, apart in shapes
        ]
        back_entries[levels] = [
            [entry(level, channel, apart ^ (channel << level), -1) for channel in (0, 1)]
            for level, apart in backs
        ]
    packed = jnp.concatenate(
        [jnp.swapaxes(interp_weight, 2, 3)]
        + [x[:, :, None].astype(jnp.float32) for x in (shift_offset, source_view)],
        axis=2,
    )
    tables = call(
        functools.partial(table_kernel, entries, views),
        [
            shaped(len(entries) * views * 2, LANES, dtype=jnp.int32),
            shaped(len(entries) * views * taps, LANES),
        ],
        packed,
        name="tables",
    )
    cone = jnp.broadcast_to(cone_weight.reshape(-1, 1), (views * crossed, LANES))

    def one(index, direction, given, base=None, first=0):
        return call(
            functools.partial(part_kernel, index, direction, first),
            shaped(*given.shape),
            *tables,
            given,
            *(() if base is None else (base,)),
            name="part",
        )

    def two(first, second, direction, given, base, other):
        return call(
            functools.partial(two_kernel, first, second, direction),
            shaped(*given.shape),
            *tables,
            given,
            base,
            other,
            scratch=[pltpu.VMEM(given.shape, jnp.float32)],
            name="two_parts",
        )

    kept = [leaf_coeffs]

    def begin(index, direction, state):
        if state is not leaf_coeffs:
            return one(index, direction, state)
        own, kept[0] = call(
            functools.partial(own_kernel, index), [whole, whole], *tables, state, name="own"
        )
        return own

    def forward_pair(steps, direction, state, first, second, third, base=None):
        own_steps, other_steps, joined = steps
        other = one(other_steps[1], direction, third)
        other = one(other_steps[0], direction, second, other)
        joined_sum = one(joined[1], direction, other, base)
        own = begin(own_steps[0], direction, state)
        return two(own_steps[1], joined[0], direction, first, own, joined_sum)

    def back_pair(steps, direction, state, first, second, third, base=None):
        own_steps, other_steps, joined = steps
        other = one(other_steps[1], direction, third)
        other = one(other_steps[0], direction, second, other)
        joined_sum = one(joined[1], direction, other, base)
        own = begin(own_steps[0], direction, state)
        return two(own_steps[1], joined[0], direction, first, own, joined_sum)

    state = leaf_coeffs
    for levels in groups[:-1]:
        steps = forward_entries[levels]
        near = 1 << levels[0]
        if len(levels) == 2:
            far = 1 << levels[1]
            received = [across_view(state, apart) for apart in (near, far, near + far)]
            state = forward_pair(steps, 1, state, *received)
        else:
            received = across_view(state, near)
            state = one(steps[0][1], 1, received, one(steps[0][0], 1, state))

    own_step, partner_step = forward_entries[groups[-1]][0]
    width = 2 * reach
    halves = call(
        halves_kernel,
        [shaped(views, width, columns), shaped(views, planes - width, columns)],
        state,
        name="halves",
    )
    halves = halves[::-1]
    received = [across_view(half, 1 << groups[-1][0]) for half in halves]
    begun = [one(own_step, 1, half) for half in halves]
    (rest, to_pair), (facing, to_across) = [
        call(
            functools.partial(edge_kernel, reach, beyond, partner_step),
            [shaped(*half.shape), message],
            *tables,
            half,
            base,
            measured,
            ray_weight,
            name="edge",
        )
        for beyond, half, base in zip((False, True), received, begun)
    ]
    from_pair = with_pair(to_pair)
    from_across = across_pairs(to_across)

    residual, cotangent = call(
        tilt_kernel,
        [whole, whole],
        cone,
        rest,
        facing,
        from_pair,
        from_across,
        measured,
        ray_weight,
        scratch=[
            pltpu.VMEM((views, columns // LANES, planes + beyond * reach, LANES), jnp.float32)
            for beyond in (4, 4, 4, 2)
        ],
        name="tilt",
    )

    residual = call(copy_kernel, whole, residual, name="residual")

    state = cotangent
    for levels in reversed(groups):
        steps = back_entries[levels]
        near = 1 << levels[0]
        base = kept[0] if levels == groups[0] else None
        if len(levels) == 2:
            far = 1 << levels[1]
            received = [across_view(state, apart) for apart in (far, near, near + far)]
            state = back_pair(steps, -1, state, *received, base)
        else:
            received = across_view(state, near)
            state = one(steps[0][1], -1, received, one(steps[0][0], -1, state, base))
    return (residual, state)


def solution(mesh):
    in_specs = (
        P("view", "slab", None),
        P("view", "slab", None),
        P("view", "slab", None),
        P("view", None),
        P(),
        P(),
        P(),
    )
    out_specs = (P("view", "slab", None), P("view", "slab", None))
    return jax.shard_map(body, mesh=mesh, in_specs=in_specs, out_specs=out_specs, check_vma=False)
```

time: 38.8 us -> 37.4 us (0.964)
  the two profiles are of different devices: /device:TPU:20 before, /device:TPU:0 now
where the time goes in v5:
time: 37.4 us; the launch traced here: 37.2 us
  starting transfers between devices  15 us (40%)
  waiting for transfers between devices  13.8 us (37%)
  Pallas kernels  5.13 us (14%)
  local copies, waits for them, and re-layouts  1.65 us (4%)
  between operations  0.86 us (2%)
  other arithmetic  0.71 us (2%)
    ppermute x9, starting transfers between devices, across_view(): lax.ppermute(x, 'view', [(i, i ^ apart) for i in range(lax.axis_size('vie...  14 us
    ppermute x9, waiting for transfers between devices, across_view(): lax.ppermute(x, 'view', [(i, i ^ apart) for i in range(lax.axis_size('vie...  12.4 us
    pallas_call x20, Pallas kernels, call(): pl.pallas_call(kernel, out_shape=out_shape, in_specs=[BLOCK] * len(args),...  5.13 us
    unnamed x12, local copies, waits for them, and re-layouts  1.5 us
    ppermute x1, waiting for transfers between devices, across_pairs(): return lax.ppermute(x, ('view', 'slab'), moves)  1.33 us
    ppermute x1, starting transfers between devices, across_pairs(): return lax.ppermute(x, ('view', 'slab'), moves)  1.01 us
  transfers between devices with their start and end apart: 11, of which 8 were waited for; matrix products, arithmetic and copies ran while one was open for 2% of the time, Pallas kernels for 9%

profile of v5, /device:TPU:0, one launch (start us, length us, event | category | flops | bytes accessed | tf_op | source)
XLA Modules:
  0.0 37.2 jit_solution(12907685912207219084)
XLA Ops:
  0.7 4.0 %collective-permute-start.2 = (f32[2,16,768]{2,1,0:T(8,128)}, f32[2,16,768]{2,1,0:T(8,128)S(1)}, u32[]{:S(2)}, u32[]{:S(2)}) collective-permute-start(f32[2,16,768]{2,1,0:T(8,128)} %given.1), channel_id=1, source_target_pairs={{0,12},{4,8},{8,4},{12,0},{16,28},{20,24},{24,20},{28,16},{1,13},{... | collective-permute-start | bytes 294920 | tf_op jit(solution)/shard_map/ppermute | solution.py:177
  4.7 0.4 %collective-permute-start.1 = (f32[2,16,768]{2,1,0:T(8,128)}, f32[2,16,768]{2,1,0:T(8,128)S(1)}, u32[]{:S(2)}, u32[]{:S(2)}) collective-permute-start(f32[2,16,768]{2,1,0:T(8,128)} %given.1), channel_id=1, source_target_pairs={{0,8},{4,12},{8,0},{12,4},{16,24},{20,28},{24,16},{28,20},{1,9},{5... | collective-permute-start | bytes 294920 | tf_op jit(solution)/shard_map/ppermute | solution.py:177
  5.3 0.7 %convert_element_type.12 = f32[3,2,16]{2,1,0:T(2,128)S(1)} convert(s32[3,2,16]{2,1,0:T(2,128)} %param.12) | non-fusion elementwise | flops 96 | bytes 768 | tf_op jit(solution)/shard_map/convert_element_type | solution.py:231
  6.2 0.9 %copy-done.2 = f32[2,16,768]{2,1,0:T(8,128)S(1)} copy-done((f32[2,16,768]{2,1,0:T(8,128)S(1)}, f32[2,16,768]{2,1,0:T(8,128)}, u32[]{:S(2)}) %copy-start.2) | copy-done | bytes 98328
  7.3 1.1 %collective-permute-done.2.given = f32[2,16,768]{2,1,0:T(8,128)S(1)} collective-permute-done((f32[2,16,768]{2,1,0:T(8,128)}, f32[2,16,768]{2,1,0:T(8,128)S(1)}, u32[]{:S(2)}, u32[]{:S(2)}) %collective-permute-start.2) | collective-permute-done | bytes 98336 | tf_op jit(solution)/shard_map/ppermute | solution.py:177
  8.6 1.4 %collective-permute-done.1.given = f32[2,16,768]{2,1,0:T(8,128)S(1)} collective-permute-done((f32[2,16,768]{2,1,0:T(8,128)}, f32[2,16,768]{2,1,0:T(8,128)S(1)}, u32[]{:S(2)}, u32[]{:S(2)}) %collective-permute-start.1) | collective-permute-done | bytes 98336 | tf_op jit(solution)/shard_map/ppermute | solution.py:177
  10.5 0.4 %two_parts.2.state = f32[2,16,768]{2,1,0:T(8,128)S(1)} custom-call(s32[64,128]{1,0:T(8,128)S(1)} %get-tuple-element.14.whole_numbers, f32[128,128]{1,0:T(8,128)S(1)} %get-tuple-element.15.weights, f32[2,16,768]{2,1,0:T(8,128)S(1)} %collective-permute-done.given, f32[2,16,768]{2,1,0:T(8,128)S(1)} %get-tuple-element.16.base, f32[2,16,768]{2,1,0:T(8,128)S(1)} %part.13.other), custom_call_target="tpu_custom_call" | custom-call | tf_op jit(solution)/shard_map/two_parts/pallas_call | solution.py:165
  10.9 2.7 %collective-permute-start.4 = (f32[2,8,768]{2,1,0:T(8,128)S(1)}, f32[2,8,768]{2,1,0:T(8,128)S(1)}, u32[]{:S(2)}, u32[]{:S(2)}) collective-permute-start(f32[2,8,768]{2,1,0:T(8,128)S(1)} %get-tuple-element.19.given), channel_id=1, source_target_pairs={{0,16},{4,20},{8,24},{12,28},{16,0},{20,4},{24,8},{28,12},{1,17},{... | collective-permute-start | bytes 147464 | tf_op jit(solution)/shard_map/ppermute | solution.py:177
  13.5 0.3 collective-permute-start.3
  14.2 1.7 %collective-permute-done.4.given = f32[2,8,768]{2,1,0:T(8,128)S(1)} collective-permute-done((f32[2,8,768]{2,1,0:T(8,128)S(1)}, f32[2,8,768]{2,1,0:T(8,128)S(1)}, u32[]{:S(2)}, u32[]{:S(2)}) %collective-permute-start.4) | collective-permute-done | bytes 49184 | tf_op jit(solution)/shard_map/ppermute | solution.py:177
  16.1 1.0 %collective-permute-start.6 = (f32[2,16,768]{2,1,0:T(8,128)S(1)}, f32[2,16,768]{2,1,0:T(8,128)S(1)}, u32[]{:S(2)}, u32[]{:S(2)}) collective-permute-start(f32[2,16,768]{2,1,0:T(8,128)S(1)} %get-tuple-element.22), channel_id=1, source_target_pairs={{0,4},{1,2},{2,1},{3,7},{4,0},{5,6},{6,5},{7,3},{8,12},{9,10},{10,... | collective-permute-start | bytes 294920 | tf_op jit(solution)/shard_map/ppermute | solution.py:192
  17.1 1.4 %collective-permute-done.3.given = f32[2,8,768]{2,1,0:T(8,128)S(1)} collective-permute-done((f32[2,8,768]{2,1,0:T(8,128)S(1)}, f32[2,8,768]{2,1,0:T(8,128)S(1)}, u32[]{:S(2)}, u32[]{:S(2)}) %collective-permute-start.3) | collective-permute-done | bytes 49184 | tf_op jit(solution)/shard_map/ppermute | solution.py:177
  18.8 0.6 %copy-done.5 = f32[2,9]{1,0:T(2,128)S(1)} copy-done((f32[2,9]{1,0:T(2,128)S(1)}, f32[2,9]{1,0:T(2,128)}, u32[]{:S(2)}) %copy-start.5) | copy-done | bytes 96
  19.4 1.3 %collective-permute-done.6.across = f32[2,16,768]{2,1,0:T(8,128)S(1)} collective-permute-done((f32[2,16,768]{2,1,0:T(8,128)S(1)}, f32[2,16,768]{2,1,0:T(8,128)S(1)}, u32[]{:S(2)}, u32[]{:S(2)}) %collective-permute-start.6) | collective-permute-done | bytes 98336 | tf_op jit(solution)/shard_map/ppermute | solution.py:192
  20.9 0.3 tilt.1
  21.1 2.8 %collective-permute-start.7 = (f32[2,16,768]{2,1,0:T(8,128)S(1)}, f32[2,16,768]{2,1,0:T(8,128)S(1)}, u32[]{:S(2)}, u32[]{:S(2)}) collective-permute-start(f32[2,16,768]{2,1,0:T(8,128)S(1)} %get-tuple-element.24.given), channel_id=1, source_target_pairs={{0,16},{4,20},{8,24},{12,28},{16,0},{20,4},{24,8},{28,12},{1,17},{... | collective-permute-start | bytes 294920 | tf_op jit(solution)/shard_map/ppermute | solution.py:177
  24.1 4.7 %collective-permute-done.7.given = f32[2,16,768]{2,1,0:T(8,128)S(1)} collective-permute-done((f32[2,16,768]{2,1,0:T(8,128)S(1)}, f32[2,16,768]{2,1,0:T(8,128)S(1)}, u32[]{:S(2)}, u32[]{:S(2)}) %collective-permute-start.7) | collective-permute-done | bytes 98336 | tf_op jit(solution)/shard_map/ppermute | solution.py:177
  29.0 1.1 %collective-permute-start.10 = (f32[2,16,768]{2,1,0:T(8,128)S(1)}, f32[2,16,768]{2,1,0:T(8,128)S(1)}, u32[]{:S(2)}, u32[]{:S(2)}) collective-permute-start(f32[2,16,768]{2,1,0:T(8,128)S(1)} %part.17.given), channel_id=1, source_target_pairs={{0,12},{4,8},{8,4},{12,0},{16,28},{20,24},{24,20},{28,16},{1,13},{... | collective-permute-start | bytes 294920 | tf_op jit(solution)/shard_map/ppermute | solution.py:177
  30.2 0.9 %collective-permute-start.9 = (f32[2,16,768]{2,1,0:T(8,128)S(1)}, f32[2,16,768]{2,1,0:T(8,128)S(1)}, u32[]{:S(2)}, u32[]{:S(2)}) collective-permute-start(f32[2,16,768]{2,1,0:T(8,128)S(1)} %part.17.given), channel_id=1, source_target_pairs={{0,4},{4,0},{8,12},{12,8},{16,20},{20,16},{24,28},{28,24},{1,5},{5... | collective-permute-start | bytes 294920 | tf_op jit(solution)/shard_map/ppermute | solution.py:177
  31.1 1.5 %collective-permute-start.8 = (f32[2,16,768]{2,1,0:T(8,128)S(1)}, f32[2,16,768]{2,1,0:T(8,128)S(1)}, u32[]{:S(2)}, u32[]{:S(2)}) collective-permute-start(f32[2,16,768]{2,1,0:T(8,128)S(1)} %part.17.given), channel_id=1, source_target_pairs={{0,8},{4,12},{8,0},{12,4},{16,24},{20,28},{24,16},{28,20},{1,9},{5... | collective-permute-start | bytes 294920 | tf_op jit(solution)/shard_map/ppermute | solution.py:177
  32.6 0.6 %residual.1 = f32[2,16,768]{2,1,0:T(8,128)} custom-call(f32[2,16,768]{2,1,0:T(8,128)S(1)} %get-tuple-element.23.given), custom_call_target="tpu_custom_call" | custom-call | tf_op jit(solution)/shard_map/residual/pallas_call | solution.py:165
  33.4 1.9 %collective-permute-done.10.given = f32[2,16,768]{2,1,0:T(8,128)S(1)} collective-permute-done((f32[2,16,768]{2,1,0:T(8,128)S(1)}, f32[2,16,768]{2,1,0:T(8,128)S(1)}, u32[]{:S(2)}, u32[]{:S(2)}) %collective-permute-start.10) | collective-permute-done | bytes 98336 | tf_op jit(solution)/shard_map/ppermute | solution.py:177
  35.9 0.2 part.21.other
  36.1 1.0 %two_parts.3 = f32[2,16,768]{2,1,0:T(8,128)} custom-call(s32[64,128]{1,0:T(8,128)S(1)} %get-tuple-element.14.whole_numbers, f32[128,128]{1,0:T(8,128)S(1)} %get-tuple-element.15.weights, f32[2,16,768]{2,1,0:T(8,128)S(1)} %collective-permute-done.8.given, f32[2,16,768]{2,1,0:T(8,128)S(1)} %part.18.base, f32[2,16,768]{2,1,0:T(8,128)S(1)} %part.21.other), custom_call_target="tpu_custom_call" | custom-call | tf_op jit(solution)/shard_map/two_parts/pallas_call | solution.py:165
  (35 shorter events, 3.2 us)
Async XLA Ops:
  0.6 5.4 %copy-start.4 = (s32[3,2,16]{2,1,0:T(2,128)S(1)}, s32[3,2,16]{2,1,0:T(2,128)}, u32[]{:S(2)}) copy-start(s32[3,2,16]{2,1,0:T(2,128)} %param.13) | copy-start | bytes 1156
  0.6 5.4 %copy-start.3 = (f32[3,2,16,4]{2,3,1,0:T(4,128)S(1)}, f32[3,2,16,4]{2,3,1,0:T(4,128)}, u32[]{:S(2)}) copy-start(f32[3,2,16,4]{2,3,1,0:T(4,128)} %param.11) | copy-start | bytes 4612
  0.7 7.8 %collective-permute-start.2 = (f32[2,16,768]{2,1,0:T(8,128)}, f32[2,16,768]{2,1,0:T(8,128)S(1)}, u32[]{:S(2)}, u32[]{:S(2)}) collective-permute-start(f32[2,16,768]{2,1,0:T(8,128)} %given.1), channel_id=1, source_target_pairs={{0,12},{4,8},{8,4},{12,0},{16,28},{20,24},{24,20},{28,16},{1,13},{... | collective-permute-start | bytes 294920 | tf_op jit(solution)/shard_map/ppermute | solution.py:177
  4.7 5.4 %collective-permute-start.1 = (f32[2,16,768]{2,1,0:T(8,128)}, f32[2,16,768]{2,1,0:T(8,128)S(1)}, u32[]{:S(2)}, u32[]{:S(2)}) collective-permute-start(f32[2,16,768]{2,1,0:T(8,128)} %given.1), channel_id=1, source_target_pairs={{0,8},{4,12},{8,0},{12,4},{16,24},{20,28},{24,16},{28,20},{1,9},{5... | collective-permute-start | bytes 294920 | tf_op jit(solution)/shard_map/ppermute | solution.py:177
  5.1 5.3 %collective-permute-start = (f32[2,16,768]{2,1,0:T(8,128)}, f32[2,16,768]{2,1,0:T(8,128)S(1)}, u32[]{:S(2)}, u32[]{:S(2)}) collective-permute-start(f32[2,16,768]{2,1,0:T(8,128)} %given.1), channel_id=1, source_target_pairs={{0,4},{4,0},{8,12},{12,8},{16,20},{20,16},{24,28},{28,24},{1,5},{5... | collective-permute-start | bytes 294920 | tf_op jit(solution)/shard_map/ppermute | solution.py:177
  6.2 0.9 %copy-start.2 = (f32[2,16,768]{2,1,0:T(8,128)S(1)}, f32[2,16,768]{2,1,0:T(8,128)}, u32[]{:S(2)}) copy-start(f32[2,16,768]{2,1,0:T(8,128)} %given.1) | copy-start | bytes 294916
  10.9 5.1 %collective-permute-start.4 = (f32[2,8,768]{2,1,0:T(8,128)S(1)}, f32[2,8,768]{2,1,0:T(8,128)S(1)}, u32[]{:S(2)}, u32[]{:S(2)}) collective-permute-start(f32[2,8,768]{2,1,0:T(8,128)S(1)} %get-tuple-element.19.given), channel_id=1, source_target_pairs={{0,16},{4,20},{8,24},{12,28},{16,0},{20,4},{24,8},{28,12},{1,17},{... | collective-permute-start | bytes 147464 | tf_op jit(solution)/shard_map/ppermute | solution.py:177
  13.5 5.0 %collective-permute-start.3 = (f32[2,8,768]{2,1,0:T(8,128)S(1)}, f32[2,8,768]{2,1,0:T(8,128)S(1)}, u32[]{:S(2)}, u32[]{:S(2)}) collective-permute-start(f32[2,8,768]{2,1,0:T(8,128)S(1)} %get-tuple-element.17.given), channel_id=1, source_target_pairs={{0,16},{4,20},{8,24},{12,28},{16,0},{20,4},{24,8},{28,12},{1,17},{... | collective-permute-start | bytes 147464 | tf_op jit(solution)/shard_map/ppermute | solution.py:177
  14.0 1.9 %copy-start = (f32[2,16,768]{2,1,0:T(8,128)S(1)}, f32[2,16,768]{2,1,0:T(8,128)}, u32[]{:S(2)}) copy-start(f32[2,16,768]{2,1,0:T(8,128)} %measured.5) | copy-start | bytes 294916
  14.0 1.9 %copy-start.1 = (f32[2,16,768]{2,1,0:T(8,128)S(1)}, f32[2,16,768]{2,1,0:T(8,128)}, u32[]{:S(2)}) copy-start(f32[2,16,768]{2,1,0:T(8,128)} %ray.5) | copy-start | bytes 294916
  16.1 4.7 %collective-permute-start.6 = (f32[2,16,768]{2,1,0:T(8,128)S(1)}, f32[2,16,768]{2,1,0:T(8,128)S(1)}, u32[]{:S(2)}, u32[]{:S(2)}) collective-permute-start(f32[2,16,768]{2,1,0:T(8,128)S(1)} %get-tuple-element.22), channel_id=1, source_target_pairs={{0,4},{1,2},{2,1},{3,7},{4,0},{5,6},{6,5},{7,3},{8,12},{9,10},{10,... | collective-permute-start | bytes 294920 | tf_op jit(solution)/shard_map/ppermute | solution.py:192
  18.7 0.7 %copy-start.5 = (f32[2,9]{1,0:T(2,128)S(1)}, f32[2,9]{1,0:T(2,128)}, u32[]{:S(2)}) copy-start(f32[2,9]{1,0:T(2,128)} %param.10) | copy-start | bytes 220
  18.7 2.1 %collective-permute-start.5 = (f32[2,16,768]{2,1,0:T(8,128)S(1)}, f32[2,16,768]{2,1,0:T(8,128)S(1)}, u32[]{:S(2)}, u32[]{:S(2)}) collective-permute-start(f32[2,16,768]{2,1,0:T(8,128)S(1)} %get-tuple-element.21), channel_id=1, source_target_pairs={{0,1},{1,0},{2,3},{3,2},{4,5},{5,4},{6,7},{7,6},{8,9},{9,8},{10,11... | collective-permute-start | bytes 294920 | tf_op jit(solution)/shard_map/ppermute | solution.py:181
  21.1 7.7 %collective-permute-start.7 = (f32[2,16,768]{2,1,0:T(8,128)S(1)}, f32[2,16,768]{2,1,0:T(8,128)S(1)}, u32[]{:S(2)}, u32[]{:S(2)}) collective-permute-start(f32[2,16,768]{2,1,0:T(8,128)S(1)} %get-tuple-element.24.given), channel_id=1, source_target_pairs={{0,16},{4,20},{8,24},{12,28},{16,0},{20,4},{24,8},{28,12},{1,17},{... | collective-permute-start | bytes 294920 | tf_op jit(solution)/shard_map/ppermute | solution.py:177
  29.0 6.3 %collective-permute-start.10 = (f32[2,16,768]{2,1,0:T(8,128)S(1)}, f32[2,16,768]{2,1,0:T(8,128)S(1)}, u32[]{:S(2)}, u32[]{:S(2)}) collective-permute-start(f32[2,16,768]{2,1,0:T(8,128)S(1)} %part.17.given), channel_id=1, source_target_pairs={{0,12},{4,8},{8,4},{12,0},{16,28},{20,24},{24,20},{28,16},{1,13},{... | collective-permute-start | bytes 294920 | tf_op jit(solution)/shard_map/ppermute | solution.py:177
  30.2 5.6 %collective-permute-start.9 = (f32[2,16,768]{2,1,0:T(8,128)S(1)}, f32[2,16,768]{2,1,0:T(8,128)S(1)}, u32[]{:S(2)}, u32[]{:S(2)}) collective-permute-start(f32[2,16,768]{2,1,0:T(8,128)S(1)} %part.17.given), channel_id=1, source_target_pairs={{0,4},{4,0},{8,12},{12,8},{16,20},{20,16},{24,28},{28,24},{1,5},{5... | collective-permute-start | bytes 294920 | tf_op jit(solution)/shard_map/ppermute | solution.py:177
  31.1 5.1 %collective-permute-start.8 = (f32[2,16,768]{2,1,0:T(8,128)S(1)}, f32[2,16,768]{2,1,0:T(8,128)S(1)}, u32[]{:S(2)}, u32[]{:S(2)}) collective-permute-start(f32[2,16,768]{2,1,0:T(8,128)S(1)} %part.17.given), channel_id=1, source_target_pairs={{0,8},{4,12},{8,0},{12,4},{16,24},{20,28},{24,16},{28,20},{1,9},{5... | collective-permute-start | bytes 294920 | tf_op jit(solution)/shard_map/ppermute | solution.py:177

commit v6 on v5

--- a/solution.py
+++ b/solution.py
@@ -12,16 +12,17 @@
 SMALL = pltpu.CompilerParams(vmem_limit_bytes=8 << 20)
 
 
-def shifted_sum(rows, moves, weights, total):
+def shifted_sum(rows, move, weights):
     planes, columns = rows.shape
     count = columns // LANES
     tiles = [rows[:, LANES * j : LANES * (j + 1)] for j in range(count)]
     lane = lax.broadcasted_iota(jnp.int32, (planes, LANES), 1)
     nothing = jnp.zeros((planes, LANES), jnp.float32)
-    for move, weight in zip(moves, weights):
-        turned = [pltpu.roll(tile, (LANES - move) & (LANES - 1), 1) for tile in tiles]
-        below = lane + move < 0
-        above = lane + move >= LANES
+    total = [None] * count
+    for k, weight in enumerate(weights):
+        turned = [pltpu.roll(tile, (LANES - move - k) & (LANES - 1), 1) for tile in tiles]
+        below = lane + (move + k) < 0
+        above = lane + (move + k) >= LANES
         for j in range(count):
             left = turned[j - 1] if j > 0 else nothing
             right = turned[j + 1] if j + 1 < count else nothing
@@ -52,37 +53,45 @@
     views, planes, columns = given.shape
     taps = weights.shape[0] // (whole_numbers.shape[0] // 2)
     count = columns // LANES
-    if direction < 0:
-        out[...] = jnp.zeros(out.shape, jnp.float32) if base is None else base[...]
-    for v in range(views):
-        at = index * views + v
-        begin, source = whole_numbers[2 * at, 0], whole_numbers[2 * at + 1, 0]
-        moves = [begin + direction * k for k in range(taps)]
+    rows = [index * views + v for v in range(views)]
+    begins = [whole_numbers[2 * at, 0] for at in rows]
+    sources = [whole_numbers[2 * at + 1, 0] for at in rows]
+    sums = []
+    for v, at in enumerate(rows):
         factors = [
             jnp.broadcast_to(weights[pl.ds(at * taps + k, 1), :], (planes, LANES))
             for k in range(taps)
         ]
         if direction > 0:
-            total = [None] * count
-            if base is not None:
-                total = [base[v, :, LANES * j : LANES * (j + 1)] for j in range(count)]
-            total = shifted_sum(given[source], moves, factors, total)
-            for j in range(count):
-                out[v, :, LANES * j : LANES * (j + 1)] = total[j]
+            sums.append(shifted_sum(given[sources[v]], begins[v], factors))
         else:
-            total = shifted_sum(given[v], moves, factors, [None] * count)
-            out[source] = out[source] + jnp.concatenate(total, axis=1)
-
-
-def part_kernel(index, direction, first, whole_numbers, weights, given, *refs):
-    out = refs[-1]
-    base = refs[0].at[:, pl.ds(first, out.shape[1])] if len(refs) == 2 else None
-    level_part(index, direction, whole_numbers, weights, given, base, out)
+            sums.append(shifted_sum(given[v], begins[v] - (taps - 1), factors[::-1]))
+    for m in range(views):
+        for j in range(count):
+            at = pl.ds(LANES * j, LANES)
+            if direction > 0:
+                total = sums[m][j]
+            else:
+                total = sum(jnp.where(sources[v] == m, sums[v][j], 0.0) for v in range(views))
+            out[m, :, at] = total if base is None else base[m, :, at] + total
+
+
+def part_kernel(index, direction, whole_numbers, weights, given, *refs):
+    base = refs[0] if len(refs) == 2 else None
+    level_part(index, direction, whole_numbers, weights, given, base, refs[-1])
 
 
 def own_kernel(index, whole_numbers, weights, given, out, kept):
     level_part(index, 1, whole_numbers, weights, given, None, out)
     kept[...] = given[...]
+
+
+def four_kernel(steps, direction, whole_numbers, weights, first, second, own, other, *refs):
+    out, near, far, joined = refs
+    level_part(steps[0], direction, whole_numbers, weights, second, other, far)
+    level_part(steps[1], direction, whole_numbers, weights, first, own, near)
+    level_part(steps[2], direction, whole_numbers, weights, far, None, joined)
+    level_part(steps[3], direction, whole_numbers, weights, near, joined, out)
 
 
 def two_kernel(first, second, direction, whole_numbers, weights, given, base, other, out, between):
@@ -113,7 +122,7 @@
 
 
 def tilt_kernel(
-    cone, rest, facing, pair, across, measured, ray, residual, cotangent, wide, seen, lengths, weighted
+    beyond, cone, facing, rest, message, measured, ray, residual, cotangent, wide, seen, lengths, weighted
 ):
     views, planes, columns = measured.shape
     width = facing.shape[1]
@@ -121,40 +130,45 @@
     crossed = cone.shape[0] // views
     slab = lax.axis_index("slab")
     odd = slab % 2
-    at_end = (slab == 0) | (slab == lax.axis_size("slab") - 1)
-    far = planes + width
-    extended = planes + 2 * reach
-    own = pl.ds(width, planes)
-    at_facing = pl.ds(pl.multiple_of(width + odd * (planes - width), width), width)
-    at_rest = pl.ds(pl.multiple_of(width + (1 - odd) * width, width), planes - width)
+    high = odd if beyond else 1 - odd
+    outside = beyond & ((slab == 0) | (slab == lax.axis_size("slab") - 1))
+    begin = (1 - high) * width
+    at_edge = pl.ds(pl.multiple_of(high * planes, width), width)
+    at_own = pl.ds(pl.multiple_of(begin, width), planes)
+    at_facing = pl.ds(pl.multiple_of(begin + odd * (planes - width), width), width)
+    at_rest = pl.ds(pl.multiple_of(begin + (1 - odd) * width, width), planes - width)
+    out = residual.shape[1]
+    extended = out + 2 * reach
+    first = pl.multiple_of(high * (planes - out - width), width)
     for v in range(views):
         factors = [cone[pl.ds(v * crossed + e, 1), :] for e in range(crossed)]
         for j in range(columns // LANES):
             at = pl.ds(LANES * j, LANES)
+            mixed = jnp.where(outside, 0.0, message[v, width:, at])
             wide[v, j, at_facing] = facing[v, :, at]
             wide[v, j, at_rest] = rest[v, :, at]
-            seen[v, j, own] = measured[v, :, at]
-            lengths[v, j, own] = ray[v, :, at]
-            for message, side, outside in ((pair, 1 - odd, False), (across, odd, at_end)):
-                edge = pl.ds(pl.multiple_of(side * far, width), width)
-                mixed = jnp.where(outside, 0.0, message[v, width:, at])
-                wide[v, j, edge] = jnp.where(outside, 0.0, message[v, :width, at])
-                seen[v, j, edge] = mixed
-                lengths[v, j, edge] = pltpu.roll(mixed, reach, 0)
-            total = factors[0] * wide[v, j, pl.ds(0, extended)]
+            wide[v, j, at_edge] = jnp.where(outside, 0.0, message[v, :width, at])
+            seen[v, j, at_own] = measured[v, :, at]
+            seen[v, j, at_edge] = mixed
+            lengths[v, j, at_own] = ray[v, :, at]
+            lengths[v, j, at_edge] = pltpu.roll(mixed, reach, 0)
+            total = factors[0] * wide[v, j, pl.ds(first, extended)]
             for e in range(1, crossed):
-                total = total + factors[e] * wide[v, j, pl.ds(e, extended)]
-            left = seen[v, j, pl.ds(reach, extended)] - total
-            weighted[v, j] = lengths[v, j, pl.ds(reach, extended)] * left
-            residual[v, :, at] = left[reach : reach + planes]
-            total = factors[0] * weighted[v, j, pl.ds(2 * reach, planes)]
+                total = total + factors[e] * wide[v, j, pl.ds(first + e, extended)]
+            left = seen[v, j, pl.ds(first + reach, extended)] - total
+            weighted[v, j] = lengths[v, j, pl.ds(first + reach, extended)] * left
+            residual[v, :, at] = left[reach : reach + out]
+            total = factors[0] * weighted[v, j, pl.ds(2 * reach, out)]
             for e in range(1, crossed):
-                total = total + factors[e] * weighted[v, j, pl.ds(2 * reach - e, planes)]
+                total = total + factors[e] * weighted[v, j, pl.ds(2 * reach - e, out)]
             cotangent[v, :, at] = total
 
 
-def copy_kernel(given, out):
-    out[...] = given[...]
+def unite_kernel(facing, rest, out):
+    planes, width = out.shape[1], facing.shape[1]
+    odd = lax.axis_index("slab") % 2
+    out[:, pl.ds(pl.multiple_of(odd * (planes - width), width), width), :] = facing[...]
+    out[:, pl.ds(pl.multiple_of((1 - odd) * width, width), planes - width), :] = rest[...]
 
 
 def shaped(*shape, dtype=jnp.float32):
@@ -213,7 +227,6 @@
     forward_entries, back_entries = {}, {}
     for levels in groups:
         low, high = levels[0], levels[-1]
-        shapes = [(low, 0), (low, 1)]
         if len(levels) == 2:
             shapes = [(low, 0), (low, 1 << high), (high, 0)]
             backs = [(high, 0), (high, 1 << low), (low, 0)]
@@ -242,9 +255,9 @@
     )
     cone = jnp.broadcast_to(cone_weight.reshape(-1, 1), (views * crossed, LANES))
 
-    def one(index, direction, given, base=None, first=0):
+    def one(index, direction, given, base=None):
         return call(
-            functools.partial(part_kernel, index, direction, first),
+            functools.partial(part_kernel, index, direction),
             shaped(*given.shape),
             *tables,
             given,
@@ -274,13 +287,22 @@
         )
         return own
 
-    def forward_pair(steps, direction, state, first, second, third, base=None):
+    def forward_pair(steps, direction, state, first, second, third):
         own_steps, other_steps, joined = steps
         other = one(other_steps[1], direction, third)
-        other = one(other_steps[0], direction, second, other)
-        joined_sum = one(joined[1], direction, other, base)
         own = begin(own_steps[0], direction, state)
-        return two(own_steps[1], joined[0], direction, first, own, joined_sum)
+        numbers = (other_steps[0], own_steps[1], joined[1], joined[0])
+        return call(
+            functools.partial(four_kernel, numbers, direction),
+            shaped(*state.shape),
+            *tables,
+            first,
+            second,
+            own,
+            other,
+            scratch=[pltpu.VMEM(state.shape, jnp.float32)] * 3,
+            name="four_parts",
+        )
 
     def back_pair(steps, direction, state, first, second, third, base=None):
         own_steps, other_steps, joined = steps
@@ -329,27 +351,35 @@
     from_pair = with_pair(to_pair)
     from_across = across_pairs(to_across)
 
-    residual, cotangent = call(
-        tilt_kernel,
-        [whole, whole],
-        cone,
-        rest,
-        facing,
-        from_pair,
-        from_across,
-        measured,
-        ray_weight,
-        scratch=[
-            pltpu.VMEM((views, columns // LANES, planes + beyond * reach, LANES), jnp.float32)
-            for beyond in (4, 4, 4, 2)
-        ],
-        name="tilt",
-    )
-
-    residual = call(copy_kernel, whole, residual, name="residual")
-
-    state = cotangent
-    for levels in reversed(groups):
+    def tilt(beyond, received, like):
+        return call(
+            functools.partial(tilt_kernel, beyond),
+            [shaped(*like.shape)] * 2,
+            cone,
+            facing,
+            rest,
+            received,
+            measured,
+            ray_weight,
+            scratch=[
+                pltpu.VMEM((views, columns // LANES, rows, LANES), jnp.float32)
+                for rows in [planes + width] * 3 + [like.shape[1] + width]
+            ],
+            name="tilt",
+        )
+
+    last = groups[-1][0]
+    own_step, partner_step = back_entries[groups[-1]][0]
+    residuals, sums = [], []
+    for beyond, received, like in ((False, from_pair, rest), (True, from_across, facing)):
+        residual, cotangent = tilt(beyond, received, like)
+        received = across_view(cotangent, 1 << last)
+        begun = one(own_step, -1, cotangent)
+        residuals.insert(0, residual)
+        sums.insert(0, one(partner_step, -1, received, begun))
+    residual = call(unite_kernel, whole, *residuals, name="residual")
+    state = call(unite_kernel, whole, *sums, name="unite")
+    for levels in reversed(groups[:-1]):
         steps = back_entries[levels]
         near = 1 << levels[0]
         base = kept[0] if levels == groups[0] else None

time: 37.4 us -> 37.4 us (level)
  waiting for transfers between devices: 13.8 us -> 15.3 us
  starting transfers between devices: 15 us -> 14.1 us
  local copies, waits for them, and re-layouts: 1.65 us -> 1.06 us
    ppermute x9 -> x10, starting transfers between devices: 14 us -> 12.1 us  [across_view(): lax.ppermute(x, 'view', [(i, i ^ apart) for i in range(lax.axis_size('vie...]
    ppermute x1, starting transfers between devices: 1.01 us -> 1.99 us  [across_pairs(): return lax.ppermute(x, ('view', 'slab'), moves)]
    ppermute x1, waiting for transfers between devices: 1.33 us -> 2.27 us  [across_pairs(): return lax.ppermute(x, ('view', 'slab'), moves)]
    unnamed x12, local copies, waits for them, and re-layouts: 1.5 us -> 0.91 us
    ppermute x9 -> x10, waiting for transfers between devices: 12.4 us -> 13 us  [across_view(): lax.ppermute(x, 'view', [(i, i ^ apart) for i in range(lax.axis_size('vie...]
    pallas_call x20 -> x22, Pallas kernels: 5.13 us -> 5.21 us  [call(): pl.pallas_call(kernel, out_shape=out_shape, in_specs=[BLOCK] * len(args),...]
  transfers between devices with their start and end apart: 11 -> 12, of which waited for: 8 -> 11; matrix products, arithmetic and copies ran while one was open for 2% -> 2% of each run, Pallas kernels for 9% -> 9%
where the time goes in v6:
time: 37.4 us; the launch traced here: 37.2 us
  waiting for transfers between devices  15.3 us (41%)
  starting transfers between devices  14.1 us (38%)
  Pallas kernels  5.21 us (14%)
  local copies, waits for them, and re-layouts  1.06 us (3%)
  between operations  0.85 us (2%)
  other arithmetic  0.71 us (2%)
    ppermute x10, waiting for transfers between devices, across_view(): lax.ppermute(x, 'view', [(i, i ^ apart) for i in range(lax.axis_size('vie...  13 us
    ppermute x10, starting transfers between devices, across_view(): lax.ppermute(x, 'view', [(i, i ^ apart) for i in range(lax.axis_size('vie...  12.1 us
    pallas_call x22, Pallas kernels, call(): pl.pallas_call(kernel, out_shape=out_shape, in_specs=[BLOCK] * len(args),...  5.21 us
    ppermute x1, waiting for transfers between devices, across_pairs(): return lax.ppermute(x, ('view', 'slab'), moves)  2.27 us
    ppermute x1, starting transfers between devices, across_pairs(): return lax.ppermute(x, ('view', 'slab'), moves)  1.99 us
    unnamed x12, local copies, waits for them, and re-layouts  0.91 us
  transfers between devices with their start and end apart: 12, of which 11 were waited for; matrix products, arithmetic and copies ran while one was open for 2% of the time, Pallas kernels for 9%

profile of v6, /device:TPU:0, one launch (start us, length us, event | category | flops | bytes accessed | tf_op | source)
XLA Modules:
  0.0 37.2 jit_solution(1666742593057860995)
XLA Ops:
  0.7 4.0 %collective-permute-start.2 = (f32[2,16,768]{2,1,0:T(8,128)}, f32[2,16,768]{2,1,0:T(8,128)S(1)}, u32[]{:S(2)}, u32[]{:S(2)}) collective-permute-start(f32[2,16,768]{2,1,0:T(8,128)} %given.1), channel_id=1, source_target_pairs={{0,12},{4,8},{8,4},{12,0},{16,28},{20,24},{24,20},{28,16},{1,13},{... | collective-permute-start | bytes 294920 | tf_op jit(solution)/shard_map/ppermute | solution.py:191
  4.7 0.5 %collective-permute-start = (f32[2,16,768]{2,1,0:T(8,128)}, f32[2,16,768]{2,1,0:T(8,128)S(1)}, u32[]{:S(2)}, u32[]{:S(2)}) collective-permute-start(f32[2,16,768]{2,1,0:T(8,128)} %given.1), channel_id=1, source_target_pairs={{0,4},{4,0},{8,12},{12,8},{16,20},{20,16},{24,28},{28,24},{1,5},{5... | collective-permute-start | bytes 294920 | tf_op jit(solution)/shard_map/ppermute | solution.py:191
  5.3 0.7 %convert_element_type.12 = f32[3,2,16]{2,1,0:T(2,128)S(1)} convert(s32[3,2,16]{2,1,0:T(2,128)} %param.12) | non-fusion elementwise | flops 96 | bytes 768 | tf_op jit(solution)/shard_map/convert_element_type | solution.py:244
  6.2 0.9 %copy-done.2 = f32[2,16,768]{2,1,0:T(8,128)S(1)} copy-done((f32[2,16,768]{2,1,0:T(8,128)S(1)}, f32[2,16,768]{2,1,0:T(8,128)}, u32[]{:S(2)}) %copy-start.2) | copy-done | bytes 98328
  7.3 0.9 %collective-permute-done.2.given = f32[2,16,768]{2,1,0:T(8,128)S(1)} collective-permute-done((f32[2,16,768]{2,1,0:T(8,128)}, f32[2,16,768]{2,1,0:T(8,128)S(1)}, u32[]{:S(2)}, u32[]{:S(2)}) %collective-permute-start.2) | collective-permute-done | bytes 98336 | tf_op jit(solution)/shard_map/ppermute | solution.py:191
  8.4 1.4 %collective-permute-done.first = f32[2,16,768]{2,1,0:T(8,128)S(1)} collective-permute-done((f32[2,16,768]{2,1,0:T(8,128)}, f32[2,16,768]{2,1,0:T(8,128)S(1)}, u32[]{:S(2)}, u32[]{:S(2)}) %collective-permute-start) | collective-permute-done | bytes 98336 | tf_op jit(solution)/shard_map/ppermute | solution.py:191
  9.8 0.2 collective-permute-done.1.second
  10.0 0.5 %four_parts.1.state = f32[2,16,768]{2,1,0:T(8,128)S(1)} custom-call(s32[64,128]{1,0:T(8,128)S(1)} %get-tuple-element.16.whole_numbers, f32[128,128]{1,0:T(8,128)S(1)} %get-tuple-element.17.weights, f32[2,16,768]{2,1,0:T(8,128)S(1)} %collective-permute-done.first, f32[2,16,768]{2,1,0:T(8,128)S(1)} %collective-permute-done.1.second, ...), custom_call_target="tpu_custom_call" | custom-call | tf_op jit(solution)/shard_map/four_parts/pallas_call | solution.py:179
  10.6 2.7 %collective-permute-start.4 = (f32[2,8,768]{2,1,0:T(8,128)S(1)}, f32[2,8,768]{2,1,0:T(8,128)S(1)}, u32[]{:S(2)}, u32[]{:S(2)}) collective-permute-start(f32[2,8,768]{2,1,0:T(8,128)S(1)} %get-tuple-element.21.given), channel_id=1, source_target_pairs={{0,16},{4,20},{8,24},{12,28},{16,0},{20,4},{24,8},{28,12},{1,17},{... | collective-permute-start | bytes 147464 | tf_op jit(solution)/shard_map/ppermute | solution.py:191
  13.2 0.3 collective-permute-start.3
  13.7 2.4 %collective-permute-done.4.given = f32[2,8,768]{2,1,0:T(8,128)S(1)} collective-permute-done((f32[2,8,768]{2,1,0:T(8,128)S(1)}, f32[2,8,768]{2,1,0:T(8,128)S(1)}, u32[]{:S(2)}, u32[]{:S(2)}) %collective-permute-start.4) | collective-permute-done | bytes 49184 | tf_op jit(solution)/shard_map/ppermute | solution.py:191
  16.5 1.8 %collective-permute-done.3.given = f32[2,8,768]{2,1,0:T(8,128)S(1)} collective-permute-done((f32[2,8,768]{2,1,0:T(8,128)S(1)}, f32[2,8,768]{2,1,0:T(8,128)S(1)}, u32[]{:S(2)}, u32[]{:S(2)}) %collective-permute-start.3) | collective-permute-done | bytes 49184 | tf_op jit(solution)/shard_map/ppermute | solution.py:191
  18.5 2.0 %collective-permute-start.5 = (f32[2,16,768]{2,1,0:T(8,128)S(1)}, f32[2,16,768]{2,1,0:T(8,128)S(1)}, u32[]{:S(2)}, u32[]{:S(2)}) collective-permute-start(f32[2,16,768]{2,1,0:T(8,128)S(1)} %get-tuple-element.23), channel_id=1, source_target_pairs={{0,4},{1,2},{2,1},{3,7},{4,0},{5,6},{6,5},{7,3},{8,12},{9,10},{10,... | collective-permute-start | bytes 294920 | tf_op jit(solution)/shard_map/ppermute | solution.py:206
  20.9 2.3 %collective-permute-done.5.message = f32[2,16,768]{2,1,0:T(8,128)S(1)} collective-permute-done((f32[2,16,768]{2,1,0:T(8,128)S(1)}, f32[2,16,768]{2,1,0:T(8,128)S(1)}, u32[]{:S(2)}, u32[]{:S(2)}) %collective-permute-start.5) | collective-permute-done | bytes 98336 | tf_op jit(solution)/shard_map/ppermute | solution.py:206
  23.4 0.7 %collective-permute-start.7 = (f32[2,8,768]{2,1,0:T(8,128)S(1)}, f32[2,8,768]{2,1,0:T(8,128)S(1)}, u32[]{:S(2)}, u32[]{:S(2)}) collective-permute-start(f32[2,8,768]{2,1,0:T(8,128)S(1)} %get-tuple-element.27.given), channel_id=1, source_target_pairs={{0,16},{4,20},{8,24},{12,28},{16,0},{20,4},{24,8},{28,12},{1,17},{... | collective-permute-start | bytes 147464 | tf_op jit(solution)/shard_map/ppermute | solution.py:191
  24.4 2.2 %collective-permute-done.8.given = f32[2,8,768]{2,1,0:T(8,128)S(1)} collective-permute-done((f32[2,8,768]{2,1,0:T(8,128)S(1)}, f32[2,8,768]{2,1,0:T(8,128)S(1)}, u32[]{:S(2)}, u32[]{:S(2)}) %collective-permute-start.8) | collective-permute-done | bytes 49184 | tf_op jit(solution)/shard_map/ppermute | solution.py:191
  26.7 1.7 %collective-permute-done.7.given = f32[2,8,768]{2,1,0:T(8,128)S(1)} collective-permute-done((f32[2,8,768]{2,1,0:T(8,128)S(1)}, f32[2,8,768]{2,1,0:T(8,128)S(1)}, u32[]{:S(2)}, u32[]{:S(2)}) %collective-permute-start.7) | collective-permute-done | bytes 49184 | tf_op jit(solution)/shard_map/ppermute | solution.py:191
  28.7 1.7 %collective-permute-start.11 = (f32[2,16,768]{2,1,0:T(8,128)S(1)}, f32[2,16,768]{2,1,0:T(8,128)S(1)}, u32[]{:S(2)}, u32[]{:S(2)}) collective-permute-start(f32[2,16,768]{2,1,0:T(8,128)S(1)} %unite.1.given), channel_id=1, source_target_pairs={{0,12},{4,8},{8,4},{12,0},{16,28},{20,24},{24,20},{28,16},{1,13},{... | collective-permute-start | bytes 294920 | tf_op jit(solution)/shard_map/ppermute | solution.py:191
  30.3 1.2 %collective-permute-start.10 = (f32[2,16,768]{2,1,0:T(8,128)S(1)}, f32[2,16,768]{2,1,0:T(8,128)S(1)}, u32[]{:S(2)}, u32[]{:S(2)}) collective-permute-start(f32[2,16,768]{2,1,0:T(8,128)S(1)} %unite.1.given), channel_id=1, source_target_pairs={{0,4},{4,0},{8,12},{12,8},{16,20},{20,16},{24,28},{28,24},{1,5},{5... | collective-permute-start | bytes 294920 | tf_op jit(solution)/shard_map/ppermute | solution.py:191
  31.6 0.7 %collective-permute-start.9 = (f32[2,16,768]{2,1,0:T(8,128)S(1)}, f32[2,16,768]{2,1,0:T(8,128)S(1)}, u32[]{:S(2)}, u32[]{:S(2)}) collective-permute-start(f32[2,16,768]{2,1,0:T(8,128)S(1)} %unite.1.given), channel_id=1, source_target_pairs={{0,8},{4,12},{8,0},{12,4},{16,24},{20,28},{24,16},{28,20},{1,9},{5... | collective-permute-start | bytes 294920 | tf_op jit(solution)/shard_map/ppermute | solution.py:191
  32.3 0.7 %residual.1 = f32[2,16,768]{2,1,0:T(8,128)} custom-call(f32[2,8,768]{2,1,0:T(8,128)S(1)} %get-tuple-element.24.facing, f32[2,8,768]{2,1,0:T(8,128)S(1)} %get-tuple-element.26.rest), custom_call_target="tpu_custom_call" | custom-call | tf_op jit(solution)/shard_map/residual/pallas_call | solution.py:179
  33.2 1.6 %collective-permute-done.11.given = f32[2,16,768]{2,1,0:T(8,128)S(1)} collective-permute-done((f32[2,16,768]{2,1,0:T(8,128)S(1)}, f32[2,16,768]{2,1,0:T(8,128)S(1)}, u32[]{:S(2)}, u32[]{:S(2)}) %collective-permute-start.11) | collective-permute-done | bytes 98336 | tf_op jit(solution)/shard_map/ppermute | solution.py:191
  35.0 0.7 %collective-permute-done.10.given = f32[2,16,768]{2,1,0:T(8,128)S(1)} collective-permute-done((f32[2,16,768]{2,1,0:T(8,128)S(1)}, f32[2,16,768]{2,1,0:T(8,128)S(1)}, u32[]{:S(2)}, u32[]{:S(2)}) %collective-permute-start.10) | collective-permute-done | bytes 98336 | tf_op jit(solution)/shard_map/ppermute | solution.py:191
  36.2 1.0 %two_parts.1 = f32[2,16,768]{2,1,0:T(8,128)} custom-call(s32[64,128]{1,0:T(8,128)S(1)} %get-tuple-element.16.whole_numbers, f32[128,128]{1,0:T(8,128)S(1)} %get-tuple-element.17.weights, f32[2,16,768]{2,1,0:T(8,128)S(1)} %collective-permute-done.9.given, f32[2,16,768]{2,1,0:T(8,128)S(1)} %part.18.base, f32[2,16,768]{2,1,0:T(8,128)S(1)} %part.21.other), custom_call_target="tpu_custom_call" | custom-call | tf_op jit(solution)/shard_map/two_parts/pallas_call | solution.py:179
  (39 shorter events, 3.6 us)
Async XLA Ops:
  0.6 5.4 %copy-start.4 = (s32[3,2,16]{2,1,0:T(2,128)S(1)}, s32[3,2,16]{2,1,0:T(2,128)}, u32[]{:S(2)}) copy-start(s32[3,2,16]{2,1,0:T(2,128)} %param.13) | copy-start | bytes 1156
  0.6 5.4 %copy-start.3 = (f32[3,2,16,4]{2,3,1,0:T(4,128)S(1)}, f32[3,2,16,4]{2,3,1,0:T(4,128)}, u32[]{:S(2)}) copy-start(f32[3,2,16,4]{2,3,1,0:T(4,128)} %param.11) | copy-start | bytes 4612
  0.7 7.5 %collective-permute-start.2 = (f32[2,16,768]{2,1,0:T(8,128)}, f32[2,16,768]{2,1,0:T(8,128)S(1)}, u32[]{:S(2)}, u32[]{:S(2)}) collective-permute-start(f32[2,16,768]{2,1,0:T(8,128)} %given.1), channel_id=1, source_target_pairs={{0,12},{4,8},{8,4},{12,0},{16,28},{20,24},{24,20},{28,16},{1,13},{... | collective-permute-start | bytes 294920 | tf_op jit(solution)/shard_map/ppermute | solution.py:191
  4.7 5.1 %collective-permute-start = (f32[2,16,768]{2,1,0:T(8,128)}, f32[2,16,768]{2,1,0:T(8,128)S(1)}, u32[]{:S(2)}, u32[]{:S(2)}) collective-permute-start(f32[2,16,768]{2,1,0:T(8,128)} %given.1), channel_id=1, source_target_pairs={{0,4},{4,0},{8,12},{12,8},{16,20},{20,16},{24,28},{28,24},{1,5},{5... | collective-permute-start | bytes 294920 | tf_op jit(solution)/shard_map/ppermute | solution.py:191
  5.2 4.8 %collective-permute-start.1 = (f32[2,16,768]{2,1,0:T(8,128)}, f32[2,16,768]{2,1,0:T(8,128)S(1)}, u32[]{:S(2)}, u32[]{:S(2)}) collective-permute-start(f32[2,16,768]{2,1,0:T(8,128)} %given.1), channel_id=1, source_target_pairs={{0,8},{4,12},{8,0},{12,4},{16,24},{20,28},{24,16},{28,20},{1,9},{5... | collective-permute-start | bytes 294920 | tf_op jit(solution)/shard_map/ppermute | solution.py:191
  6.2 0.9 %copy-start.2 = (f32[2,16,768]{2,1,0:T(8,128)S(1)}, f32[2,16,768]{2,1,0:T(8,128)}, u32[]{:S(2)}) copy-start(f32[2,16,768]{2,1,0:T(8,128)} %given.1) | copy-start | bytes 294916
  10.6 5.5 %collective-permute-start.4 = (f32[2,8,768]{2,1,0:T(8,128)S(1)}, f32[2,8,768]{2,1,0:T(8,128)S(1)}, u32[]{:S(2)}, u32[]{:S(2)}) collective-permute-start(f32[2,8,768]{2,1,0:T(8,128)S(1)} %get-tuple-element.21.given), channel_id=1, source_target_pairs={{0,16},{4,20},{8,24},{12,28},{16,0},{20,4},{24,8},{28,12},{1,17},{... | collective-permute-start | bytes 147464 | tf_op jit(solution)/shard_map/ppermute | solution.py:191
  13.2 2.9 %copy-start = (f32[2,16,768]{2,1,0:T(8,128)S(1)}, f32[2,16,768]{2,1,0:T(8,128)}, u32[]{:S(2)}) copy-start(f32[2,16,768]{2,1,0:T(8,128)} %measured.7) | copy-start | bytes 294916
  13.2 2.9 %copy-start.1 = (f32[2,16,768]{2,1,0:T(8,128)S(1)}, f32[2,16,768]{2,1,0:T(8,128)}, u32[]{:S(2)}) copy-start(f32[2,16,768]{2,1,0:T(8,128)} %ray.7) | copy-start | bytes 294916
  13.2 5.1 %collective-permute-start.3 = (f32[2,8,768]{2,1,0:T(8,128)S(1)}, f32[2,8,768]{2,1,0:T(8,128)S(1)}, u32[]{:S(2)}, u32[]{:S(2)}) collective-permute-start(f32[2,8,768]{2,1,0:T(8,128)S(1)} %get-tuple-element.19.given), channel_id=1, source_target_pairs={{0,16},{4,20},{8,24},{12,28},{16,0},{20,4},{24,8},{28,12},{1,17},{... | collective-permute-start | bytes 147464 | tf_op jit(solution)/shard_map/ppermute | solution.py:191
  16.3 4.3 %collective-permute-start.6 = (f32[2,16,768]{2,1,0:T(8,128)S(1)}, f32[2,16,768]{2,1,0:T(8,128)S(1)}, u32[]{:S(2)}, u32[]{:S(2)}) collective-permute-start(f32[2,16,768]{2,1,0:T(8,128)S(1)} %get-tuple-element.25), channel_id=1, source_target_pairs={{0,1},{1,0},{2,3},{3,2},{4,5},{5,4},{6,7},{7,6},{8,9},{9,8},{10,11... | collective-permute-start | bytes 294920 | tf_op jit(solution)/shard_map/ppermute | solution.py:195
  18.5 2.0 %copy-start.5 = (f32[2,9]{1,0:T(2,128)S(1)}, f32[2,9]{1,0:T(2,128)}, u32[]{:S(2)}) copy-start(f32[2,9]{1,0:T(2,128)} %param.10) | copy-start | bytes 220
  18.5 4.7 %collective-permute-start.5 = (f32[2,16,768]{2,1,0:T(8,128)S(1)}, f32[2,16,768]{2,1,0:T(8,128)S(1)}, u32[]{:S(2)}, u32[]{:S(2)}) collective-permute-start(f32[2,16,768]{2,1,0:T(8,128)S(1)} %get-tuple-element.23), channel_id=1, source_target_pairs={{0,4},{1,2},{2,1},{3,7},{4,0},{5,6},{6,5},{7,3},{8,12},{9,10},{10,... | collective-permute-start | bytes 294920 | tf_op jit(solution)/shard_map/ppermute | solution.py:206
  20.8 5.7 %collective-permute-start.8 = (f32[2,8,768]{2,1,0:T(8,128)S(1)}, f32[2,8,768]{2,1,0:T(8,128)S(1)}, u32[]{:S(2)}, u32[]{:S(2)}) collective-permute-start(f32[2,8,768]{2,1,0:T(8,128)S(1)} %get-tuple-element.28.given), channel_id=1, source_target_pairs={{0,16},{4,20},{8,24},{12,28},{16,0},{20,4},{24,8},{28,12},{1,17},{... | collective-permute-start | bytes 147464 | tf_op jit(solution)/shard_map/ppermute | solution.py:191
  23.4 5.1 %collective-permute-start.7 = (f32[2,8,768]{2,1,0:T(8,128)S(1)}, f32[2,8,768]{2,1,0:T(8,128)S(1)}, u32[]{:S(2)}, u32[]{:S(2)}) collective-permute-start(f32[2,8,768]{2,1,0:T(8,128)S(1)} %get-tuple-element.27.given), channel_id=1, source_target_pairs={{0,16},{4,20},{8,24},{12,28},{16,0},{20,4},{24,8},{28,12},{1,17},{... | collective-permute-start | bytes 147464 | tf_op jit(solution)/shard_map/ppermute | solution.py:191
  28.7 6.1 %collective-permute-start.11 = (f32[2,16,768]{2,1,0:T(8,128)S(1)}, f32[2,16,768]{2,1,0:T(8,128)S(1)}, u32[]{:S(2)}, u32[]{:S(2)}) collective-permute-start(f32[2,16,768]{2,1,0:T(8,128)S(1)} %unite.1.given), channel_id=1, source_target_pairs={{0,12},{4,8},{8,4},{12,0},{16,28},{20,24},{24,20},{28,16},{1,13},{... | collective-permute-start | bytes 294920 | tf_op jit(solution)/shard_map/ppermute | solution.py:191
  30.3 5.3 %collective-permute-start.10 = (f32[2,16,768]{2,1,0:T(8,128)S(1)}, f32[2,16,768]{2,1,0:T(8,128)S(1)}, u32[]{:S(2)}, u32[]{:S(2)}) collective-permute-start(f32[2,16,768]{2,1,0:T(8,128)S(1)} %unite.1.given), channel_id=1, source_target_pairs={{0,4},{4,0},{8,12},{12,8},{16,20},{20,16},{24,28},{28,24},{1,5},{5... | collective-permute-start | bytes 294920 | tf_op jit(solution)/shard_map/ppermute | solution.py:191
  31.6 4.6 %collective-permute-start.9 = (f32[2,16,768]{2,1,0:T(8,128)S(1)}, f32[2,16,768]{2,1,0:T(8,128)S(1)}, u32[]{:S(2)}, u32[]{:S(2)}) collective-permute-start(f32[2,16,768]{2,1,0:T(8,128)S(1)} %unite.1.given), channel_id=1, source_target_pairs={{0,8},{4,12},{8,0},{12,4},{16,24},{20,28},{24,16},{28,20},{1,9},{5... | collective-permute-start | bytes 294920 | tf_op jit(solution)/shard_map/ppermute | solution.py:191

commit v7 on v5

--- a/solution.py
+++ b/solution.py
@@ -97,23 +97,27 @@
     rest[...] = state[:, pl.ds(pl.multiple_of((1 - odd) * width, width), planes - width), :]
 
 
-def edge_kernel(
-    reach, beyond, index, whole_numbers, weights, given, base, measured, ray, out, message
-):
+def mix_kernel(reach, measured, ray, token, pair, across):
+    width = 2 * reach
+    odd = lax.axis_index("slab") % 2
+    row = lax.broadcasted_iota(jnp.int32, pair.shape, 1)
+    for mixed, top in ((pair, 1 - odd), (across, odd)):
+        edge = pl.ds(pl.multiple_of(top * (measured.shape[1] - width), width), width)
+        own = (row >= reach) == (top == 1)
+        mixed[...] = jnp.where(own, measured[:, edge], pltpu.roll(ray[:, edge], reach, 1))
+
+
+def edge_kernel(reach, beyond, index, whole_numbers, weights, given, base, out, message):
     level_part(index, 1, whole_numbers, weights, given, base, out)
     width = 2 * reach
     odd = lax.axis_index("slab") % 2
     top = odd if beyond else 1 - odd
     last = pl.multiple_of(top * (out.shape[1] - width), width)
-    message[:, :width] = out[:, pl.ds(last, width), :]
-    edge = pl.ds(pl.multiple_of(top * (measured.shape[1] - width), width), width)
-    row = lax.broadcasted_iota(jnp.int32, (out.shape[0], width, out.shape[2]), 1)
-    own = (row >= reach) == (top == 1)
-    message[:, width:] = jnp.where(own, measured[:, edge], pltpu.roll(ray[:, edge], reach, 1))
+    message[...] = out[:, pl.ds(last, width), :]
 
 
 def tilt_kernel(
-    cone, rest, facing, pair, across, measured, ray, residual, cotangent, wide, seen, lengths, weighted
+    cone, rest, facing, pair, across, pair_mix, across_mix, measured, ray, residual, cotangent, wide, seen, lengths, weighted
 ):
     views, planes, columns = measured.shape
     width = facing.shape[1]
@@ -135,10 +139,13 @@
             wide[v, j, at_rest] = rest[v, :, at]
             seen[v, j, own] = measured[v, :, at]
             lengths[v, j, own] = ray[v, :, at]
-            for message, side, outside in ((pair, 1 - odd, False), (across, odd, at_end)):
+            for message, mixture, side, outside in (
+                (pair, pair_mix, 1 - odd, False),
+                (across, across_mix, odd, at_end),
+            ):
                 edge = pl.ds(pl.multiple_of(side * far, width), width)
-                mixed = jnp.where(outside, 0.0, message[v, width:, at])
-                wide[v, j, edge] = jnp.where(outside, 0.0, message[v, :width, at])
+                mixed = jnp.where(outside, 0.0, mixture[v, :, at])
+                wide[v, j, edge] = jnp.where(outside, 0.0, message[v, :, at])
                 seen[v, j, edge] = mixed
                 lengths[v, j, edge] = pltpu.roll(mixed, reach, 0)
             total = factors[0] * wide[v, j, pl.ds(0, extended)]
@@ -201,7 +208,7 @@
     groups = [(i, i + 1) for i in range(0, level_count - 2, 2)]
     groups += [(i,) for i in range(2 * len(groups), level_count)]
     whole = shaped(views, planes, columns)
-    message = shaped(views, 4 * reach, columns)
+    message = shaped(views, 2 * reach, columns)
     assert 2 * reach == 8 and planes % 16 == 0 and columns % LANES == 0
 
     entries = []
@@ -302,6 +309,16 @@
             received = across_view(state, near)
             state = one(steps[0][1], 1, received, one(steps[0][0], 1, state))
 
+    pair_mix, across_mix = call(
+        functools.partial(mix_kernel, reach),
+        [message, message],
+        measured,
+        ray_weight,
+        kept[0],
+        name="mix",
+    )
+    pair_mix, across_mix = with_pair(pair_mix), across_pairs(across_mix)
+
     own_step, partner_step = forward_entries[groups[-1]][0]
     width = 2 * reach
     halves = call(
@@ -320,8 +337,6 @@
             *tables,
             half,
             base,
-            measured,
-            ray_weight,
             name="edge",
         )
         for beyond, half, base in zip((False, True), received, begun)
@@ -337,6 +352,8 @@
         facing,
         from_pair,
         from_across,
+        pair_mix,
+        across_mix,
         measured,
         ray_weight,
         scratch=[

time: 37.4 us -> 36.8 us (0.984)
  waiting for transfers between devices: 13.8 us -> 12.2 us
  starting transfers between devices: 15 us -> 16.1 us
    ppermute x9, waiting for transfers between devices: 12.4 us -> 11.4 us  [across_view(): lax.ppermute(x, 'view', [(i, i ^ apart) for i in range(lax.axis_size('vie...]
    ppermute x1 -> x2, starting transfers between devices: 1.01 us -> 1.99 us  [across_pairs(): return lax.ppermute(x, ('view', 'slab'), moves)]
    ppermute x1 -> x2, waiting for transfers between devices: 1.33 us -> 0.8 us  [across_pairs(): return lax.ppermute(x, ('view', 'slab'), moves)]
    pallas_call x20 -> x21, Pallas kernels: 5.13 us -> 5.15 us  [call(): pl.pallas_call(kernel, out_shape=out_shape, in_specs=[BLOCK] * len(args),...]
  transfers between devices with their start and end apart: 11 -> 13, of which waited for: 8 -> 8; matrix products, arithmetic and copies ran while one was open for 2% -> 2% of each run, Pallas kernels for 9% -> 9%
where the time goes in v7:
time: 36.8 us; the launch traced here: 36.7 us
  starting transfers between devices  16.1 us (44%)
  waiting for transfers between devices  12.2 us (33%)
  Pallas kernels  5.15 us (14%)
  local copies, waits for them, and re-layouts  1.65 us (4%)
  between operations  0.88 us (2%)
  other arithmetic  0.71 us (2%)
    ppermute x9, starting transfers between devices, across_view(): lax.ppermute(x, 'view', [(i, i ^ apart) for i in range(lax.axis_size('vie...  14 us
    ppermute x9, waiting for transfers between devices, across_view(): lax.ppermute(x, 'view', [(i, i ^ apart) for i in range(lax.axis_size('vie...  11.4 us
    pallas_call x21, Pallas kernels, call(): pl.pallas_call(kernel, out_shape=out_shape, in_specs=[BLOCK] * len(args),...  5.15 us
    ppermute x2, starting transfers between devices, across_pairs(): return lax.ppermute(x, ('view', 'slab'), moves)  1.99 us
    unnamed x12, local copies, waits for them, and re-layouts  1.5 us
    ppermute x2, waiting for transfers between devices, across_pairs(): return lax.ppermute(x, ('view', 'slab'), moves)  0.8 us
  transfers between devices with their start and end apart: 13, of which 8 were waited for; matrix products, arithmetic and copies ran while one was open for 2% of the time, Pallas kernels for 9%

profile of v7, /device:TPU:0, one launch (start us, length us, event | category | flops | bytes accessed | tf_op | source)
XLA Modules:
  0.0 36.7 jit_solution(15803125126211066285)
XLA Ops:
  0.7 4.0 %collective-permute-start.2 = (f32[2,16,768]{2,1,0:T(8,128)}, f32[2,16,768]{2,1,0:T(8,128)S(1)}, u32[]{:S(2)}, u32[]{:S(2)}) collective-permute-start(f32[2,16,768]{2,1,0:T(8,128)} %given.1), channel_id=1, source_target_pairs={{0,12},{4,8},{8,4},{12,0},{16,28},{20,24},{24,20},{28,16},{1,13},{... | collective-permute-start | bytes 294920 | tf_op jit(solution)/shard_map/ppermute | solution.py:184
  4.7 0.4 %collective-permute-start.1 = (f32[2,16,768]{2,1,0:T(8,128)}, f32[2,16,768]{2,1,0:T(8,128)S(1)}, u32[]{:S(2)}, u32[]{:S(2)}) collective-permute-start(f32[2,16,768]{2,1,0:T(8,128)} %given.1), channel_id=1, source_target_pairs={{0,8},{4,12},{8,0},{12,4},{16,24},{20,28},{24,16},{28,20},{1,9},{5... | collective-permute-start | bytes 294920 | tf_op jit(solution)/shard_map/ppermute | solution.py:184
  5.3 0.7 %convert_element_type.12 = f32[3,2,16]{2,1,0:T(2,128)S(1)} convert(s32[3,2,16]{2,1,0:T(2,128)} %param.12) | non-fusion elementwise | flops 96 | bytes 768 | tf_op jit(solution)/shard_map/convert_element_type | solution.py:238
  6.2 0.9 %copy-done.2 = f32[2,16,768]{2,1,0:T(8,128)S(1)} copy-done((f32[2,16,768]{2,1,0:T(8,128)S(1)}, f32[2,16,768]{2,1,0:T(8,128)}, u32[]{:S(2)}) %copy-start.2) | copy-done | bytes 98328
  7.3 1.1 %collective-permute-done.2.given = f32[2,16,768]{2,1,0:T(8,128)S(1)} collective-permute-done((f32[2,16,768]{2,1,0:T(8,128)}, f32[2,16,768]{2,1,0:T(8,128)S(1)}, u32[]{:S(2)}, u32[]{:S(2)}) %collective-permute-start.2) | collective-permute-done | bytes 98336 | tf_op jit(solution)/shard_map/ppermute | solution.py:184
  8.6 1.4 %collective-permute-done.1.given = f32[2,16,768]{2,1,0:T(8,128)S(1)} collective-permute-done((f32[2,16,768]{2,1,0:T(8,128)}, f32[2,16,768]{2,1,0:T(8,128)S(1)}, u32[]{:S(2)}, u32[]{:S(2)}) %collective-permute-start.1) | collective-permute-done | bytes 98336 | tf_op jit(solution)/shard_map/ppermute | solution.py:184
  10.5 0.4 %two_parts.2.state = f32[2,16,768]{2,1,0:T(8,128)S(1)} custom-call(s32[64,128]{1,0:T(8,128)S(1)} %get-tuple-element.16.whole_numbers, f32[128,128]{1,0:T(8,128)S(1)} %get-tuple-element.17.weights, f32[2,16,768]{2,1,0:T(8,128)S(1)} %collective-permute-done.given, f32[2,16,768]{2,1,0:T(8,128)S(1)} %get-tuple-element.18.base, f32[2,16,768]{2,1,0:T(8,128)S(1)} %part.13.other), custom_call_target="tpu_custom_call" | custom-call | tf_op jit(solution)/shard_map/two_parts/pallas_call | solution.py:172
  10.9 2.7 %collective-permute-start.4 = (f32[2,8,768]{2,1,0:T(8,128)S(1)}, f32[2,8,768]{2,1,0:T(8,128)S(1)}, u32[]{:S(2)}, u32[]{:S(2)}) collective-permute-start(f32[2,8,768]{2,1,0:T(8,128)S(1)} %get-tuple-element.21.given), channel_id=1, source_target_pairs={{0,16},{4,20},{8,24},{12,28},{16,0},{20,4},{24,8},{28,12},{1,17},{... | collective-permute-start | bytes 147464 | tf_op jit(solution)/shard_map/ppermute | solution.py:184
  13.6 0.3 collective-permute-start.3
  14.0 1.0 %collective-permute-start.8 = (f32[2,8,768]{2,1,0:T(8,128)S(1)}, f32[2,8,768]{2,1,0:T(8,128)S(1)}, u32[]{:S(2)}, u32[]{:S(2)}) collective-permute-start(f32[2,8,768]{2,1,0:T(8,128)S(1)} %get-tuple-element.27), channel_id=1, source_target_pairs={{0,4},{1,2},{2,1},{3,7},{4,0},{5,6},{6,5},{7,3},{8,12},{9,10},{10,... | collective-permute-start | bytes 147464 | tf_op jit(solution)/shard_map/ppermute | solution.py:199
  15.3 0.6 %collective-permute-done.4.given = f32[2,8,768]{2,1,0:T(8,128)S(1)} collective-permute-done((f32[2,8,768]{2,1,0:T(8,128)S(1)}, f32[2,8,768]{2,1,0:T(8,128)S(1)}, u32[]{:S(2)}, u32[]{:S(2)}) %collective-permute-start.4) | collective-permute-done | bytes 49184 | tf_op jit(solution)/shard_map/ppermute | solution.py:184
  16.1 1.0 %collective-permute-start.6 = (f32[2,8,768]{2,1,0:T(8,128)S(1)}, f32[2,8,768]{2,1,0:T(8,128)S(1)}, u32[]{:S(2)}, u32[]{:S(2)}) collective-permute-start(f32[2,8,768]{2,1,0:T(8,128)S(1)} %get-tuple-element.24), channel_id=1, source_target_pairs={{0,4},{1,2},{2,1},{3,7},{4,0},{5,6},{6,5},{7,3},{8,12},{9,10},{10,... | collective-permute-start | bytes 147464 | tf_op jit(solution)/shard_map/ppermute | solution.py:199
  17.1 1.4 %collective-permute-done.3.given = f32[2,8,768]{2,1,0:T(8,128)S(1)} collective-permute-done((f32[2,8,768]{2,1,0:T(8,128)S(1)}, f32[2,8,768]{2,1,0:T(8,128)S(1)}, u32[]{:S(2)}, u32[]{:S(2)}) %collective-permute-start.3) | collective-permute-done | bytes 49184 | tf_op jit(solution)/shard_map/ppermute | solution.py:184
  18.8 0.6 %copy-done.5 = f32[2,9]{1,0:T(2,128)S(1)} copy-done((f32[2,9]{1,0:T(2,128)S(1)}, f32[2,9]{1,0:T(2,128)}, u32[]{:S(2)}) %copy-start.5) | copy-done | bytes 96
  19.5 0.8 %collective-permute-done.6.across = f32[2,8,768]{2,1,0:T(8,128)S(1)} collective-permute-done((f32[2,8,768]{2,1,0:T(8,128)S(1)}, f32[2,8,768]{2,1,0:T(8,128)S(1)}, u32[]{:S(2)}, u32[]{:S(2)}) %collective-permute-start.6) | collective-permute-done | bytes 49184 | tf_op jit(solution)/shard_map/ppermute | solution.py:199
  20.3 0.3 tilt.1
  20.6 2.8 %collective-permute-start.9 = (f32[2,16,768]{2,1,0:T(8,128)S(1)}, f32[2,16,768]{2,1,0:T(8,128)S(1)}, u32[]{:S(2)}, u32[]{:S(2)}) collective-permute-start(f32[2,16,768]{2,1,0:T(8,128)S(1)} %get-tuple-element.29.given), channel_id=1, source_target_pairs={{0,16},{4,20},{8,24},{12,28},{16,0},{20,4},{24,8},{28,12},{1,17},{... | collective-permute-start | bytes 294920 | tf_op jit(solution)/shard_map/ppermute | solution.py:184
  23.6 4.7 %collective-permute-done.9.given = f32[2,16,768]{2,1,0:T(8,128)S(1)} collective-permute-done((f32[2,16,768]{2,1,0:T(8,128)S(1)}, f32[2,16,768]{2,1,0:T(8,128)S(1)}, u32[]{:S(2)}, u32[]{:S(2)}) %collective-permute-start.9) | collective-permute-done | bytes 98336 | tf_op jit(solution)/shard_map/ppermute | solution.py:184
  28.5 1.1 %collective-permute-start.12 = (f32[2,16,768]{2,1,0:T(8,128)S(1)}, f32[2,16,768]{2,1,0:T(8,128)S(1)}, u32[]{:S(2)}, u32[]{:S(2)}) collective-permute-start(f32[2,16,768]{2,1,0:T(8,128)S(1)} %part.17.given), channel_id=1, source_target_pairs={{0,12},{4,8},{8,4},{12,0},{16,28},{20,24},{24,20},{28,16},{1,13},{... | collective-permute-start | bytes 294920 | tf_op jit(solution)/shard_map/ppermute | solution.py:184
  29.6 1.0 %collective-permute-start.11 = (f32[2,16,768]{2,1,0:T(8,128)S(1)}, f32[2,16,768]{2,1,0:T(8,128)S(1)}, u32[]{:S(2)}, u32[]{:S(2)}) collective-permute-start(f32[2,16,768]{2,1,0:T(8,128)S(1)} %part.17.given), channel_id=1, source_target_pairs={{0,4},{4,0},{8,12},{12,8},{16,20},{20,16},{24,28},{28,24},{1,5},{5... | collective-permute-start | bytes 294920 | tf_op jit(solution)/shard_map/ppermute | solution.py:184
  30.6 1.5 %collective-permute-start.10 = (f32[2,16,768]{2,1,0:T(8,128)S(1)}, f32[2,16,768]{2,1,0:T(8,128)S(1)}, u32[]{:S(2)}, u32[]{:S(2)}) collective-permute-start(f32[2,16,768]{2,1,0:T(8,128)S(1)} %part.17.given), channel_id=1, source_target_pairs={{0,8},{4,12},{8,0},{12,4},{16,24},{20,28},{24,16},{28,20},{1,9},{5... | collective-permute-start | bytes 294920 | tf_op jit(solution)/shard_map/ppermute | solution.py:184
  32.1 0.6 %residual.1 = f32[2,16,768]{2,1,0:T(8,128)} custom-call(f32[2,16,768]{2,1,0:T(8,128)S(1)} %get-tuple-element.28.given), custom_call_target="tpu_custom_call" | custom-call | tf_op jit(solution)/shard_map/residual/pallas_call | solution.py:172
  32.9 1.9 %collective-permute-done.12.given = f32[2,16,768]{2,1,0:T(8,128)S(1)} collective-permute-done((f32[2,16,768]{2,1,0:T(8,128)S(1)}, f32[2,16,768]{2,1,0:T(8,128)S(1)}, u32[]{:S(2)}, u32[]{:S(2)}) %collective-permute-start.12) | collective-permute-done | bytes 98336 | tf_op jit(solution)/shard_map/ppermute | solution.py:184
  35.6 1.0 %two_parts.3 = f32[2,16,768]{2,1,0:T(8,128)} custom-call(s32[64,128]{1,0:T(8,128)S(1)} %get-tuple-element.16.whole_numbers, f32[128,128]{1,0:T(8,128)S(1)} %get-tuple-element.17.weights, f32[2,16,768]{2,1,0:T(8,128)S(1)} %collective-permute-done.10.given, f32[2,16,768]{2,1,0:T(8,128)S(1)} %part.18.base, f32[2,16,768]{2,1,0:T(8,128)S(1)} %part.21.other), custom_call_target="tpu_custom_call" | custom-call | tf_op jit(solution)/shard_map/two_parts/pallas_call | solution.py:172
  (40 shorter events, 3.5 us)
Async XLA Ops:
  0.6 5.4 %copy-start.4 = (s32[3,2,16]{2,1,0:T(2,128)S(1)}, s32[3,2,16]{2,1,0:T(2,128)}, u32[]{:S(2)}) copy-start(s32[3,2,16]{2,1,0:T(2,128)} %param.13) | copy-start | bytes 1156
  0.6 5.4 %copy-start.3 = (f32[3,2,16,4]{2,3,1,0:T(4,128)S(1)}, f32[3,2,16,4]{2,3,1,0:T(4,128)}, u32[]{:S(2)}) copy-start(f32[3,2,16,4]{2,3,1,0:T(4,128)} %param.11) | copy-start | bytes 4612
  0.7 7.8 %collective-permute-start.2 = (f32[2,16,768]{2,1,0:T(8,128)}, f32[2,16,768]{2,1,0:T(8,128)S(1)}, u32[]{:S(2)}, u32[]{:S(2)}) collective-permute-start(f32[2,16,768]{2,1,0:T(8,128)} %given.1), channel_id=1, source_target_pairs={{0,12},{4,8},{8,4},{12,0},{16,28},{20,24},{24,20},{28,16},{1,13},{... | collective-permute-start | bytes 294920 | tf_op jit(solution)/shard_map/ppermute | solution.py:184
  4.7 5.4 %collective-permute-start.1 = (f32[2,16,768]{2,1,0:T(8,128)}, f32[2,16,768]{2,1,0:T(8,128)S(1)}, u32[]{:S(2)}, u32[]{:S(2)}) collective-permute-start(f32[2,16,768]{2,1,0:T(8,128)} %given.1), channel_id=1, source_target_pairs={{0,8},{4,12},{8,0},{12,4},{16,24},{20,28},{24,16},{28,20},{1,9},{5... | collective-permute-start | bytes 294920 | tf_op jit(solution)/shard_map/ppermute | solution.py:184
  5.1 5.3 %collective-permute-start = (f32[2,16,768]{2,1,0:T(8,128)}, f32[2,16,768]{2,1,0:T(8,128)S(1)}, u32[]{:S(2)}, u32[]{:S(2)}) collective-permute-start(f32[2,16,768]{2,1,0:T(8,128)} %given.1), channel_id=1, source_target_pairs={{0,4},{4,0},{8,12},{12,8},{16,20},{20,16},{24,28},{28,24},{1,5},{5... | collective-permute-start | bytes 294920 | tf_op jit(solution)/shard_map/ppermute | solution.py:184
  6.2 0.9 %copy-start.2 = (f32[2,16,768]{2,1,0:T(8,128)S(1)}, f32[2,16,768]{2,1,0:T(8,128)}, u32[]{:S(2)}) copy-start(f32[2,16,768]{2,1,0:T(8,128)} %given.1) | copy-start | bytes 294916
  10.5 3.4 %copy-start.1 = (f32[2,16,768]{2,1,0:T(8,128)S(1)}, f32[2,16,768]{2,1,0:T(8,128)}, u32[]{:S(2)}) copy-start(f32[2,16,768]{2,1,0:T(8,128)} %ray.3) | copy-start | bytes 294916
  10.9 3.0 %copy-start = (f32[2,16,768]{2,1,0:T(8,128)S(1)}, f32[2,16,768]{2,1,0:T(8,128)}, u32[]{:S(2)}) copy-start(f32[2,16,768]{2,1,0:T(8,128)} %measured.3) | copy-start | bytes 294916
  10.9 5.1 %collective-permute-start.4 = (f32[2,8,768]{2,1,0:T(8,128)S(1)}, f32[2,8,768]{2,1,0:T(8,128)S(1)}, u32[]{:S(2)}, u32[]{:S(2)}) collective-permute-start(f32[2,8,768]{2,1,0:T(8,128)S(1)} %get-tuple-element.21.given), channel_id=1, source_target_pairs={{0,16},{4,20},{8,24},{12,28},{16,0},{20,4},{24,8},{28,12},{1,17},{... | collective-permute-start | bytes 147464 | tf_op jit(solution)/shard_map/ppermute | solution.py:184
  13.6 5.0 %collective-permute-start.3 = (f32[2,8,768]{2,1,0:T(8,128)S(1)}, f32[2,8,768]{2,1,0:T(8,128)S(1)}, u32[]{:S(2)}, u32[]{:S(2)}) collective-permute-start(f32[2,8,768]{2,1,0:T(8,128)S(1)} %get-tuple-element.19.given), channel_id=1, source_target_pairs={{0,16},{4,20},{8,24},{12,28},{16,0},{20,4},{24,8},{28,12},{1,17},{... | collective-permute-start | bytes 147464 | tf_op jit(solution)/shard_map/ppermute | solution.py:184
  13.9 5.6 %collective-permute-start.7 = (f32[2,8,768]{2,1,0:T(8,128)S(1)}, f32[2,8,768]{2,1,0:T(8,128)S(1)}, u32[]{:S(2)}, u32[]{:S(2)}) collective-permute-start(f32[2,8,768]{2,1,0:T(8,128)S(1)} %get-tuple-element.26), channel_id=1, source_target_pairs={{0,1},{1,0},{2,3},{3,2},{4,5},{5,4},{6,7},{7,6},{8,9},{9,8},{10,11... | collective-permute-start | bytes 147464 | tf_op jit(solution)/shard_map/ppermute | solution.py:188
  14.0 5.5 %collective-permute-start.8 = (f32[2,8,768]{2,1,0:T(8,128)S(1)}, f32[2,8,768]{2,1,0:T(8,128)S(1)}, u32[]{:S(2)}, u32[]{:S(2)}) collective-permute-start(f32[2,8,768]{2,1,0:T(8,128)S(1)} %get-tuple-element.27), channel_id=1, source_target_pairs={{0,4},{1,2},{2,1},{3,7},{4,0},{5,6},{6,5},{7,3},{8,12},{9,10},{10,... | collective-permute-start | bytes 147464 | tf_op jit(solution)/shard_map/ppermute | solution.py:199
  16.1 4.2 %collective-permute-start.6 = (f32[2,8,768]{2,1,0:T(8,128)S(1)}, f32[2,8,768]{2,1,0:T(8,128)S(1)}, u32[]{:S(2)}, u32[]{:S(2)}) collective-permute-start(f32[2,8,768]{2,1,0:T(8,128)S(1)} %get-tuple-element.24), channel_id=1, source_target_pairs={{0,4},{1,2},{2,1},{3,7},{4,0},{5,6},{6,5},{7,3},{8,12},{9,10},{10,... | collective-permute-start | bytes 147464 | tf_op jit(solution)/shard_map/ppermute | solution.py:199
  18.7 0.7 %copy-start.5 = (f32[2,9]{1,0:T(2,128)S(1)}, f32[2,9]{1,0:T(2,128)}, u32[]{:S(2)}) copy-start(f32[2,9]{1,0:T(2,128)} %param.10) | copy-start | bytes 220
  18.7 1.6 %collective-permute-start.5 = (f32[2,8,768]{2,1,0:T(8,128)S(1)}, f32[2,8,768]{2,1,0:T(8,128)S(1)}, u32[]{:S(2)}, u32[]{:S(2)}) collective-permute-start(f32[2,8,768]{2,1,0:T(8,128)S(1)} %get-tuple-element.23), channel_id=1, source_target_pairs={{0,1},{1,0},{2,3},{3,2},{4,5},{5,4},{6,7},{7,6},{8,9},{9,8},{10,11... | collective-permute-start | bytes 147464 | tf_op jit(solution)/shard_map/ppermute | solution.py:188
  20.6 7.7 %collective-permute-start.9 = (f32[2,16,768]{2,1,0:T(8,128)S(1)}, f32[2,16,768]{2,1,0:T(8,128)S(1)}, u32[]{:S(2)}, u32[]{:S(2)}) collective-permute-start(f32[2,16,768]{2,1,0:T(8,128)S(1)} %get-tuple-element.29.given), channel_id=1, source_target_pairs={{0,16},{4,20},{8,24},{12,28},{16,0},{20,4},{24,8},{28,12},{1,17},{... | collective-permute-start | bytes 294920 | tf_op jit(solution)/shard_map/ppermute | solution.py:184
  28.5 6.3 %collective-permute-start.12 = (f32[2,16,768]{2,1,0:T(8,128)S(1)}, f32[2,16,768]{2,1,0:T(8,128)S(1)}, u32[]{:S(2)}, u32[]{:S(2)}) collective-permute-start(f32[2,16,768]{2,1,0:T(8,128)S(1)} %part.17.given), channel_id=1, source_target_pairs={{0,12},{4,8},{8,4},{12,0},{16,28},{20,24},{24,20},{28,16},{1,13},{... | collective-permute-start | bytes 294920 | tf_op jit(solution)/shard_map/ppermute | solution.py:184
  29.6 5.6 %collective-permute-start.11 = (f32[2,16,768]{2,1,0:T(8,128)S(1)}, f32[2,16,768]{2,1,0:T(8,128)S(1)}, u32[]{:S(2)}, u32[]{:S(2)}) collective-permute-start(f32[2,16,768]{2,1,0:T(8,128)S(1)} %part.17.given), channel_id=1, source_target_pairs={{0,4},{4,0},{8,12},{12,8},{16,20},{20,16},{24,28},{28,24},{1,5},{5... | collective-permute-start | bytes 294920 | tf_op jit(solution)/shard_map/ppermute | solution.py:184
  30.6 5.0 %collective-permute-start.10 = (f32[2,16,768]{2,1,0:T(8,128)S(1)}, f32[2,16,768]{2,1,0:T(8,128)S(1)}, u32[]{:S(2)}, u32[]{:S(2)}) collective-permute-start(f32[2,16,768]{2,1,0:T(8,128)S(1)} %part.17.given), channel_id=1, source_target_pairs={{0,8},{4,12},{8,0},{12,4},{16,24},{20,28},{24,16},{28,20},{1,9},{5... | collective-permute-start | bytes 294920 | tf_op jit(solution)/shard_map/ppermute | solution.py:184

commit v8 on v7

--- a/solution.py
+++ b/solution.py
@@ -12,16 +12,17 @@
 SMALL = pltpu.CompilerParams(vmem_limit_bytes=8 << 20)
 
 
-def shifted_sum(rows, moves, weights, total):
+def shifted_sum(rows, move, weights):
     planes, columns = rows.shape
     count = columns // LANES
     tiles = [rows[:, LANES * j : LANES * (j + 1)] for j in range(count)]
     lane = lax.broadcasted_iota(jnp.int32, (planes, LANES), 1)
     nothing = jnp.zeros((planes, LANES), jnp.float32)
-    for move, weight in zip(moves, weights):
-        turned = [pltpu.roll(tile, (LANES - move) & (LANES - 1), 1) for tile in tiles]
-        below = lane + move < 0
-        above = lane + move >= LANES
+    total = [None] * count
+    for k, weight in enumerate(weights):
+        turned = [pltpu.roll(tile, (LANES - move - k) & (LANES - 1), 1) for tile in tiles]
+        below = lane + (move + k) < 0
+        above = lane + (move + k) >= LANES
         for j in range(count):
             left = turned[j - 1] if j > 0 else nothing
             right = turned[j + 1] if j + 1 < count else nothing
@@ -52,26 +53,27 @@
     views, planes, columns = given.shape
     taps = weights.shape[0] // (whole_numbers.shape[0] // 2)
     count = columns // LANES
-    if direction < 0:
-        out[...] = jnp.zeros(out.shape, jnp.float32) if base is None else base[...]
-    for v in range(views):
-        at = index * views + v
-        begin, source = whole_numbers[2 * at, 0], whole_numbers[2 * at + 1, 0]
-        moves = [begin + direction * k for k in range(taps)]
+    rows = [index * views + v for v in range(views)]
+    begins = [whole_numbers[2 * at, 0] for at in rows]
+    sources = [whole_numbers[2 * at + 1, 0] for at in rows]
+    sums = []
+    for v, at in enumerate(rows):
         factors = [
             jnp.broadcast_to(weights[pl.ds(at * taps + k, 1), :], (planes, LANES))
             for k in range(taps)
         ]
         if direction > 0:
-            total = [None] * count
-            if base is not None:
-                total = [base[v, :, LANES * j : LANES * (j + 1)] for j in range(count)]
-            total = shifted_sum(given[source], moves, factors, total)
-            for j in range(count):
-                out[v, :, LANES * j : LANES * (j + 1)] = total[j]
+            sums.append(shifted_sum(given[sources[v]], begins[v], factors))
         else:
-            total = shifted_sum(given[v], moves, factors, [None] * count)
-            out[source] = out[source] + jnp.concatenate(total, axis=1)
+            sums.append(shifted_sum(given[v], begins[v] - (taps - 1), factors[::-1]))
+    for m in range(views):
+        for j in range(count):
+            at = pl.ds(LANES * j, LANES)
+            if direction > 0:
+                total = sums[m][j]
+            else:
+                total = sum(jnp.where(sources[v] == m, sums[v][j], 0.0) for v in range(views))
+            out[m, :, at] = total if base is None else base[m, :, at] + total
 
 
 def part_kernel(index, direction, first, whole_numbers, weights, given, *refs):
@@ -317,7 +319,8 @@
         kept[0],
         name="mix",
     )
-    pair_mix, across_mix = with_pair(pair_mix), across_pairs(across_mix)
+    across_mix = across_pairs(across_mix)
+    pair_mix = with_pair(pair_mix)
 
     own_step, partner_step = forward_entries[groups[-1]][0]
     width = 2 * reach

time: 36.8 us -> 36.9 us (level)
  no operation moved by 1% of the time
where the time goes in v8:
time: 36.9 us; the launch traced here: 36.7 us
  starting transfers between devices  16.1 us (44%)
  waiting for transfers between devices  12.2 us (33%)
  Pallas kernels  5.21 us (14%)
  local copies, waits for them, and re-layouts  1.65 us (4%)
  between operations  0.88 us (2%)
  other arithmetic  0.71 us (2%)
    ppermute x9, starting transfers between devices, across_view(): lax.ppermute(x, 'view', [(i, i ^ apart) for i in range(lax.axis_size('vie...  14 us
    ppermute x9, waiting for transfers between devices, across_view(): lax.ppermute(x, 'view', [(i, i ^ apart) for i in range(lax.axis_size('vie...  11.4 us
    pallas_call x21, Pallas kernels, call(): pl.pallas_call(kernel, out_shape=out_shape, in_specs=[BLOCK] * len(args),...  5.21 us
    ppermute x2, starting transfers between devices, across_pairs(): return lax.ppermute(x, ('view', 'slab'), moves)  1.99 us
    unnamed x12, local copies, waits for them, and re-layouts  1.5 us
    ppermute x2, waiting for transfers between devices, across_pairs(): return lax.ppermute(x, ('view', 'slab'), moves)  0.8 us
  transfers between devices with their start and end apart: 13, of which 8 were waited for; matrix products, arithmetic and copies ran while one was open for 2% of the time, Pallas kernels for 9%

profile of v8, /device:TPU:0, one launch (start us, length us, event | category | flops | bytes accessed | tf_op | source)
XLA Modules:
  0.0 36.7 jit_solution(4290410682242225106)
XLA Ops:
  0.7 4.0 %collective-permute-start.2 = (f32[2,16,768]{2,1,0:T(8,128)}, f32[2,16,768]{2,1,0:T(8,128)S(1)}, u32[]{:S(2)}, u32[]{:S(2)}) collective-permute-start(f32[2,16,768]{2,1,0:T(8,128)} %given.1), channel_id=1, source_target_pairs={{0,12},{4,8},{8,4},{12,0},{16,28},{20,24},{24,20},{28,16},{1,13},{... | collective-permute-start | bytes 294920 | tf_op jit(solution)/shard_map/ppermute | solution.py:186
  4.7 0.4 %collective-permute-start.1 = (f32[2,16,768]{2,1,0:T(8,128)}, f32[2,16,768]{2,1,0:T(8,128)S(1)}, u32[]{:S(2)}, u32[]{:S(2)}) collective-permute-start(f32[2,16,768]{2,1,0:T(8,128)} %given.1), channel_id=1, source_target_pairs={{0,8},{4,12},{8,0},{12,4},{16,24},{20,28},{24,16},{28,20},{1,9},{5... | collective-permute-start | bytes 294920 | tf_op jit(solution)/shard_map/ppermute | solution.py:186
  5.3 0.7 %convert_element_type.12 = f32[3,2,16]{2,1,0:T(2,128)S(1)} convert(s32[3,2,16]{2,1,0:T(2,128)} %param.12) | non-fusion elementwise | flops 96 | bytes 768 | tf_op jit(solution)/shard_map/convert_element_type | solution.py:240
  6.2 0.9 %copy-done.2 = f32[2,16,768]{2,1,0:T(8,128)S(1)} copy-done((f32[2,16,768]{2,1,0:T(8,128)S(1)}, f32[2,16,768]{2,1,0:T(8,128)}, u32[]{:S(2)}) %copy-start.2) | copy-done | bytes 98328
  7.3 1.1 %collective-permute-done.2.given = f32[2,16,768]{2,1,0:T(8,128)S(1)} collective-permute-done((f32[2,16,768]{2,1,0:T(8,128)}, f32[2,16,768]{2,1,0:T(8,128)S(1)}, u32[]{:S(2)}, u32[]{:S(2)}) %collective-permute-start.2) | collective-permute-done | bytes 98336 | tf_op jit(solution)/shard_map/ppermute | solution.py:186
  8.6 1.4 %collective-permute-done.1.given = f32[2,16,768]{2,1,0:T(8,128)S(1)} collective-permute-done((f32[2,16,768]{2,1,0:T(8,128)}, f32[2,16,768]{2,1,0:T(8,128)S(1)}, u32[]{:S(2)}, u32[]{:S(2)}) %collective-permute-start.1) | collective-permute-done | bytes 98336 | tf_op jit(solution)/shard_map/ppermute | solution.py:186
  10.5 0.4 %two_parts.2.state = f32[2,16,768]{2,1,0:T(8,128)S(1)} custom-call(s32[64,128]{1,0:T(8,128)S(1)} %get-tuple-element.16.whole_numbers, f32[128,128]{1,0:T(8,128)S(1)} %get-tuple-element.17.weights, f32[2,16,768]{2,1,0:T(8,128)S(1)} %collective-permute-done.given, f32[2,16,768]{2,1,0:T(8,128)S(1)} %get-tuple-element.18.base, f32[2,16,768]{2,1,0:T(8,128)S(1)} %part.13.other), custom_call_target="tpu_custom_call" | custom-call | tf_op jit(solution)/shard_map/two_parts/pallas_call | solution.py:174
  10.9 2.7 %collective-permute-start.4 = (f32[2,8,768]{2,1,0:T(8,128)S(1)}, f32[2,8,768]{2,1,0:T(8,128)S(1)}, u32[]{:S(2)}, u32[]{:S(2)}) collective-permute-start(f32[2,8,768]{2,1,0:T(8,128)S(1)} %get-tuple-element.21.given), channel_id=1, source_target_pairs={{0,16},{4,20},{8,24},{12,28},{16,0},{20,4},{24,8},{28,12},{1,17},{... | collective-permute-start | bytes 147464 | tf_op jit(solution)/shard_map/ppermute | solution.py:186
  13.6 0.3 collective-permute-start.3
  14.0 1.0 %collective-permute-start.8 = (f32[2,8,768]{2,1,0:T(8,128)S(1)}, f32[2,8,768]{2,1,0:T(8,128)S(1)}, u32[]{:S(2)}, u32[]{:S(2)}) collective-permute-start(f32[2,8,768]{2,1,0:T(8,128)S(1)} %get-tuple-element.27), channel_id=1, source_target_pairs={{0,4},{1,2},{2,1},{3,7},{4,0},{5,6},{6,5},{7,3},{8,12},{9,10},{10,... | collective-permute-start | bytes 147464 | tf_op jit(solution)/shard_map/ppermute | solution.py:201
  15.3 0.6 %collective-permute-done.4.given = f32[2,8,768]{2,1,0:T(8,128)S(1)} collective-permute-done((f32[2,8,768]{2,1,0:T(8,128)S(1)}, f32[2,8,768]{2,1,0:T(8,128)S(1)}, u32[]{:S(2)}, u32[]{:S(2)}) %collective-permute-start.4) | collective-permute-done | bytes 49184 | tf_op jit(solution)/shard_map/ppermute | solution.py:186
  16.1 1.0 %collective-permute-start.6 = (f32[2,8,768]{2,1,0:T(8,128)S(1)}, f32[2,8,768]{2,1,0:T(8,128)S(1)}, u32[]{:S(2)}, u32[]{:S(2)}) collective-permute-start(f32[2,8,768]{2,1,0:T(8,128)S(1)} %get-tuple-element.24), channel_id=1, source_target_pairs={{0,4},{1,2},{2,1},{3,7},{4,0},{5,6},{6,5},{7,3},{8,12},{9,10},{10,... | collective-permute-start | bytes 147464 | tf_op jit(solution)/shard_map/ppermute | solution.py:201
  17.1 1.4 %collective-permute-done.3.given = f32[2,8,768]{2,1,0:T(8,128)S(1)} collective-permute-done((f32[2,8,768]{2,1,0:T(8,128)S(1)}, f32[2,8,768]{2,1,0:T(8,128)S(1)}, u32[]{:S(2)}, u32[]{:S(2)}) %collective-permute-start.3) | collective-permute-done | bytes 49184 | tf_op jit(solution)/shard_map/ppermute | solution.py:186
  18.8 0.6 %copy-done.5 = f32[2,9]{1,0:T(2,128)S(1)} copy-done((f32[2,9]{1,0:T(2,128)S(1)}, f32[2,9]{1,0:T(2,128)}, u32[]{:S(2)}) %copy-start.5) | copy-done | bytes 96
  19.5 0.8 %collective-permute-done.6.across = f32[2,8,768]{2,1,0:T(8,128)S(1)} collective-permute-done((f32[2,8,768]{2,1,0:T(8,128)S(1)}, f32[2,8,768]{2,1,0:T(8,128)S(1)}, u32[]{:S(2)}, u32[]{:S(2)}) %collective-permute-start.6) | collective-permute-done | bytes 49184 | tf_op jit(solution)/shard_map/ppermute | solution.py:201
  20.4 0.3 tilt.1
  20.6 2.8 %collective-permute-start.9 = (f32[2,16,768]{2,1,0:T(8,128)S(1)}, f32[2,16,768]{2,1,0:T(8,128)S(1)}, u32[]{:S(2)}, u32[]{:S(2)}) collective-permute-start(f32[2,16,768]{2,1,0:T(8,128)S(1)} %get-tuple-element.29.given), channel_id=1, source_target_pairs={{0,16},{4,20},{8,24},{12,28},{16,0},{20,4},{24,8},{28,12},{1,17},{... | collective-permute-start | bytes 294920 | tf_op jit(solution)/shard_map/ppermute | solution.py:186
  23.6 4.7 %collective-permute-done.9.given = f32[2,16,768]{2,1,0:T(8,128)S(1)} collective-permute-done((f32[2,16,768]{2,1,0:T(8,128)S(1)}, f32[2,16,768]{2,1,0:T(8,128)S(1)}, u32[]{:S(2)}, u32[]{:S(2)}) %collective-permute-start.9) | collective-permute-done | bytes 98336 | tf_op jit(solution)/shard_map/ppermute | solution.py:186
  28.5 1.1 %collective-permute-start.12 = (f32[2,16,768]{2,1,0:T(8,128)S(1)}, f32[2,16,768]{2,1,0:T(8,128)S(1)}, u32[]{:S(2)}, u32[]{:S(2)}) collective-permute-start(f32[2,16,768]{2,1,0:T(8,128)S(1)} %part.17.given), channel_id=1, source_target_pairs={{0,12},{4,8},{8,4},{12,0},{16,28},{20,24},{24,20},{28,16},{1,13},{... | collective-permute-start | bytes 294920 | tf_op jit(solution)/shard_map/ppermute | solution.py:186
  29.6 1.0 %collective-permute-start.11 = (f32[2,16,768]{2,1,0:T(8,128)S(1)}, f32[2,16,768]{2,1,0:T(8,128)S(1)}, u32[]{:S(2)}, u32[]{:S(2)}) collective-permute-start(f32[2,16,768]{2,1,0:T(8,128)S(1)} %part.17.given), channel_id=1, source_target_pairs={{0,4},{4,0},{8,12},{12,8},{16,20},{20,16},{24,28},{28,24},{1,5},{5... | collective-permute-start | bytes 294920 | tf_op jit(solution)/shard_map/ppermute | solution.py:186
  30.6 1.5 %collective-permute-start.10 = (f32[2,16,768]{2,1,0:T(8,128)S(1)}, f32[2,16,768]{2,1,0:T(8,128)S(1)}, u32[]{:S(2)}, u32[]{:S(2)}) collective-permute-start(f32[2,16,768]{2,1,0:T(8,128)S(1)} %part.17.given), channel_id=1, source_target_pairs={{0,8},{4,12},{8,0},{12,4},{16,24},{20,28},{24,16},{28,20},{1,9},{5... | collective-permute-start | bytes 294920 | tf_op jit(solution)/shard_map/ppermute | solution.py:186
  32.1 0.6 %residual.1 = f32[2,16,768]{2,1,0:T(8,128)} custom-call(f32[2,16,768]{2,1,0:T(8,128)S(1)} %get-tuple-element.28.given), custom_call_target="tpu_custom_call" | custom-call | tf_op jit(solution)/shard_map/residual/pallas_call | solution.py:174
  33.0 1.9 %collective-permute-done.12.given = f32[2,16,768]{2,1,0:T(8,128)S(1)} collective-permute-done((f32[2,16,768]{2,1,0:T(8,128)S(1)}, f32[2,16,768]{2,1,0:T(8,128)S(1)}, u32[]{:S(2)}, u32[]{:S(2)}) %collective-permute-start.12) | collective-permute-done | bytes 98336 | tf_op jit(solution)/shard_map/ppermute | solution.py:186
  35.7 1.0 %two_parts.3 = f32[2,16,768]{2,1,0:T(8,128)} custom-call(s32[64,128]{1,0:T(8,128)S(1)} %get-tuple-element.16.whole_numbers, f32[128,128]{1,0:T(8,128)S(1)} %get-tuple-element.17.weights, f32[2,16,768]{2,1,0:T(8,128)S(1)} %collective-permute-done.10.given, f32[2,16,768]{2,1,0:T(8,128)S(1)} %part.18.base, f32[2,16,768]{2,1,0:T(8,128)S(1)} %part.21.other), custom_call_target="tpu_custom_call" | custom-call | tf_op jit(solution)/shard_map/two_parts/pallas_call | solution.py:174
  (40 shorter events, 3.6 us)
Async XLA Ops:
  0.6 5.4 %copy-start.4 = (s32[3,2,16]{2,1,0:T(2,128)S(1)}, s32[3,2,16]{2,1,0:T(2,128)}, u32[]{:S(2)}) copy-start(s32[3,2,16]{2,1,0:T(2,128)} %param.13) | copy-start | bytes 1156
  0.6 5.4 %copy-start.3 = (f32[3,2,16,4]{2,3,1,0:T(4,128)S(1)}, f32[3,2,16,4]{2,3,1,0:T(4,128)}, u32[]{:S(2)}) copy-start(f32[3,2,16,4]{2,3,1,0:T(4,128)} %param.11) | copy-start | bytes 4612
  0.7 7.8 %collective-permute-start.2 = (f32[2,16,768]{2,1,0:T(8,128)}, f32[2,16,768]{2,1,0:T(8,128)S(1)}, u32[]{:S(2)}, u32[]{:S(2)}) collective-permute-start(f32[2,16,768]{2,1,0:T(8,128)} %given.1), channel_id=1, source_target_pairs={{0,12},{4,8},{8,4},{12,0},{16,28},{20,24},{24,20},{28,16},{1,13},{... | collective-permute-start | bytes 294920 | tf_op jit(solution)/shard_map/ppermute | solution.py:186
  4.7 5.4 %collective-permute-start.1 = (f32[2,16,768]{2,1,0:T(8,128)}, f32[2,16,768]{2,1,0:T(8,128)S(1)}, u32[]{:S(2)}, u32[]{:S(2)}) collective-permute-start(f32[2,16,768]{2,1,0:T(8,128)} %given.1), channel_id=1, source_target_pairs={{0,8},{4,12},{8,0},{12,4},{16,24},{20,28},{24,16},{28,20},{1,9},{5... | collective-permute-start | bytes 294920 | tf_op jit(solution)/shard_map/ppermute | solution.py:186
  5.1 5.3 %collective-permute-start = (f32[2,16,768]{2,1,0:T(8,128)}, f32[2,16,768]{2,1,0:T(8,128)S(1)}, u32[]{:S(2)}, u32[]{:S(2)}) collective-permute-start(f32[2,16,768]{2,1,0:T(8,128)} %given.1), channel_id=1, source_target_pairs={{0,4},{4,0},{8,12},{12,8},{16,20},{20,16},{24,28},{28,24},{1,5},{5... | collective-permute-start | bytes 294920 | tf_op jit(solution)/shard_map/ppermute | solution.py:186
  6.2 0.9 %copy-start.2 = (f32[2,16,768]{2,1,0:T(8,128)S(1)}, f32[2,16,768]{2,1,0:T(8,128)}, u32[]{:S(2)}) copy-start(f32[2,16,768]{2,1,0:T(8,128)} %given.1) | copy-start | bytes 294916
  10.5 3.4 %copy-start.1 = (f32[2,16,768]{2,1,0:T(8,128)S(1)}, f32[2,16,768]{2,1,0:T(8,128)}, u32[]{:S(2)}) copy-start(f32[2,16,768]{2,1,0:T(8,128)} %ray.3) | copy-start | bytes 294916
  10.9 3.0 %copy-start = (f32[2,16,768]{2,1,0:T(8,128)S(1)}, f32[2,16,768]{2,1,0:T(8,128)}, u32[]{:S(2)}) copy-start(f32[2,16,768]{2,1,0:T(8,128)} %measured.3) | copy-start | bytes 294916
  10.9 5.1 %collective-permute-start.4 = (f32[2,8,768]{2,1,0:T(8,128)S(1)}, f32[2,8,768]{2,1,0:T(8,128)S(1)}, u32[]{:S(2)}, u32[]{:S(2)}) collective-permute-start(f32[2,8,768]{2,1,0:T(8,128)S(1)} %get-tuple-element.21.given), channel_id=1, source_target_pairs={{0,16},{4,20},{8,24},{12,28},{16,0},{20,4},{24,8},{28,12},{1,17},{... | collective-permute-start | bytes 147464 | tf_op jit(solution)/shard_map/ppermute | solution.py:186
  13.6 5.0 %collective-permute-start.3 = (f32[2,8,768]{2,1,0:T(8,128)S(1)}, f32[2,8,768]{2,1,0:T(8,128)S(1)}, u32[]{:S(2)}, u32[]{:S(2)}) collective-permute-start(f32[2,8,768]{2,1,0:T(8,128)S(1)} %get-tuple-element.19.given), channel_id=1, source_target_pairs={{0,16},{4,20},{8,24},{12,28},{16,0},{20,4},{24,8},{28,12},{1,17},{... | collective-permute-start | bytes 147464 | tf_op jit(solution)/shard_map/ppermute | solution.py:186
  13.9 5.6 %collective-permute-start.7 = (f32[2,8,768]{2,1,0:T(8,128)S(1)}, f32[2,8,768]{2,1,0:T(8,128)S(1)}, u32[]{:S(2)}, u32[]{:S(2)}) collective-permute-start(f32[2,8,768]{2,1,0:T(8,128)S(1)} %get-tuple-element.26), channel_id=1, source_target_pairs={{0,1},{1,0},{2,3},{3,2},{4,5},{5,4},{6,7},{7,6},{8,9},{9,8},{10,11... | collective-permute-start | bytes 147464 | tf_op jit(solution)/shard_map/ppermute | solution.py:190
  14.0 5.5 %collective-permute-start.8 = (f32[2,8,768]{2,1,0:T(8,128)S(1)}, f32[2,8,768]{2,1,0:T(8,128)S(1)}, u32[]{:S(2)}, u32[]{:S(2)}) collective-permute-start(f32[2,8,768]{2,1,0:T(8,128)S(1)} %get-tuple-element.27), channel_id=1, source_target_pairs={{0,4},{1,2},{2,1},{3,7},{4,0},{5,6},{6,5},{7,3},{8,12},{9,10},{10,... | collective-permute-start | bytes 147464 | tf_op jit(solution)/shard_map/ppermute | solution.py:201
  16.1 4.2 %collective-permute-start.6 = (f32[2,8,768]{2,1,0:T(8,128)S(1)}, f32[2,8,768]{2,1,0:T(8,128)S(1)}, u32[]{:S(2)}, u32[]{:S(2)}) collective-permute-start(f32[2,8,768]{2,1,0:T(8,128)S(1)} %get-tuple-element.24), channel_id=1, source_target_pairs={{0,4},{1,2},{2,1},{3,7},{4,0},{5,6},{6,5},{7,3},{8,12},{9,10},{10,... | collective-permute-start | bytes 147464 | tf_op jit(solution)/shard_map/ppermute | solution.py:201
  18.7 0.7 %copy-start.5 = (f32[2,9]{1,0:T(2,128)S(1)}, f32[2,9]{1,0:T(2,128)}, u32[]{:S(2)}) copy-start(f32[2,9]{1,0:T(2,128)} %param.10) | copy-start | bytes 220
  18.7 1.6 %collective-permute-start.5 = (f32[2,8,768]{2,1,0:T(8,128)S(1)}, f32[2,8,768]{2,1,0:T(8,128)S(1)}, u32[]{:S(2)}, u32[]{:S(2)}) collective-permute-start(f32[2,8,768]{2,1,0:T(8,128)S(1)} %get-tuple-element.23), channel_id=1, source_target_pairs={{0,1},{1,0},{2,3},{3,2},{4,5},{5,4},{6,7},{7,6},{8,9},{9,8},{10,11... | collective-permute-start | bytes 147464 | tf_op jit(solution)/shard_map/ppermute | solution.py:190
  20.6 7.7 %collective-permute-start.9 = (f32[2,16,768]{2,1,0:T(8,128)S(1)}, f32[2,16,768]{2,1,0:T(8,128)S(1)}, u32[]{:S(2)}, u32[]{:S(2)}) collective-permute-start(f32[2,16,768]{2,1,0:T(8,128)S(1)} %get-tuple-element.29.given), channel_id=1, source_target_pairs={{0,16},{4,20},{8,24},{12,28},{16,0},{20,4},{24,8},{28,12},{1,17},{... | collective-permute-start | bytes 294920 | tf_op jit(solution)/shard_map/ppermute | solution.py:186
  28.5 6.3 %collective-permute-start.12 = (f32[2,16,768]{2,1,0:T(8,128)S(1)}, f32[2,16,768]{2,1,0:T(8,128)S(1)}, u32[]{:S(2)}, u32[]{:S(2)}) collective-permute-start(f32[2,16,768]{2,1,0:T(8,128)S(1)} %part.17.given), channel_id=1, source_target_pairs={{0,12},{4,8},{8,4},{12,0},{16,28},{20,24},{24,20},{28,16},{1,13},{... | collective-permute-start | bytes 294920 | tf_op jit(solution)/shard_map/ppermute | solution.py:186
  29.6 5.6 %collective-permute-start.11 = (f32[2,16,768]{2,1,0:T(8,128)S(1)}, f32[2,16,768]{2,1,0:T(8,128)S(1)}, u32[]{:S(2)}, u32[]{:S(2)}) collective-permute-start(f32[2,16,768]{2,1,0:T(8,128)S(1)} %part.17.given), channel_id=1, source_target_pairs={{0,4},{4,0},{8,12},{12,8},{16,20},{20,16},{24,28},{28,24},{1,5},{5... | collective-permute-start | bytes 294920 | tf_op jit(solution)/shard_map/ppermute | solution.py:186
  30.6 5.0 %collective-permute-start.10 = (f32[2,16,768]{2,1,0:T(8,128)S(1)}, f32[2,16,768]{2,1,0:T(8,128)S(1)}, u32[]{:S(2)}, u32[]{:S(2)}) collective-permute-start(f32[2,16,768]{2,1,0:T(8,128)S(1)} %part.17.given), channel_id=1, source_target_pairs={{0,8},{4,12},{8,0},{12,4},{16,24},{20,28},{24,16},{28,20},{1,9},{5... | collective-permute-start | bytes 294920 | tf_op jit(solution)/shard_map/ppermute | solution.py:186

commit v9 on v8

--- a/solution.py
+++ b/solution.py
@@ -178,6 +178,7 @@
         out_specs=jax.tree.map(lambda _: BLOCK, out_shape),
         scratch_shapes=scratch,
         compiler_params=SMALL,
+        cost_estimate=pl.CostEstimate(flops=10**8, bytes_accessed=2 * 10**6, transcendentals=0),
         name=name,
     )(*args)
 

time: 36.9 us -> 36.9 us (level)
  no operation moved by 1% of the time
where the time goes in v9:
time: 36.9 us; the launch traced here: 36.7 us
  starting transfers between devices  16.1 us (44%)
  waiting for transfers between devices  12.3 us (33%)
  Pallas kernels  5.21 us (14%)
  local copies, waits for them, and re-layouts  1.53 us (4%)
  between operations  0.88 us (2%)
  other arithmetic  0.71 us (2%)
    ppermute x9, starting transfers between devices, across_view(): lax.ppermute(x, 'view', [(i, i ^ apart) for i in range(lax.axis_size('vie...  14 us
    ppermute x9, waiting for transfers between devices, across_view(): lax.ppermute(x, 'view', [(i, i ^ apart) for i in range(lax.axis_size('vie...  11.5 us
    pallas_call x21, Pallas kernels, call(): pl.pallas_call(kernel, out_shape=out_shape, in_specs=[BLOCK] * len(args),...  5.21 us
    ppermute x2, starting transfers between devices, across_pairs(): return lax.ppermute(x, ('view', 'slab'), moves)  2 us
    unnamed x12, local copies, waits for them, and re-layouts  1.38 us
    ppermute x2, waiting for transfers between devices, across_pairs(): return lax.ppermute(x, ('view', 'slab'), moves)  0.8 us
  transfers between devices with their start and end apart: 13, of which 8 were waited for; matrix products, arithmetic and copies ran while one was open for 2% of the time, Pallas kernels for 9%

profile of v9, /device:TPU:0, one launch (start us, length us, event | category | flops | bytes accessed | tf_op | source)
XLA Modules:
  0.0 36.7 jit_solution(390250753860394188)
XLA Ops:
  0.7 4.0 %collective-permute-start.2 = (f32[2,16,768]{2,1,0:T(8,128)}, f32[2,16,768]{2,1,0:T(8,128)S(1)}, u32[]{:S(2)}, u32[]{:S(2)}) collective-permute-start(f32[2,16,768]{2,1,0:T(8,128)} %given.1), channel_id=1, source_target_pairs={{0,12},{4,8},{8,4},{12,0},{16,28},{20,24},{24,20},{28,16},{1,13},{... | collective-permute-start | bytes 294920 | tf_op jit(solution)/shard_map/ppermute | solution.py:187
  4.7 0.4 %collective-permute-start.1 = (f32[2,16,768]{2,1,0:T(8,128)}, f32[2,16,768]{2,1,0:T(8,128)S(1)}, u32[]{:S(2)}, u32[]{:S(2)}) collective-permute-start(f32[2,16,768]{2,1,0:T(8,128)} %given.1), channel_id=1, source_target_pairs={{0,8},{4,12},{8,0},{12,4},{16,24},{20,28},{24,16},{28,20},{1,9},{5... | collective-permute-start | bytes 294920 | tf_op jit(solution)/shard_map/ppermute | solution.py:187
  5.3 0.7 %convert_element_type.12 = f32[3,2,16]{2,1,0:T(2,128)S(1)} convert(s32[3,2,16]{2,1,0:T(2,128)} %param.12) | non-fusion elementwise | flops 96 | bytes 768 | tf_op jit(solution)/shard_map/convert_element_type | solution.py:241
  6.2 0.8 %copy-done.2 = f32[2,16,768]{2,1,0:T(8,128)S(1)} copy-done((f32[2,16,768]{2,1,0:T(8,128)S(1)}, f32[2,16,768]{2,1,0:T(8,128)}, u32[]{:S(2)}) %copy-start.2) | copy-done | bytes 98328
  7.1 1.3 %collective-permute-done.2.given = f32[2,16,768]{2,1,0:T(8,128)S(1)} collective-permute-done((f32[2,16,768]{2,1,0:T(8,128)}, f32[2,16,768]{2,1,0:T(8,128)S(1)}, u32[]{:S(2)}, u32[]{:S(2)}) %collective-permute-start.2) | collective-permute-done | bytes 98336 | tf_op jit(solution)/shard_map/ppermute | solution.py:187
  8.6 1.4 %collective-permute-done.1.given = f32[2,16,768]{2,1,0:T(8,128)S(1)} collective-permute-done((f32[2,16,768]{2,1,0:T(8,128)}, f32[2,16,768]{2,1,0:T(8,128)S(1)}, u32[]{:S(2)}, u32[]{:S(2)}) %collective-permute-start.1) | collective-permute-done | bytes 98336 | tf_op jit(solution)/shard_map/ppermute | solution.py:187
  10.5 0.4 %two_parts.2.state = f32[2,16,768]{2,1,0:T(8,128)S(1)} custom-call(s32[64,128]{1,0:T(8,128)S(1)} %get-tuple-element.16.whole_numbers, f32[128,128]{1,0:T(8,128)S(1)} %get-tuple-element.17.weights, f32[2,16,768]{2,1,0:T(8,128)S(1)} %collective-permute-done.given, f32[2,16,768]{2,1,0:T(8,128)S(1)} %get-tuple-element.18.base, f32[2,16,768]{2,1,0:T(8,128)S(1)} %part.13.other), custom_call_target="tpu_custom_call" | custom-call | flops 100000000 | bytes 2000000 | tf_op jit(solution)/shard_map/two_parts/pallas_call | solution.py:174
  10.9 2.7 %collective-permute-start.4 = (f32[2,8,768]{2,1,0:T(8,128)S(1)}, f32[2,8,768]{2,1,0:T(8,128)S(1)}, u32[]{:S(2)}, u32[]{:S(2)}) collective-permute-start(f32[2,8,768]{2,1,0:T(8,128)S(1)} %get-tuple-element.21.given), channel_id=1, source_target_pairs={{0,16},{4,20},{8,24},{12,28},{16,0},{20,4},{24,8},{28,12},{1,17},{... | collective-permute-start | bytes 147464 | tf_op jit(solution)/shard_map/ppermute | solution.py:187
  13.6 0.3 collective-permute-start.3
  14.0 1.0 %collective-permute-start.8 = (f32[2,8,768]{2,1,0:T(8,128)S(1)}, f32[2,8,768]{2,1,0:T(8,128)S(1)}, u32[]{:S(2)}, u32[]{:S(2)}) collective-permute-start(f32[2,8,768]{2,1,0:T(8,128)S(1)} %get-tuple-element.27), channel_id=1, source_target_pairs={{0,4},{1,2},{2,1},{3,7},{4,0},{5,6},{6,5},{7,3},{8,12},{9,10},{10,... | collective-permute-start | bytes 147464 | tf_op jit(solution)/shard_map/ppermute | solution.py:202
  15.3 0.6 %collective-permute-done.4.given = f32[2,8,768]{2,1,0:T(8,128)S(1)} collective-permute-done((f32[2,8,768]{2,1,0:T(8,128)S(1)}, f32[2,8,768]{2,1,0:T(8,128)S(1)}, u32[]{:S(2)}, u32[]{:S(2)}) %collective-permute-start.4) | collective-permute-done | bytes 49184 | tf_op jit(solution)/shard_map/ppermute | solution.py:187
  16.1 1.0 %collective-permute-start.6 = (f32[2,8,768]{2,1,0:T(8,128)S(1)}, f32[2,8,768]{2,1,0:T(8,128)S(1)}, u32[]{:S(2)}, u32[]{:S(2)}) collective-permute-start(f32[2,8,768]{2,1,0:T(8,128)S(1)} %get-tuple-element.24), channel_id=1, source_target_pairs={{0,4},{1,2},{2,1},{3,7},{4,0},{5,6},{6,5},{7,3},{8,12},{9,10},{10,... | collective-permute-start | bytes 147464 | tf_op jit(solution)/shard_map/ppermute | solution.py:202
  17.1 1.4 %collective-permute-done.3.given = f32[2,8,768]{2,1,0:T(8,128)S(1)} collective-permute-done((f32[2,8,768]{2,1,0:T(8,128)S(1)}, f32[2,8,768]{2,1,0:T(8,128)S(1)}, u32[]{:S(2)}, u32[]{:S(2)}) %collective-permute-start.3) | collective-permute-done | bytes 49184 | tf_op jit(solution)/shard_map/ppermute | solution.py:187
  18.8 0.6 %copy-done.5 = f32[2,9]{1,0:T(2,128)S(1)} copy-done((f32[2,9]{1,0:T(2,128)S(1)}, f32[2,9]{1,0:T(2,128)}, u32[]{:S(2)}) %copy-start.5) | copy-done | bytes 96
  19.5 0.8 %collective-permute-done.6.across = f32[2,8,768]{2,1,0:T(8,128)S(1)} collective-permute-done((f32[2,8,768]{2,1,0:T(8,128)S(1)}, f32[2,8,768]{2,1,0:T(8,128)S(1)}, u32[]{:S(2)}, u32[]{:S(2)}) %collective-permute-start.6) | collective-permute-done | bytes 49184 | tf_op jit(solution)/shard_map/ppermute | solution.py:202
  20.4 0.3 tilt.1
  20.6 2.8 %collective-permute-start.9 = (f32[2,16,768]{2,1,0:T(8,128)S(1)}, f32[2,16,768]{2,1,0:T(8,128)S(1)}, u32[]{:S(2)}, u32[]{:S(2)}) collective-permute-start(f32[2,16,768]{2,1,0:T(8,128)S(1)} %get-tuple-element.29.given), channel_id=1, source_target_pairs={{0,16},{4,20},{8,24},{12,28},{16,0},{20,4},{24,8},{28,12},{1,17},{... | collective-permute-start | bytes 294920 | tf_op jit(solution)/shard_map/ppermute | solution.py:187
  23.6 4.7 %collective-permute-done.9.given = f32[2,16,768]{2,1,0:T(8,128)S(1)} collective-permute-done((f32[2,16,768]{2,1,0:T(8,128)S(1)}, f32[2,16,768]{2,1,0:T(8,128)S(1)}, u32[]{:S(2)}, u32[]{:S(2)}) %collective-permute-start.9) | collective-permute-done | bytes 98336 | tf_op jit(solution)/shard_map/ppermute | solution.py:187
  28.5 1.1 %collective-permute-start.12 = (f32[2,16,768]{2,1,0:T(8,128)S(1)}, f32[2,16,768]{2,1,0:T(8,128)S(1)}, u32[]{:S(2)}, u32[]{:S(2)}) collective-permute-start(f32[2,16,768]{2,1,0:T(8,128)S(1)} %part.17.given), channel_id=1, source_target_pairs={{0,12},{4,8},{8,4},{12,0},{16,28},{20,24},{24,20},{28,16},{1,13},{... | collective-permute-start | bytes 294920 | tf_op jit(solution)/shard_map/ppermute | solution.py:187
  29.7 1.0 %collective-permute-start.11 = (f32[2,16,768]{2,1,0:T(8,128)S(1)}, f32[2,16,768]{2,1,0:T(8,128)S(1)}, u32[]{:S(2)}, u32[]{:S(2)}) collective-permute-start(f32[2,16,768]{2,1,0:T(8,128)S(1)} %part.17.given), channel_id=1, source_target_pairs={{0,4},{4,0},{8,12},{12,8},{16,20},{20,16},{24,28},{28,24},{1,5},{5... | collective-permute-start | bytes 294920 | tf_op jit(solution)/shard_map/ppermute | solution.py:187
  30.6 1.5 %collective-permute-start.10 = (f32[2,16,768]{2,1,0:T(8,128)S(1)}, f32[2,16,768]{2,1,0:T(8,128)S(1)}, u32[]{:S(2)}, u32[]{:S(2)}) collective-permute-start(f32[2,16,768]{2,1,0:T(8,128)S(1)} %part.17.given), channel_id=1, source_target_pairs={{0,8},{4,12},{8,0},{12,4},{16,24},{20,28},{24,16},{28,20},{1,9},{5... | collective-permute-start | bytes 294920 | tf_op jit(solution)/shard_map/ppermute | solution.py:187
  32.1 0.6 %residual.1 = f32[2,16,768]{2,1,0:T(8,128)} custom-call(f32[2,16,768]{2,1,0:T(8,128)S(1)} %get-tuple-element.28.given), custom_call_target="tpu_custom_call" | custom-call | flops 100000000 | bytes 2000000 | tf_op jit(solution)/shard_map/residual/pallas_call | solution.py:174
  33.0 1.9 %collective-permute-done.12.given = f32[2,16,768]{2,1,0:T(8,128)S(1)} collective-permute-done((f32[2,16,768]{2,1,0:T(8,128)S(1)}, f32[2,16,768]{2,1,0:T(8,128)S(1)}, u32[]{:S(2)}, u32[]{:S(2)}) %collective-permute-start.12) | collective-permute-done | bytes 98336 | tf_op jit(solution)/shard_map/ppermute | solution.py:187
  35.7 1.0 %two_parts.3 = f32[2,16,768]{2,1,0:T(8,128)} custom-call(s32[64,128]{1,0:T(8,128)S(1)} %get-tuple-element.16.whole_numbers, f32[128,128]{1,0:T(8,128)S(1)} %get-tuple-element.17.weights, f32[2,16,768]{2,1,0:T(8,128)S(1)} %collective-permute-done.10.given, f32[2,16,768]{2,1,0:T(8,128)S(1)} %part.18.base, f32[2,16,768]{2,1,0:T(8,128)S(1)} %part.21.other), custom_call_target="tpu_custom_call" | custom-call | flops 100000000 | bytes 2000000 | tf_op jit(solution)/shard_map/two_parts/pallas_call | solution.py:174
  (40 shorter events, 3.6 us)
Async XLA Ops:
  0.6 5.4 %copy-start.4 = (s32[3,2,16]{2,1,0:T(2,128)S(1)}, s32[3,2,16]{2,1,0:T(2,128)}, u32[]{:S(2)}) copy-start(s32[3,2,16]{2,1,0:T(2,128)} %param.13) | copy-start | bytes 1156
  0.6 5.4 %copy-start.3 = (f32[3,2,16,4]{2,3,1,0:T(4,128)S(1)}, f32[3,2,16,4]{2,3,1,0:T(4,128)}, u32[]{:S(2)}) copy-start(f32[3,2,16,4]{2,3,1,0:T(4,128)} %param.11) | copy-start | bytes 4612
  0.7 7.8 %collective-permute-start.2 = (f32[2,16,768]{2,1,0:T(8,128)}, f32[2,16,768]{2,1,0:T(8,128)S(1)}, u32[]{:S(2)}, u32[]{:S(2)}) collective-permute-start(f32[2,16,768]{2,1,0:T(8,128)} %given.1), channel_id=1, source_target_pairs={{0,12},{4,8},{8,4},{12,0},{16,28},{20,24},{24,20},{28,16},{1,13},{... | collective-permute-start | bytes 294920 | tf_op jit(solution)/shard_map/ppermute | solution.py:187
  4.7 5.4 %collective-permute-start.1 = (f32[2,16,768]{2,1,0:T(8,128)}, f32[2,16,768]{2,1,0:T(8,128)S(1)}, u32[]{:S(2)}, u32[]{:S(2)}) collective-permute-start(f32[2,16,768]{2,1,0:T(8,128)} %given.1), channel_id=1, source_target_pairs={{0,8},{4,12},{8,0},{12,4},{16,24},{20,28},{24,16},{28,20},{1,9},{5... | collective-permute-start | bytes 294920 | tf_op jit(solution)/shard_map/ppermute | solution.py:187
  5.1 5.3 %collective-permute-start = (f32[2,16,768]{2,1,0:T(8,128)}, f32[2,16,768]{2,1,0:T(8,128)S(1)}, u32[]{:S(2)}, u32[]{:S(2)}) collective-permute-start(f32[2,16,768]{2,1,0:T(8,128)} %given.1), channel_id=1, source_target_pairs={{0,4},{4,0},{8,12},{12,8},{16,20},{20,16},{24,28},{28,24},{1,5},{5... | collective-permute-start | bytes 294920 | tf_op jit(solution)/shard_map/ppermute | solution.py:187
  6.0 0.9 %copy-start.2 = (f32[2,16,768]{2,1,0:T(8,128)S(1)}, f32[2,16,768]{2,1,0:T(8,128)}, u32[]{:S(2)}) copy-start(f32[2,16,768]{2,1,0:T(8,128)} %given.1) | copy-start | bytes 294916
  10.9 3.0 %copy-start = (f32[2,16,768]{2,1,0:T(8,128)S(1)}, f32[2,16,768]{2,1,0:T(8,128)}, u32[]{:S(2)}) copy-start(f32[2,16,768]{2,1,0:T(8,128)} %measured.3) | copy-start | bytes 294916
  10.9 3.0 %copy-start.1 = (f32[2,16,768]{2,1,0:T(8,128)S(1)}, f32[2,16,768]{2,1,0:T(8,128)}, u32[]{:S(2)}) copy-start(f32[2,16,768]{2,1,0:T(8,128)} %ray.3) | copy-start | bytes 294916
  10.9 5.1 %collective-permute-start.4 = (f32[2,8,768]{2,1,0:T(8,128)S(1)}, f32[2,8,768]{2,1,0:T(8,128)S(1)}, u32[]{:S(2)}, u32[]{:S(2)}) collective-permute-start(f32[2,8,768]{2,1,0:T(8,128)S(1)} %get-tuple-element.21.given), channel_id=1, source_target_pairs={{0,16},{4,20},{8,24},{12,28},{16,0},{20,4},{24,8},{28,12},{1,17},{... | collective-permute-start | bytes 147464 | tf_op jit(solution)/shard_map/ppermute | solution.py:187
  13.6 5.0 %collective-permute-start.3 = (f32[2,8,768]{2,1,0:T(8,128)S(1)}, f32[2,8,768]{2,1,0:T(8,128)S(1)}, u32[]{:S(2)}, u32[]{:S(2)}) collective-permute-start(f32[2,8,768]{2,1,0:T(8,128)S(1)} %get-tuple-element.19.given), channel_id=1, source_target_pairs={{0,16},{4,20},{8,24},{12,28},{16,0},{20,4},{24,8},{28,12},{1,17},{... | collective-permute-start | bytes 147464 | tf_op jit(solution)/shard_map/ppermute | solution.py:187
  13.9 5.6 %collective-permute-start.7 = (f32[2,8,768]{2,1,0:T(8,128)S(1)}, f32[2,8,768]{2,1,0:T(8,128)S(1)}, u32[]{:S(2)}, u32[]{:S(2)}) collective-permute-start(f32[2,8,768]{2,1,0:T(8,128)S(1)} %get-tuple-element.26), channel_id=1, source_target_pairs={{0,1},{1,0},{2,3},{3,2},{4,5},{5,4},{6,7},{7,6},{8,9},{9,8},{10,11... | collective-permute-start | bytes 147464 | tf_op jit(solution)/shard_map/ppermute | solution.py:191
  14.0 5.5 %collective-permute-start.8 = (f32[2,8,768]{2,1,0:T(8,128)S(1)}, f32[2,8,768]{2,1,0:T(8,128)S(1)}, u32[]{:S(2)}, u32[]{:S(2)}) collective-permute-start(f32[2,8,768]{2,1,0:T(8,128)S(1)} %get-tuple-element.27), channel_id=1, source_target_pairs={{0,4},{1,2},{2,1},{3,7},{4,0},{5,6},{6,5},{7,3},{8,12},{9,10},{10,... | collective-permute-start | bytes 147464 | tf_op jit(solution)/shard_map/ppermute | solution.py:202
  16.1 4.2 %collective-permute-start.6 = (f32[2,8,768]{2,1,0:T(8,128)S(1)}, f32[2,8,768]{2,1,0:T(8,128)S(1)}, u32[]{:S(2)}, u32[]{:S(2)}) collective-permute-start(f32[2,8,768]{2,1,0:T(8,128)S(1)} %get-tuple-element.24), channel_id=1, source_target_pairs={{0,4},{1,2},{2,1},{3,7},{4,0},{5,6},{6,5},{7,3},{8,12},{9,10},{10,... | collective-permute-start | bytes 147464 | tf_op jit(solution)/shard_map/ppermute | solution.py:202
  18.7 0.7 %copy-start.5 = (f32[2,9]{1,0:T(2,128)S(1)}, f32[2,9]{1,0:T(2,128)}, u32[]{:S(2)}) copy-start(f32[2,9]{1,0:T(2,128)} %param.10) | copy-start | bytes 220
  18.7 1.6 %collective-permute-start.5 = (f32[2,8,768]{2,1,0:T(8,128)S(1)}, f32[2,8,768]{2,1,0:T(8,128)S(1)}, u32[]{:S(2)}, u32[]{:S(2)}) collective-permute-start(f32[2,8,768]{2,1,0:T(8,128)S(1)} %get-tuple-element.23), channel_id=1, source_target_pairs={{0,1},{1,0},{2,3},{3,2},{4,5},{5,4},{6,7},{7,6},{8,9},{9,8},{10,11... | collective-permute-start | bytes 147464 | tf_op jit(solution)/shard_map/ppermute | solution.py:191
  20.6 7.7 %collective-permute-start.9 = (f32[2,16,768]{2,1,0:T(8,128)S(1)}, f32[2,16,768]{2,1,0:T(8,128)S(1)}, u32[]{:S(2)}, u32[]{:S(2)}) collective-permute-start(f32[2,16,768]{2,1,0:T(8,128)S(1)} %get-tuple-element.29.given), channel_id=1, source_target_pairs={{0,16},{4,20},{8,24},{12,28},{16,0},{20,4},{24,8},{28,12},{1,17},{... | collective-permute-start | bytes 294920 | tf_op jit(solution)/shard_map/ppermute | solution.py:187
  28.5 6.3 %collective-permute-start.12 = (f32[2,16,768]{2,1,0:T(8,128)S(1)}, f32[2,16,768]{2,1,0:T(8,128)S(1)}, u32[]{:S(2)}, u32[]{:S(2)}) collective-permute-start(f32[2,16,768]{2,1,0:T(8,128)S(1)} %part.17.given), channel_id=1, source_target_pairs={{0,12},{4,8},{8,4},{12,0},{16,28},{20,24},{24,20},{28,16},{1,13},{... | collective-permute-start | bytes 294920 | tf_op jit(solution)/shard_map/ppermute | solution.py:187
  29.7 5.6 %collective-permute-start.11 = (f32[2,16,768]{2,1,0:T(8,128)S(1)}, f32[2,16,768]{2,1,0:T(8,128)S(1)}, u32[]{:S(2)}, u32[]{:S(2)}) collective-permute-start(f32[2,16,768]{2,1,0:T(8,128)S(1)} %part.17.given), channel_id=1, source_target_pairs={{0,4},{4,0},{8,12},{12,8},{16,20},{20,16},{24,28},{28,24},{1,5},{5... | collective-permute-start | bytes 294920 | tf_op jit(solution)/shard_map/ppermute | solution.py:187
  30.6 5.0 %collective-permute-start.10 = (f32[2,16,768]{2,1,0:T(8,128)S(1)}, f32[2,16,768]{2,1,0:T(8,128)S(1)}, u32[]{:S(2)}, u32[]{:S(2)}) collective-permute-start(f32[2,16,768]{2,1,0:T(8,128)S(1)} %part.17.given), channel_id=1, source_target_pairs={{0,8},{4,12},{8,0},{12,4},{16,24},{20,28},{24,16},{28,20},{1,9},{5... | collective-permute-start | bytes 294920 | tf_op jit(solution)/shard_map/ppermute | solution.py:187
